TPU v7x, 512 devices: a whole 4x8x8 slice. The times are simulated.
512 devices in a mesh: tm: 16 (over y_hi, z), space: 32 (over x, y_lo, core).
Axes of the slice: x: 4, y: 8 (y_hi: 2, y_lo: 4; y = y_hi * 4 + y_lo), z: 8, core: 2. Of those that a mesh axis runs over, the one named last changes fastest.
Arguments:
- forcing: float32 [256, 3, 64, 8, 128], P('tm', None, 'space'), may hold values from -6 to 6
- start_field: float32 [3, 64, 8, 128], P(None, 'space'), may hold values from -6 to 6
- iterate: float32 [256, 3, 64, 8, 128], P('tm', None, 'space'), may hold values from -12 to 12
- region: int32 [64, 8, 128], P('space'), may hold values from 0 to 2
- conductance: float32 [3], replicated, may hold values from 0.5 to 4
Outputs:
- updated: float32 [256, 3, 64, 8, 128], P('tm', None, 'space')
All inputs are finite; a program needn't handle non-finite values.
Results may differ from a plain program's by a relative error of at most 0.00013.
Values sent between devices are 32-bit elements; how exact they have to be, the bound alone decides.
No kernel may reach another device: no remote copies, remote signals or barrier semaphores. Data moves between devices by JAX's collectives and lax.ppermute only.
A program may use at most 64 MiB of HBM per device.

v0:
```python
import math

import jax
import jax.numpy as jnp
from jax import lax
from jax.sharding import PartitionSpec as P

SWEEPS = 12


ALPHA = 0.1
LOWER = 0.02
UPPER = 1.0
SIGMA_TOP = 4.0
CURL_TOP = 12.0


def from_behind(value, axis, steps):
    count = lax.axis_size(axis)
    initial, last = (max(0, -steps), min(count, count - steps))
    return lax.ppermute(value, axis, [(source, source + steps) for source in range(initial, last)])


def broadcast(array, axis, root):
    mine = lax.axis_index(axis) == root
    return lax.psum(jnp.where(mine, array, jnp.zeros_like(array)), axis)


def forward_step(values, axis):
    inner = lax.slice_in_dim(values, 1, values.shape[axis], axis=axis)
    border = jnp.zeros_like(lax.slice_in_dim(values, 0, 1, axis=axis))
    return jnp.concatenate([inner, border], axis) - values


def backward_step(values, axis):
    inner = lax.slice_in_dim(values, 0, values.shape[axis] - 1, axis=axis)
    border = jnp.zeros_like(lax.slice_in_dim(values, 0, 1, axis=axis))
    return jnp.concatenate([border, inner], axis) - values


def curl_forward(field):
    field_x, field_y, field_z = (field[:, 0], field[:, 1], field[:, 2])
    lead_x, lead_y, lead_z = (field_x[:, :-1], field_y[:, :-1], field_z[:, :-1])
    flux_x = forward_step(lead_z, 2) - forward_step(lead_y, 3)
    flux_y = forward_step(lead_x, 3) - (field_z[:, 1:] - field_z[:, :-1])
    flux_z = field_y[:, 1:] - field_y[:, :-1] - forward_step(lead_x, 2)
    return jnp.stack([flux_x, flux_y, flux_z], axis=1)


def curl_adjoint(flux):
    flux_x, flux_y, flux_z = (flux[:, 0], flux[:, 1], flux[:, 2])
    tail_x, tail_y, tail_z = (flux_x[:, 1:], flux_y[:, 1:], flux_z[:, 1:])
    field_x = backward_step(tail_y, 3) - backward_step(tail_z, 2)
    field_y = flux_z[:, :-1] - flux_z[:, 1:] - backward_step(tail_x, 3)
    field_z = backward_step(tail_x, 2) - (flux_y[:, :-1] - flux_y[:, 1:])
    return jnp.stack([field_x, field_y, field_z], axis=1)


def brick_curl(field):
    upper = from_behind(field[:, :, :1], "space", -1)
    flux = curl_forward(jnp.concatenate([field, upper], 2))
    lower = from_behind(flux[:, :, -1:], "space", 1)
    return curl_adjoint(jnp.concatenate([lower, flux], 2))


def pair_terms(pairs, window):
    gamma = ALPHA ** (1.0 / window)
    angle = 2.0 * math.pi * pairs.astype(jnp.float32) / window
    plain = 1.0 - gamma * jnp.cos(angle)
    p_plus = jnp.where(pairs == 0, 1.0 - gamma, plain)
    p_minus = jnp.where(pairs == 0, 1.0 + gamma, plain)
    q_term = jnp.where(pairs == 0, 0.0, gamma * jnp.sin(angle))
    bound = jnp.sqrt(jnp.maximum(p_plus, p_minus) ** 2 + q_term**2) * SIGMA_TOP + CURL_TOP
    return (p_plus, p_minus, q_term, bound * bound)


def cas_table(freqs, window):
    moments = jnp.arange(window)
    product = freqs[:, None] * moments[None, :] % window
    angle = 2.0 * math.pi * product.astype(jnp.float32) / window
    return jnp.cos(angle) + jnp.sin(angle)


def powers(window, sign):
    gamma = jnp.float32(ALPHA ** (sign / window))
    return jnp.power(gamma, jnp.arange(window).astype(jnp.float32))


def frequency_order(window, steps):
    slots = jnp.arange(window)
    half = steps // 2
    within = slots % steps
    pairs = slots // steps * half + within % half
    mirror = jnp.where(pairs == 0, window // 2, window - pairs)
    return jnp.where(within < half, pairs, mirror)


def chebyshev_terms(count):
    center = (UPPER + LOWER) / 2.0
    radius = (UPPER - LOWER) / 2.0
    spread_ratio = center / radius
    weight_now = 1.0 / spread_ratio
    carry_terms, push_terms = ([], [])
    for _ in range(count):
        weight_next = 1.0 / (2.0 * spread_ratio - weight_now)
        carry_terms.append(weight_next * weight_now)
        push_terms.append(2.0 * weight_next / radius)
        weight_now = weight_next
    return (jnp.asarray(carry_terms, jnp.float32), jnp.asarray(push_terms, jnp.float32), center)


def per_device(forcing, start_field, iterate, region, conductance):
    steps = forcing.shape[0]
    half = steps // 2
    groups = lax.axis_size("tm")
    window = steps * groups
    depth_z = forcing.shape[4]
    sigma = jnp.zeros(region.shape, jnp.float32)
    for material in range(3):
        sigma = sigma + conductance[material] * (region == material).astype(jnp.float32)
    order = frequency_order(window, steps)
    forward_table = cas_table(order, window) * powers(window, 1.0)[None, :]
    inverse_table = cas_table(order, window).T * (powers(window, -1.0) / window)[:, None]
    flat = forcing.reshape(steps, groups, -1, depth_z)
    spread = jnp.einsum(
        "kn,ngrz->kgrz",
        forward_table,
        lax.all_to_all(flat, "tm", split_axis=1, concat_axis=0, tiled=True),
        precision=lax.Precision.HIGHEST,
    )
    spectrum = lax.all_to_all(spread, "tm", split_axis=0, concat_axis=1, tiled=True).reshape(
        forcing.shape
    )
    latest = broadcast(iterate[steps - 1], "tm", lax.axis_size("tm") - 1)
    spectrum = spectrum + (sigma * (start_field - ALPHA * latest))[None]
    pairs = lax.axis_index("tm") * half + jnp.arange(half)
    p_plus, p_minus, q_term, scale = pair_terms(pairs, window)
    diagonal_coef = jnp.concatenate([p_plus, p_minus]).reshape(steps, 1, 1, 1, 1)
    cross = q_term.reshape(half, 1, 1, 1, 1)
    norm_scale = jnp.concatenate([scale, scale]).reshape(steps, 1, 1, 1, 1)

    def couple(values, sign, weights):
        swapped = jnp.concatenate([-cross * values[half:], cross * values[:half]], 0)
        return weights * (diagonal_coef * values + sign * swapped)

    def normal(values):
        first = brick_curl(values) + couple(values, 1.0, sigma)
        return (brick_curl(first) + couple(first, -1.0, sigma)) / norm_scale

    start = (brick_curl(spectrum) + couple(spectrum, -1.0, sigma)) / norm_scale
    carry_terms, push_terms, center = chebyshev_terms(SWEEPS - 1)

    def sweep(sweep_index, carry_state):
        current, residual, direction = carry_state
        current = current + direction
        residual = residual - normal(direction)
        direction = carry_terms[sweep_index] * direction + push_terms[sweep_index] * residual
        return (current, residual, direction)

    current, residual, direction = lax.fori_loop(
        0, SWEEPS - 1, sweep, (jnp.zeros_like(start), start, start / center)
    )
    solution = (current + direction).reshape(steps, groups, -1, depth_z)
    spread_back = jnp.einsum(
        "nk,kgrz->ngrz",
        inverse_table,
        lax.all_to_all(solution, "tm", split_axis=1, concat_axis=0, tiled=True),
        precision=lax.Precision.HIGHEST,
    )
    updated = lax.all_to_all(spread_back, "tm", split_axis=0, concat_axis=1, tiled=True)
    return updated.reshape(forcing.shape)


def solution(mesh):
    placed = (
        P("tm", None, "space", None, None),
        P(None, "space", None, None),
        P("tm", None, "space", None, None),
        P("space", None, None),
        P(),
    )
    return jax.shard_map(
        per_device,
        mesh=mesh,
        in_specs=placed,
        out_specs=P("tm", None, "space", None, None),
        check_vma=False,
    )
```

profile of v0, /device:TPU:2, one launch (start us, length us, event | category | flops | bytes accessed | tf_op | source)
XLA Modules:
  0.0 573.4 jit_solution(8178410556712829692)
XLA Ops:
  1.9 15.7 %all-to-all-start = ((f32[16,16,3,128]{3,0,2,1:T(8,128)}), f32[16,16,3,128]{3,0,2,1:T(8,128)S(1)}, u32[]{:S(2)}, u32[]{:S(2)}) async-start(f32[16,16,3,128]{3,0,2,1:T(8,128)} %bitcast.2), calls=%async_computation | async-start | bytes 786432 | tf_op jit(solution)/shard_map/all_to_all | solution.py:128
  18.4 14.4 %all-to-all-done = f32[16,16,3,128]{3,0,2,1:T(8,128)S(1)} async-done(((f32[16,16,3,128]{3,0,2,1:T(8,128)}), f32[16,16,3,128]{3,0,2,1:T(8,128)S(1)}, u32[]{:S(2)}, u32[]{:S(2)}) %all-to-all-start) | async-done | bytes 393248 | tf_op jit(solution)/shard_map/all_to_all | solution.py:128
  35.8 6.0 %all-to-all-start.1 = ((f32[256,1,3,128]{3,1,2,0:T(1,128)}), f32[256,1,3,128]{3,1,2,0:T(1,128)S(1)}, u32[]{:S(2)}, u32[]{:S(2)}) async-start(f32[256,1,3,128]{3,1,2,0:T(1,128)} %copy.86), calls=%async_computation.1 | async-start | bytes 786432 | tf_op jit(solution)/shard_map/all_to_all | solution.py:131
  41.9 99.3 %psum.7 = f32[3,2,8,128]{3,2,1,0:T(8,128)S(1)} all-reduce(f32[3,2,8,128]{3,2,1,0:T(8,128)S(1)} %select_bitcast_fusion), channel_id=1, replica_groups=mesh['tm'=16,'space'=32] {'tm'}, use_global_device_ids=true, to_apply=%region_0.1 | all-reduce | flops 6144 | bytes 49152 | tf_op jit(solution)/shard_map/psum | solution.py:26
  149.4 3.7 collective-permute-start.5
  153.2 6.1 %collective-permute-done.5 = f32[16,3,1,8,128]{4,0,3,2,1:T(8,128)S(1)} collective-permute-done((f32[16,3,1,8,128]{4,0,3,2,1:T(8,128)S(1)}, f32[16,3,1,8,128]{4,0,3,2,1:T(8,128)S(1)}, u32[]{:S(2)}, u32[]{:S(2)}) %collective-permute-start.5) | collective-permute-done | bytes 196640 | tf_op jit(solution)/shard_map/ppermute | solution.py:21
  160.7 373.3 %while.22 = (s32[]{:T(128)}, f32[16,3,2,8,128]{4,3,2,1,0:T(8,128)S(1)}, f32[16,3,2,8,128]{4,3,2,1,0:T(8,128)S(1)}, f32[16,3,2,8,128]{4,3,2,1,0:T(8,128)S(1)}, f3...) while((s32[]{:T(128)}, ...), condition=%wide.region_2.3_spmd.clone.clone.clone.clone, body=%wide.region_1.2_spmd.sunk.clone.clone.clone.clone.sunk | while | flops 4767803 | bytes 30532288 | solution.py:160
  168.3 7.9 %collective-permute-done.1 = f32[16,3,1,8,128]{4,3,2,0,1:T(8,128)S(1)} collective-permute-done((f32[16,3,1,8,128]{4,3,2,0,1:T(8,128)S(1)}, f32[16,3,1,8,128]{4,3,2,0,1:T(8,128)S(1)}, u32[]{:S(2)}, u32[]{:S(2)}) %collective-permute-start.1) | collective-permute-done | bytes 196640 | tf_op jit(solution)/shard_map/while/body/eval_jaxpr/ppermute | solution.py:21
  184.2 8.1 %collective-permute-done.3 = f32[16,3,1,8,128]{4,3,2,0,1:T(8,128)S(1)} collective-permute-done((f32[16,3,1,8,128]{4,3,2,0,1:T(8,128)S(1)}, f32[16,3,1,8,128]{4,3,2,0,1:T(8,128)S(1)}, u32[]{:S(2)}, u32[]{:S(2)}) %collective-permute-start.3) | collective-permute-done | bytes 196640 | tf_op jit(solution)/shard_map/while/body/eval_jaxpr/ppermute | solution.py:21
  201.9 8.0 %collective-permute-done.1 = f32[16,3,1,8,128]{4,3,2,0,1:T(8,128)S(1)} collective-permute-done((f32[16,3,1,8,128]{4,3,2,0,1:T(8,128)S(1)}, f32[16,3,1,8,128]{4,3,2,0,1:T(8,128)S(1)}, u32[]{:S(2)}, u32[]{:S(2)}) %collective-permute-start.1) | collective-permute-done | bytes 196640 | tf_op jit(solution)/shard_map/while/body/eval_jaxpr/ppermute | solution.py:21
  217.9 8.1 %collective-permute-done.3 = f32[16,3,1,8,128]{4,3,2,0,1:T(8,128)S(1)} collective-permute-done((f32[16,3,1,8,128]{4,3,2,0,1:T(8,128)S(1)}, f32[16,3,1,8,128]{4,3,2,0,1:T(8,128)S(1)}, u32[]{:S(2)}, u32[]{:S(2)}) %collective-permute-start.3) | collective-permute-done | bytes 196640 | tf_op jit(solution)/shard_map/while/body/eval_jaxpr/ppermute | solution.py:21
  235.6 8.0 %collective-permute-done.1 = f32[16,3,1,8,128]{4,3,2,0,1:T(8,128)S(1)} collective-permute-done((f32[16,3,1,8,128]{4,3,2,0,1:T(8,128)S(1)}, f32[16,3,1,8,128]{4,3,2,0,1:T(8,128)S(1)}, u32[]{:S(2)}, u32[]{:S(2)}) %collective-permute-start.1) | collective-permute-done | bytes 196640 | tf_op jit(solution)/shard_map/while/body/eval_jaxpr/ppermute | solution.py:21
  251.6 8.1 %collective-permute-done.3 = f32[16,3,1,8,128]{4,3,2,0,1:T(8,128)S(1)} collective-permute-done((f32[16,3,1,8,128]{4,3,2,0,1:T(8,128)S(1)}, f32[16,3,1,8,128]{4,3,2,0,1:T(8,128)S(1)}, u32[]{:S(2)}, u32[]{:S(2)}) %collective-permute-start.3) | collective-permute-done | bytes 196640 | tf_op jit(solution)/shard_map/while/body/eval_jaxpr/ppermute | solution.py:21
  269.2 8.0 %collective-permute-done.1 = f32[16,3,1,8,128]{4,3,2,0,1:T(8,128)S(1)} collective-permute-done((f32[16,3,1,8,128]{4,3,2,0,1:T(8,128)S(1)}, f32[16,3,1,8,128]{4,3,2,0,1:T(8,128)S(1)}, u32[]{:S(2)}, u32[]{:S(2)}) %collective-permute-start.1) | collective-permute-done | bytes 196640 | tf_op jit(solution)/shard_map/while/body/eval_jaxpr/ppermute | solution.py:21
  285.2 8.1 %collective-permute-done.3 = f32[16,3,1,8,128]{4,3,2,0,1:T(8,128)S(1)} collective-permute-done((f32[16,3,1,8,128]{4,3,2,0,1:T(8,128)S(1)}, f32[16,3,1,8,128]{4,3,2,0,1:T(8,128)S(1)}, u32[]{:S(2)}, u32[]{:S(2)}) %collective-permute-start.3) | collective-permute-done | bytes 196640 | tf_op jit(solution)/shard_map/while/body/eval_jaxpr/ppermute | solution.py:21
  302.8 8.0 %collective-permute-done.1 = f32[16,3,1,8,128]{4,3,2,0,1:T(8,128)S(1)} collective-permute-done((f32[16,3,1,8,128]{4,3,2,0,1:T(8,128)S(1)}, f32[16,3,1,8,128]{4,3,2,0,1:T(8,128)S(1)}, u32[]{:S(2)}, u32[]{:S(2)}) %collective-permute-start.1) | collective-permute-done | bytes 196640 | tf_op jit(solution)/shard_map/while/body/eval_jaxpr/ppermute | solution.py:21
  318.8 8.1 %collective-permute-done.3 = f32[16,3,1,8,128]{4,3,2,0,1:T(8,128)S(1)} collective-permute-done((f32[16,3,1,8,128]{4,3,2,0,1:T(8,128)S(1)}, f32[16,3,1,8,128]{4,3,2,0,1:T(8,128)S(1)}, u32[]{:S(2)}, u32[]{:S(2)}) %collective-permute-start.3) | collective-permute-done | bytes 196640 | tf_op jit(solution)/shard_map/while/body/eval_jaxpr/ppermute | solution.py:21
  336.4 7.9 %collective-permute-done.1 = f32[16,3,1,8,128]{4,3,2,0,1:T(8,128)S(1)} collective-permute-done((f32[16,3,1,8,128]{4,3,2,0,1:T(8,128)S(1)}, f32[16,3,1,8,128]{4,3,2,0,1:T(8,128)S(1)}, u32[]{:S(2)}, u32[]{:S(2)}) %collective-permute-start.1) | collective-permute-done | bytes 196640 | tf_op jit(solution)/shard_map/while/body/eval_jaxpr/ppermute | solution.py:21
  352.3 8.1 %collective-permute-done.3 = f32[16,3,1,8,128]{4,3,2,0,1:T(8,128)S(1)} collective-permute-done((f32[16,3,1,8,128]{4,3,2,0,1:T(8,128)S(1)}, f32[16,3,1,8,128]{4,3,2,0,1:T(8,128)S(1)}, u32[]{:S(2)}, u32[]{:S(2)}) %collective-permute-start.3) | collective-permute-done | bytes 196640 | tf_op jit(solution)/shard_map/while/body/eval_jaxpr/ppermute | solution.py:21
  370.0 7.9 %collective-permute-done.1 = f32[16,3,1,8,128]{4,3,2,0,1:T(8,128)S(1)} collective-permute-done((f32[16,3,1,8,128]{4,3,2,0,1:T(8,128)S(1)}, f32[16,3,1,8,128]{4,3,2,0,1:T(8,128)S(1)}, u32[]{:S(2)}, u32[]{:S(2)}) %collective-permute-start.1) | collective-permute-done | bytes 196640 | tf_op jit(solution)/shard_map/while/body/eval_jaxpr/ppermute | solution.py:21
  385.9 8.1 %collective-permute-done.3 = f32[16,3,1,8,128]{4,3,2,0,1:T(8,128)S(1)} collective-permute-done((f32[16,3,1,8,128]{4,3,2,0,1:T(8,128)S(1)}, f32[16,3,1,8,128]{4,3,2,0,1:T(8,128)S(1)}, u32[]{:S(2)}, u32[]{:S(2)}) %collective-permute-start.3) | collective-permute-done | bytes 196640 | tf_op jit(solution)/shard_map/while/body/eval_jaxpr/ppermute | solution.py:21
  403.6 7.9 %collective-permute-done.1 = f32[16,3,1,8,128]{4,3,2,0,1:T(8,128)S(1)} collective-permute-done((f32[16,3,1,8,128]{4,3,2,0,1:T(8,128)S(1)}, f32[16,3,1,8,128]{4,3,2,0,1:T(8,128)S(1)}, u32[]{:S(2)}, u32[]{:S(2)}) %collective-permute-start.1) | collective-permute-done | bytes 196640 | tf_op jit(solution)/shard_map/while/body/eval_jaxpr/ppermute | solution.py:21
  419.5 8.1 %collective-permute-done.3 = f32[16,3,1,8,128]{4,3,2,0,1:T(8,128)S(1)} collective-permute-done((f32[16,3,1,8,128]{4,3,2,0,1:T(8,128)S(1)}, f32[16,3,1,8,128]{4,3,2,0,1:T(8,128)S(1)}, u32[]{:S(2)}, u32[]{:S(2)}) %collective-permute-start.3) | collective-permute-done | bytes 196640 | tf_op jit(solution)/shard_map/while/body/eval_jaxpr/ppermute | solution.py:21
  437.1 7.9 %collective-permute-done.1 = f32[16,3,1,8,128]{4,3,2,0,1:T(8,128)S(1)} collective-permute-done((f32[16,3,1,8,128]{4,3,2,0,1:T(8,128)S(1)}, f32[16,3,1,8,128]{4,3,2,0,1:T(8,128)S(1)}, u32[]{:S(2)}, u32[]{:S(2)}) %collective-permute-start.1) | collective-permute-done | bytes 196640 | tf_op jit(solution)/shard_map/while/body/eval_jaxpr/ppermute | solution.py:21
  453.1 8.1 %collective-permute-done.3 = f32[16,3,1,8,128]{4,3,2,0,1:T(8,128)S(1)} collective-permute-done((f32[16,3,1,8,128]{4,3,2,0,1:T(8,128)S(1)}, f32[16,3,1,8,128]{4,3,2,0,1:T(8,128)S(1)}, u32[]{:S(2)}, u32[]{:S(2)}) %collective-permute-start.3) | collective-permute-done | bytes 196640 | tf_op jit(solution)/shard_map/while/body/eval_jaxpr/ppermute | solution.py:21
  470.7 8.0 %collective-permute-done.1 = f32[16,3,1,8,128]{4,3,2,0,1:T(8,128)S(1)} collective-permute-done((f32[16,3,1,8,128]{4,3,2,0,1:T(8,128)S(1)}, f32[16,3,1,8,128]{4,3,2,0,1:T(8,128)S(1)}, u32[]{:S(2)}, u32[]{:S(2)}) %collective-permute-start.1) | collective-permute-done | bytes 196640 | tf_op jit(solution)/shard_map/while/body/eval_jaxpr/ppermute | solution.py:21
  486.7 8.1 %collective-permute-done.3 = f32[16,3,1,8,128]{4,3,2,0,1:T(8,128)S(1)} collective-permute-done((f32[16,3,1,8,128]{4,3,2,0,1:T(8,128)S(1)}, f32[16,3,1,8,128]{4,3,2,0,1:T(8,128)S(1)}, u32[]{:S(2)}, u32[]{:S(2)}) %collective-permute-start.3) | collective-permute-done | bytes 196640 | tf_op jit(solution)/shard_map/while/body/eval_jaxpr/ppermute | solution.py:21
  504.3 8.0 %collective-permute-done.1 = f32[16,3,1,8,128]{4,3,2,0,1:T(8,128)S(1)} collective-permute-done((f32[16,3,1,8,128]{4,3,2,0,1:T(8,128)S(1)}, f32[16,3,1,8,128]{4,3,2,0,1:T(8,128)S(1)}, u32[]{:S(2)}, u32[]{:S(2)}) %collective-permute-start.1) | collective-permute-done | bytes 196640 | tf_op jit(solution)/shard_map/while/body/eval_jaxpr/ppermute | solution.py:21
  520.3 11.9 %collective-permute-done.3 = f32[16,3,1,8,128]{4,3,2,0,1:T(8,128)S(1)} collective-permute-done((f32[16,3,1,8,128]{4,3,2,0,1:T(8,128)S(1)}, f32[16,3,1,8,128]{4,3,2,0,1:T(8,128)S(1)}, u32[]{:S(2)}, u32[]{:S(2)}) %collective-permute-start.3) | collective-permute-done | bytes 196640 | tf_op jit(solution)/shard_map/while/body/eval_jaxpr/ppermute | solution.py:21
  535.0 3.6 all-to-all-start.2
  538.6 13.5 %all-to-all-done.2 = f32[16,16,3,128]{3,0,2,1:T(8,128)S(1)} async-done(((f32[16,16,3,128]{3,0,2,1:T(8,128)}), f32[16,16,3,128]{3,0,2,1:T(8,128)S(1)}, u32[]{:S(2)}, u32[]{:S(2)}) %all-to-all-start.2) | async-done | bytes 393248 | tf_op jit(solution)/shard_map/all_to_all | solution.py:167
  554.2 18.2 %all_to_all.60 = f32[256,1,3,128]{3,1,2,0:T(1,128)S(1)} all-to-all(f32[256,1,3,128]{3,1,2,0:T(1,128)S(1)} %copy.94), channel_id=1, replica_groups=mesh['tm'=16,'space'=32] {'tm'}, dimensions={0} | all-to-all | bytes 786432 | tf_op jit(solution)/shard_map/all_to_all | solution.py:170
  (555 shorter events, 208.8 us)
Async XLA Ops:
  1.9 31.0 %all-to-all-start = ((f32[16,16,3,128]{3,0,2,1:T(8,128)}), f32[16,16,3,128]{3,0,2,1:T(8,128)S(1)}, u32[]{:S(2)}, u32[]{:S(2)}) async-start(f32[16,16,3,128]{3,0,2,1:T(8,128)} %bitcast.2), calls=%async_computation | async-start | bytes 786432 | tf_op jit(solution)/shard_map/all_to_all | solution.py:128
  35.8 108.0 %all-to-all-start.1 = ((f32[256,1,3,128]{3,1,2,0:T(1,128)}), f32[256,1,3,128]{3,1,2,0:T(1,128)S(1)}, u32[]{:S(2)}, u32[]{:S(2)}) async-start(f32[256,1,3,128]{3,1,2,0:T(1,128)} %copy.86), calls=%async_computation.1 | async-start | bytes 786432 | tf_op jit(solution)/shard_map/all_to_all | solution.py:131
  149.4 9.9 %collective-permute-start.5 = (f32[16,3,1,8,128]{4,0,3,2,1:T(8,128)S(1)}, f32[16,3,1,8,128]{4,0,3,2,1:T(8,128)S(1)}, u32[]{:S(2)}, u32[]{:S(2)}) collective-permute-start(f32[16,3,1,8,128]{4,0,3,2,1:T(8,128)S(1)} %pad_maximum_fusion.6), channel_id=1, source_target_pairs={{0,1},{1,2},{2,3},{3,4},{4,5},{5,6},{6,7},{7,8},{8,9},{9,10},{10,1... | collective-permute-start | bytes 589832 | tf_op jit(solution)/shard_map/ppermute | solution.py:21
  166.3 10.0 %collective-permute-start.1 = (f32[16,3,1,8,128]{4,3,2,0,1:T(8,128)S(1)}, f32[16,3,1,8,128]{4,3,2,0,1:T(8,128)S(1)}, u32[]{:S(2)}, u32[]{:S(2)}) collective-permute-start(f32[16,3,1,8,128]{4,3,2,0,1:T(8,128)S(1)} %pad_maximum_fusion.16), channel_id=1, source_target_pairs={{0,1},{1,2},{2,3},{3,4},{4,5},{5,6},{6,7},{7,8},{8,9},{9,10},{10,1... | collective-permute-start | bytes 589832 | tf_op jit(solution)/shard_map/while/body/eval_jaxpr/ppermute | solution.py:21
  182.2 10.2 %collective-permute-start.3 = (f32[16,3,1,8,128]{4,3,2,0,1:T(8,128)S(1)}, f32[16,3,1,8,128]{4,3,2,0,1:T(8,128)S(1)}, u32[]{:S(2)}, u32[]{:S(2)}) collective-permute-start(f32[16,3,1,8,128]{4,3,2,0,1:T(8,128)S(1)} %pad_maximum_fusion.17), channel_id=1, source_target_pairs={{0,1},{1,2},{2,3},{3,4},{4,5},{5,6},{6,7},{7,8},{8,9},{9,10},{10,1... | collective-permute-start | bytes 589832 | tf_op jit(solution)/shard_map/while/body/eval_jaxpr/ppermute | solution.py:21
  199.9 10.0 %collective-permute-start.1 = (f32[16,3,1,8,128]{4,3,2,0,1:T(8,128)S(1)}, f32[16,3,1,8,128]{4,3,2,0,1:T(8,128)S(1)}, u32[]{:S(2)}, u32[]{:S(2)}) collective-permute-start(f32[16,3,1,8,128]{4,3,2,0,1:T(8,128)S(1)} %pad_maximum_fusion.16), channel_id=1, source_target_pairs={{0,1},{1,2},{2,3},{3,4},{4,5},{5,6},{6,7},{7,8},{8,9},{9,10},{10,1... | collective-permute-start | bytes 589832 | tf_op jit(solution)/shard_map/while/body/eval_jaxpr/ppermute | solution.py:21
  215.9 10.1 %collective-permute-start.3 = (f32[16,3,1,8,128]{4,3,2,0,1:T(8,128)S(1)}, f32[16,3,1,8,128]{4,3,2,0,1:T(8,128)S(1)}, u32[]{:S(2)}, u32[]{:S(2)}) collective-permute-start(f32[16,3,1,8,128]{4,3,2,0,1:T(8,128)S(1)} %pad_maximum_fusion.17), channel_id=1, source_target_pairs={{0,1},{1,2},{2,3},{3,4},{4,5},{5,6},{6,7},{7,8},{8,9},{9,10},{10,1... | collective-permute-start | bytes 589832 | tf_op jit(solution)/shard_map/while/body/eval_jaxpr/ppermute | solution.py:21
  228.0 5.1 collective-permute-start
  233.6 10.0 %collective-permute-start.1 = (f32[16,3,1,8,128]{4,3,2,0,1:T(8,128)S(1)}, f32[16,3,1,8,128]{4,3,2,0,1:T(8,128)S(1)}, u32[]{:S(2)}, u32[]{:S(2)}) collective-permute-start(f32[16,3,1,8,128]{4,3,2,0,1:T(8,128)S(1)} %pad_maximum_fusion.16), channel_id=1, source_target_pairs={{0,1},{1,2},{2,3},{3,4},{4,5},{5,6},{6,7},{7,8},{8,9},{9,10},{10,1... | collective-permute-start | bytes 589832 | tf_op jit(solution)/shard_map/while/body/eval_jaxpr/ppermute | solution.py:21
  249.6 10.1 %collective-permute-start.3 = (f32[16,3,1,8,128]{4,3,2,0,1:T(8,128)S(1)}, f32[16,3,1,8,128]{4,3,2,0,1:T(8,128)S(1)}, u32[]{:S(2)}, u32[]{:S(2)}) collective-permute-start(f32[16,3,1,8,128]{4,3,2,0,1:T(8,128)S(1)} %pad_maximum_fusion.17), channel_id=1, source_target_pairs={{0,1},{1,2},{2,3},{3,4},{4,5},{5,6},{6,7},{7,8},{8,9},{9,10},{10,1... | collective-permute-start | bytes 589832 | tf_op jit(solution)/shard_map/while/body/eval_jaxpr/ppermute | solution.py:21
  261.7 5.1 collective-permute-start
  267.2 10.0 %collective-permute-start.1 = (f32[16,3,1,8,128]{4,3,2,0,1:T(8,128)S(1)}, f32[16,3,1,8,128]{4,3,2,0,1:T(8,128)S(1)}, u32[]{:S(2)}, u32[]{:S(2)}) collective-permute-start(f32[16,3,1,8,128]{4,3,2,0,1:T(8,128)S(1)} %pad_maximum_fusion.16), channel_id=1, source_target_pairs={{0,1},{1,2},{2,3},{3,4},{4,5},{5,6},{6,7},{7,8},{8,9},{9,10},{10,1... | collective-permute-start | bytes 589832 | tf_op jit(solution)/shard_map/while/body/eval_jaxpr/ppermute | solution.py:21
  283.2 10.1 %collective-permute-start.3 = (f32[16,3,1,8,128]{4,3,2,0,1:T(8,128)S(1)}, f32[16,3,1,8,128]{4,3,2,0,1:T(8,128)S(1)}, u32[]{:S(2)}, u32[]{:S(2)}) collective-permute-start(f32[16,3,1,8,128]{4,3,2,0,1:T(8,128)S(1)} %pad_maximum_fusion.17), channel_id=1, source_target_pairs={{0,1},{1,2},{2,3},{3,4},{4,5},{5,6},{6,7},{7,8},{8,9},{9,10},{10,1... | collective-permute-start | bytes 589832 | tf_op jit(solution)/shard_map/while/body/eval_jaxpr/ppermute | solution.py:21
  295.3 5.1 collective-permute-start
  300.8 10.0 %collective-permute-start.1 = (f32[16,3,1,8,128]{4,3,2,0,1:T(8,128)S(1)}, f32[16,3,1,8,128]{4,3,2,0,1:T(8,128)S(1)}, u32[]{:S(2)}, u32[]{:S(2)}) collective-permute-start(f32[16,3,1,8,128]{4,3,2,0,1:T(8,128)S(1)} %pad_maximum_fusion.16), channel_id=1, source_target_pairs={{0,1},{1,2},{2,3},{3,4},{4,5},{5,6},{6,7},{7,8},{8,9},{9,10},{10,1... | collective-permute-start | bytes 589832 | tf_op jit(solution)/shard_map/while/body/eval_jaxpr/ppermute | solution.py:21
  316.7 10.1 %collective-permute-start.3 = (f32[16,3,1,8,128]{4,3,2,0,1:T(8,128)S(1)}, f32[16,3,1,8,128]{4,3,2,0,1:T(8,128)S(1)}, u32[]{:S(2)}, u32[]{:S(2)}) collective-permute-start(f32[16,3,1,8,128]{4,3,2,0,1:T(8,128)S(1)} %pad_maximum_fusion.17), channel_id=1, source_target_pairs={{0,1},{1,2},{2,3},{3,4},{4,5},{5,6},{6,7},{7,8},{8,9},{9,10},{10,1... | collective-permute-start | bytes 589832 | tf_op jit(solution)/shard_map/while/body/eval_jaxpr/ppermute | solution.py:21
  328.8 5.1 collective-permute-start
  334.4 10.0 %collective-permute-start.1 = (f32[16,3,1,8,128]{4,3,2,0,1:T(8,128)S(1)}, f32[16,3,1,8,128]{4,3,2,0,1:T(8,128)S(1)}, u32[]{:S(2)}, u32[]{:S(2)}) collective-permute-start(f32[16,3,1,8,128]{4,3,2,0,1:T(8,128)S(1)} %pad_maximum_fusion.16), channel_id=1, source_target_pairs={{0,1},{1,2},{2,3},{3,4},{4,5},{5,6},{6,7},{7,8},{8,9},{9,10},{10,1... | collective-permute-start | bytes 589832 | tf_op jit(solution)/shard_map/while/body/eval_jaxpr/ppermute | solution.py:21
  350.3 10.1 %collective-permute-start.3 = (f32[16,3,1,8,128]{4,3,2,0,1:T(8,128)S(1)}, f32[16,3,1,8,128]{4,3,2,0,1:T(8,128)S(1)}, u32[]{:S(2)}, u32[]{:S(2)}) collective-permute-start(f32[16,3,1,8,128]{4,3,2,0,1:T(8,128)S(1)} %pad_maximum_fusion.17), channel_id=1, source_target_pairs={{0,1},{1,2},{2,3},{3,4},{4,5},{5,6},{6,7},{7,8},{8,9},{9,10},{10,1... | collective-permute-start | bytes 589832 | tf_op jit(solution)/shard_map/while/body/eval_jaxpr/ppermute | solution.py:21
  362.4 5.1 collective-permute-start
  368.0 10.0 %collective-permute-start.1 = (f32[16,3,1,8,128]{4,3,2,0,1:T(8,128)S(1)}, f32[16,3,1,8,128]{4,3,2,0,1:T(8,128)S(1)}, u32[]{:S(2)}, u32[]{:S(2)}) collective-permute-start(f32[16,3,1,8,128]{4,3,2,0,1:T(8,128)S(1)} %pad_maximum_fusion.16), channel_id=1, source_target_pairs={{0,1},{1,2},{2,3},{3,4},{4,5},{5,6},{6,7},{7,8},{8,9},{9,10},{10,1... | collective-permute-start | bytes 589832 | tf_op jit(solution)/shard_map/while/body/eval_jaxpr/ppermute | solution.py:21
  383.9 10.1 %collective-permute-start.3 = (f32[16,3,1,8,128]{4,3,2,0,1:T(8,128)S(1)}, f32[16,3,1,8,128]{4,3,2,0,1:T(8,128)S(1)}, u32[]{:S(2)}, u32[]{:S(2)}) collective-permute-start(f32[16,3,1,8,128]{4,3,2,0,1:T(8,128)S(1)} %pad_maximum_fusion.17), channel_id=1, source_target_pairs={{0,1},{1,2},{2,3},{3,4},{4,5},{5,6},{6,7},{7,8},{8,9},{9,10},{10,1... | collective-permute-start | bytes 589832 | tf_op jit(solution)/shard_map/while/body/eval_jaxpr/ppermute | solution.py:21
  396.0 5.1 collective-permute-start
  401.5 10.0 %collective-permute-start.1 = (f32[16,3,1,8,128]{4,3,2,0,1:T(8,128)S(1)}, f32[16,3,1,8,128]{4,3,2,0,1:T(8,128)S(1)}, u32[]{:S(2)}, u32[]{:S(2)}) collective-permute-start(f32[16,3,1,8,128]{4,3,2,0,1:T(8,128)S(1)} %pad_maximum_fusion.16), channel_id=1, source_target_pairs={{0,1},{1,2},{2,3},{3,4},{4,5},{5,6},{6,7},{7,8},{8,9},{9,10},{10,1... | collective-permute-start | bytes 589832 | tf_op jit(solution)/shard_map/while/body/eval_jaxpr/ppermute | solution.py:21
  417.5 10.1 %collective-permute-start.3 = (f32[16,3,1,8,128]{4,3,2,0,1:T(8,128)S(1)}, f32[16,3,1,8,128]{4,3,2,0,1:T(8,128)S(1)}, u32[]{:S(2)}, u32[]{:S(2)}) collective-permute-start(f32[16,3,1,8,128]{4,3,2,0,1:T(8,128)S(1)} %pad_maximum_fusion.17), channel_id=1, source_target_pairs={{0,1},{1,2},{2,3},{3,4},{4,5},{5,6},{6,7},{7,8},{8,9},{9,10},{10,1... | collective-permute-start | bytes 589832 | tf_op jit(solution)/shard_map/while/body/eval_jaxpr/ppermute | solution.py:21
  435.1 10.0 %collective-permute-start.1 = (f32[16,3,1,8,128]{4,3,2,0,1:T(8,128)S(1)}, f32[16,3,1,8,128]{4,3,2,0,1:T(8,128)S(1)}, u32[]{:S(2)}, u32[]{:S(2)}) collective-permute-start(f32[16,3,1,8,128]{4,3,2,0,1:T(8,128)S(1)} %pad_maximum_fusion.16), channel_id=1, source_target_pairs={{0,1},{1,2},{2,3},{3,4},{4,5},{5,6},{6,7},{7,8},{8,9},{9,10},{10,1... | collective-permute-start | bytes 589832 | tf_op jit(solution)/shard_map/while/body/eval_jaxpr/ppermute | solution.py:21
  451.1 10.1 %collective-permute-start.3 = (f32[16,3,1,8,128]{4,3,2,0,1:T(8,128)S(1)}, f32[16,3,1,8,128]{4,3,2,0,1:T(8,128)S(1)}, u32[]{:S(2)}, u32[]{:S(2)}) collective-permute-start(f32[16,3,1,8,128]{4,3,2,0,1:T(8,128)S(1)} %pad_maximum_fusion.17), channel_id=1, source_target_pairs={{0,1},{1,2},{2,3},{3,4},{4,5},{5,6},{6,7},{7,8},{8,9},{9,10},{10,1... | collective-permute-start | bytes 589832 | tf_op jit(solution)/shard_map/while/body/eval_jaxpr/ppermute | solution.py:21
  468.7 10.0 %collective-permute-start.1 = (f32[16,3,1,8,128]{4,3,2,0,1:T(8,128)S(1)}, f32[16,3,1,8,128]{4,3,2,0,1:T(8,128)S(1)}, u32[]{:S(2)}, u32[]{:S(2)}) collective-permute-start(f32[16,3,1,8,128]{4,3,2,0,1:T(8,128)S(1)} %pad_maximum_fusion.16), channel_id=1, source_target_pairs={{0,1},{1,2},{2,3},{3,4},{4,5},{5,6},{6,7},{7,8},{8,9},{9,10},{10,1... | collective-permute-start | bytes 589832 | tf_op jit(solution)/shard_map/while/body/eval_jaxpr/ppermute | solution.py:21
  484.6 10.1 %collective-permute-start.3 = (f32[16,3,1,8,128]{4,3,2,0,1:T(8,128)S(1)}, f32[16,3,1,8,128]{4,3,2,0,1:T(8,128)S(1)}, u32[]{:S(2)}, u32[]{:S(2)}) collective-permute-start(f32[16,3,1,8,128]{4,3,2,0,1:T(8,128)S(1)} %pad_maximum_fusion.17), channel_id=1, source_target_pairs={{0,1},{1,2},{2,3},{3,4},{4,5},{5,6},{6,7},{7,8},{8,9},{9,10},{10,1... | collective-permute-start | bytes 589832 | tf_op jit(solution)/shard_map/while/body/eval_jaxpr/ppermute | solution.py:21
  502.3 10.0 %collective-permute-start.1 = (f32[16,3,1,8,128]{4,3,2,0,1:T(8,128)S(1)}, f32[16,3,1,8,128]{4,3,2,0,1:T(8,128)S(1)}, u32[]{:S(2)}, u32[]{:S(2)}) collective-permute-start(f32[16,3,1,8,128]{4,3,2,0,1:T(8,128)S(1)} %pad_maximum_fusion.16), channel_id=1, source_target_pairs={{0,1},{1,2},{2,3},{3,4},{4,5},{5,6},{6,7},{7,8},{8,9},{9,10},{10,1... | collective-permute-start | bytes 589832 | tf_op jit(solution)/shard_map/while/body/eval_jaxpr/ppermute | solution.py:21
  518.2 13.9 %collective-permute-start.3 = (f32[16,3,1,8,128]{4,3,2,0,1:T(8,128)S(1)}, f32[16,3,1,8,128]{4,3,2,0,1:T(8,128)S(1)}, u32[]{:S(2)}, u32[]{:S(2)}) collective-permute-start(f32[16,3,1,8,128]{4,3,2,0,1:T(8,128)S(1)} %pad_maximum_fusion.17), channel_id=1, source_target_pairs={{0,1},{1,2},{2,3},{3,4},{4,5},{5,6},{6,7},{7,8},{8,9},{9,10},{10,1... | collective-permute-start | bytes 589832 | tf_op jit(solution)/shard_map/while/body/eval_jaxpr/ppermute | solution.py:21
  535.0 17.1 %all-to-all-start.2 = ((f32[16,16,3,128]{3,0,2,1:T(8,128)}), f32[16,16,3,128]{3,0,2,1:T(8,128)S(1)}, u32[]{:S(2)}, u32[]{:S(2)}) async-start(f32[16,16,3,128]{3,0,2,1:T(8,128)} %bitcast.28), calls=%async_computation.2 | async-start | bytes 786432 | tf_op jit(solution)/shard_map/all_to_all | solution.py:167
  (22 other events, 290.2 us)
where the time goes:
time: 575 us; the launch traced here: 573 us
  waiting for transfers between devices  274 us (48%)
  blocking collectives  118 us (21%)
  starting transfers between devices  115 us (20%)
  other arithmetic  31.9 us (6%)
  local copies, waits for them, and re-layouts  27.7 us (5%)
    ppermute x46, waiting for transfers between devices, from_behind(): lax.ppermute(value, axis, [(source, source + steps) for source in range(i...  246 us
    psum x1, blocking collectives, broadcast(): return lax.psum(jnp.where(mine, array, jnp.zeros_like(array)), axis)  99.3 us
    ppermute x46, starting transfers between devices, from_behind(): lax.ppermute(value, axis, [(source, source + steps) for source in range(i...  90.1 us
    all_to_all x1, blocking collectives, per_device(): lax.all_to_all(spread_back, 'tm', split_axis=0, concat_axis=1, tiled=True)  18.2 us
    add x11, other arithmetic, sweep(): carry_terms[sweep_index] * direction + push_terms[sweep_index] * residual  17 us
    all_to_all x1, starting transfers between devices, per_device(): lax.all_to_all(flat, 'tm', split_axis=1, concat_axis=0, tiled=True)  15.7 us
    all_to_all x1, waiting for transfers between devices, per_device(): lax.all_to_all(flat, 'tm', split_axis=1, concat_axis=0, tiled=True)  14.4 us
    all_to_all x1, waiting for transfers between devices, per_device(): lax.all_to_all(solution, 'tm', split_axis=1, concat_axis=0, tiled=True)  13.5 us
  transfers between devices with their start and end apart: 49, of which 48 were waited for; matrix products, arithmetic and copies ran while one was open for 3% of the time, Pallas kernels for 0%

commit v1 on v0

v1 whole, which is shorter than its diff:
```python
import functools
import math

import jax
import jax.numpy as jnp
import numpy as np
from jax import lax
from jax.experimental import pallas as pl
from jax.experimental.pallas import tpu as pltpu
from jax.sharding import Mesh
from jax.sharding import PartitionSpec as P

SWEEPS = 12
ALPHA = 0.1
LOWER = 0.02
UPPER = 1.0
SIGMA_TOP = 4.0
CURL_TOP = 12.0

TM = ("yh", "z")
PAIRS = ("yl", "c", "yh", "z")
BLOCK = 16
REACH = 24
GUARD = 2


def tables(window):
    gamma = ALPHA ** (1.0 / window)
    half = window // 2
    pairs = np.arange(half)
    freqs = np.concatenate([pairs, np.where(pairs == 0, half, window - pairs)])
    moments = np.arange(window)
    angle = 2.0 * math.pi * (freqs[:, None] * moments[None, :] % window) / window
    cas = np.cos(angle) + np.sin(angle)
    forward = cas * gamma ** moments[None, :]
    inverse = cas.T * gamma ** (-moments[:, None]) / window
    return forward.astype(np.float32), inverse.astype(np.float32)


def pair_table(window):
    gamma = ALPHA ** (1.0 / window)
    pairs = np.arange(window // 2)
    theta = 2.0 * math.pi * pairs / window
    plain = 1.0 - gamma * np.cos(theta)
    p_plus = np.where(pairs == 0, 1.0 - gamma, plain)
    p_minus = np.where(pairs == 0, 1.0 + gamma, plain)
    q_term = np.where(pairs == 0, 0.0, gamma * np.sin(theta))
    bound = np.sqrt(np.maximum(p_plus, p_minus) ** 2 + q_term**2) * SIGMA_TOP + CURL_TOP
    return np.stack([p_plus, p_minus, q_term, 1.0 / bound**2]).astype(np.float32)


def chebyshev_terms(count):
    center = (UPPER + LOWER) / 2.0
    radius = (UPPER - LOWER) / 2.0
    spread_ratio = center / radius
    weight_now = 1.0 / spread_ratio
    carry_terms, push_terms = ([], [])
    for _ in range(count):
        weight_next = 1.0 / (2.0 * spread_ratio - weight_now)
        carry_terms.append(weight_next * weight_now)
        push_terms.append(2.0 * weight_next / radius)
        weight_now = weight_next
    return (carry_terms, push_terms, center)


def material(region, cond):
    return jnp.where(
        region == 0,
        cond[0],
        jnp.where(region == 1, cond[1], jnp.where(region == 2, cond[2], 0.0)),
    )


def pack_kernel(cond, forcing, start, latest, region, out):
    steps, comps, planes, ny, _ = forcing.shape
    rows = out.shape[0] // (planes * ny)
    is_first = (lax.axis_index("yh") == 0) & (lax.axis_index("z") == 0)
    for p in range(planes):
        sigma = material(region[p], cond)
        base = p * ny * rows
        for c in range(comps):
            head = forcing[0, c, p]
            head = head + jnp.where(is_first, sigma * start[c, p], 0.0)
            out[pl.ds(base + c * steps, ny, stride=rows), :] = head
            for b in range(1, steps):
                out[pl.ds(base + c * steps + b, ny, stride=rows), :] = forcing[b, c, p]
            out[pl.ds(base + comps * steps + c, ny, stride=rows), :] = -ALPHA * (
                sigma * latest[0, c, p]
            )
        for pad in range(comps * steps + comps, rows):
            out[pl.ds(base + pad, ny, stride=rows), :] = jnp.zeros_like(sigma)


def forward_kernel(cond, got, table, region, out):
    groups, _, nz = got.shape
    window = table.shape[0]
    steps = window // groups
    comps = 3
    half = window // 2
    head = lax.broadcasted_iota(jnp.int32, (window, nz), 0) == 0
    parts = []
    for c in range(comps):
        part = got[:, c * steps : (c + 1) * steps, :].reshape(window, nz)
        row = got[groups - 1, comps * steps + c : comps * steps + c + 1, :]
        parts.append(part + jnp.where(head, row, 0.0))
    spectrum = jnp.dot(
        table[...],
        jnp.concatenate(parts, axis=1),
        precision=lax.Precision.HIGHEST,
        preferred_element_type=jnp.float32,
    )
    width = comps * nz
    out[:, :width] = spectrum[:half]
    out[:, width : 2 * width] = spectrum[half:]
    line = region[lax.axis_index("yh"), pl.ds(lax.axis_index("z"), 1), :]
    out[:, 2 * width :] = jnp.broadcast_to(material(line, cond), (half, nz))


def inverse_kernel(got, table, out):
    half, wide = got.shape
    groups, rows, nz = out.shape
    steps = table.shape[0] // groups
    width = wide // 2
    dot = functools.partial(
        jnp.dot, precision=lax.Precision.HIGHEST, preferred_element_type=jnp.float32
    )
    result = dot(table[:, :half], got[:, :width]) + dot(table[:, half:], got[:, width:])
    for c in range(rows // steps):
        out[:, c * steps : (c + 1) * steps, :] = result[:, c * nz : (c + 1) * nz].reshape(
            groups, steps, nz
        )


def unpack_kernel(got, out):
    steps, comps, planes, ny, _ = out.shape
    rows = got.shape[0] // (planes * ny)
    for p in range(planes):
        for c in range(comps):
            for b in range(steps):
                out[b, c, p] = got[pl.ds(p * ny * rows + c * steps + b, ny, stride=rows), :]


def solve_kernel(terms, own, left, right, far, out, field, resid, total, sigma):
    ny, nz = field.shape[2:]
    x_at = lax.axis_index("x")
    pair = lax.axis_index(PAIRS)
    p_plus, p_minus = terms[0, pair], terms[1, pair]
    q_term, inv_scale = terms[2, pair], terms[3, pair]
    carry_terms, push_terms, center = chebyshev_terms(SWEEPS - 1)

    row = lax.broadcasted_iota(jnp.int32, (ny, nz), 0)
    lane = lax.broadcasted_iota(jnp.int32, (ny, nz), 1)
    row_first, row_last = row == 0, row == ny - 1
    lane_first, lane_last = lane == 0, lane == nz - 1

    def ahead_y(f):
        return jnp.where(row_last, 0.0, pltpu.roll(f, ny - 1, 0))

    def ahead_z(f):
        return jnp.where(lane_last, 0.0, pltpu.roll(f, nz - 1, 1))

    def behind_y(f):
        return jnp.where(row_first, 0.0, pltpu.roll(f, 1, 0))

    def behind_z(f):
        return jnp.where(lane_first, 0.0, pltpu.roll(f, 1, 1))

    def curl(now, after):
        ex, ey, ez = now
        _, ey_after, ez_after = after
        return (
            (ahead_y(ez) - ez) - (ahead_z(ey) - ey),
            (ahead_z(ex) - ex) - (ez_after - ez),
            (ey_after - ey) - (ahead_y(ex) - ex),
        )

    def adjoint(now, before):
        bx, by, bz = now
        by_before, bz_before = before
        return (
            (behind_z(by) - by) - (behind_y(bz) - bz),
            (bz_before - bz) - (behind_z(bx) - bx),
            (behind_y(bx) - bx) - (by_before - by),
        )

    def both(fn, one, two):
        return tuple(fn(one[3 * f : 3 * f + 3], two[two_at : two_at + len(two) // 2])
                     for f, two_at in ((0, 0), (1, len(two) // 2)))

    def curls(now, after):
        a, b = both(curl, now, after)
        return a + b

    def adjoints(now, before):
        a, b = both(adjoint, now, before)
        return a + b

    def tails(flux):
        return (flux[1], flux[2], flux[4], flux[5])

    def couple(values, weight, sign):
        sp, sm, sq = weight * p_plus, weight * p_minus, weight * (sign * q_term)
        up = tuple(sp * values[c] - sq * values[3 + c] for c in range(3))
        down = tuple(sm * values[3 + c] + sq * values[c] for c in range(3))
        return up + down

    def plus(a, b):
        return tuple(u + v for u, v in zip(a, b))

    def keep(flag, values):
        return tuple(jnp.where(flag, v, 0.0) for v in values)

    def load(ref, at):
        return tuple(ref[at + GUARD, k] for k in range(6))

    def store(ref, at, values):
        for k in range(6):
            ref[at + GUARD, k] = values[k]

    def fill(source, first, count):
        def one(i, _):
            line = pl.ds(pl.multiple_of(i * ny, ny), ny)
            for k in range(6):
                field[first + i + GUARD, k] = source[line, k * nz : (k + 1) * nz]
            sigma[first + i + GUARD] = source[line, 6 * nz : 7 * nz]
            return 0

        lax.fori_loop(0, count, one, 0)

    extra = far.shape[0] // ny
    low_far, high_far = REACH - BLOCK - extra, REACH + 2 * BLOCK
    blank = jnp.zeros((ny, nz), jnp.float32)
    for at in [*range(-GUARD, extra), *range(high_far, high_far + extra + GUARD)]:
        for k in range(6):
            field[at + GUARD, k] = blank
        sigma[at + GUARD] = blank
    fill(left, REACH - BLOCK, BLOCK)
    fill(own, REACH, BLOCK)
    fill(right, REACH + BLOCK, BLOCK)
    blocks = lax.axis_size("x")
    fill(far, jnp.where(x_at < blocks // 2, high_far, low_far), extra)

    grid_low = REACH - BLOCK * x_at
    grid_high = grid_low + BLOCK * blocks

    def bounds(margin):
        low = jnp.maximum(grid_low, REACH - margin)
        high = jnp.minimum(grid_high, REACH + BLOCK + margin)
        return low, high

    low, high = bounds(2 * (SWEEPS - 1))

    def start_step(i, state):
        now, before = state[:6], state[6:]
        after = load(field, i + 1)
        flux = curls(now, after)
        value = plus(adjoints(flux, before), couple(now, sigma[i + GUARD], -1.0))
        value = tuple(v * inv_scale for v in value)
        store(resid, i, value)
        store(field, i, tuple(v * (1.0 / center) for v in value))
        return after + tails(flux)

    before = tails(curls(load(field, low - 1), load(field, low)))
    before = keep(low > grid_low, before)
    lax.fori_loop(low, high, start_step, load(field, low) + before)

    def zero_total(i, _):
        for k in range(6):
            total[i, k] = blank
        return 0

    lax.fori_loop(0, BLOCK, zero_total, 0)

    for s in range(SWEEPS - 1):
        low, high = bounds(2 * (SWEEPS - 2 - s))
        keep_low, keep_high = low > grid_low, high < grid_high
        carry_term, push_term = carry_terms[s], push_terms[s]

        def add_total(i, _):
            for k in range(6):
                total[i, k] = total[i, k] + field[i + REACH + GUARD, k]
            return 0

        lax.fori_loop(0, BLOCK, add_total, 0)

        def advance(i, now, before, after):
            flux = curls(now, after)
            return plus(adjoints(flux, before), couple(now, sigma[i + GUARD], 1.0)), tails(flux)

        def finish(i, first_now, first_after, before):
            flux = curls(first_now, first_after)
            value = plus(adjoints(flux, before), couple(first_now, sigma[i + GUARD], -1.0))
            rest = tuple(r - v * inv_scale for r, v in zip(load(resid, i), value))
            store(resid, i, rest)
            store(
                field,
                i,
                tuple(carry_term * d + push_term * r for d, r in zip(load(field, i), rest)),
            )
            return tails(flux)

        def sweep_step(i, state):
            now, before, first, first_before = (
                state[:6],
                state[6:10],
                state[10:16],
                state[16:20],
            )
            after = load(field, i + 1)
            first_after, before = advance(i, now, before, after)
            first_before = finish(i - 1, first, first_after, first_before)
            return after + before + first_after + first_before

        now = load(field, low - 1)
        before = tails(curls(load(field, low - 2), now))
        after = load(field, low)
        first_low, before = advance(low - 1, now, before, after)
        before = keep(keep_low, before)
        now, after = after, load(field, low + 1)
        first, before = advance(low, now, before, after)
        first_before = keep(keep_low, tails(curls(first_low, first)))
        now, before, first, first_before = (
            lambda st: (st[:6], st[6:10], st[10:16], st[16:20])
        )(lax.fori_loop(low + 1, high, sweep_step, after + before + first + first_before))
        last, _ = advance(high, now, before, load(field, high + 1))
        finish(high - 1, first, keep(keep_high, last), first_before)

    def write(i, _):
        line = pl.ds(pl.multiple_of(i * ny, ny), ny)
        for k in range(6):
            out[line, k * nz : (k + 1) * nz] = total[i, k] + field[i + REACH + GUARD, k]
        return 0

    lax.fori_loop(0, BLOCK, write, 0)


def per_device(forcing, start_field, iterate, region, conductance):
    steps, comps, planes, ny, nz = forcing.shape
    groups = lax.axis_size(TM)
    window = steps * groups
    half = window // 2
    forward_table, inverse_table = tables(window)
    vmem = pl.BlockSpec(memory_space=pltpu.VMEM)
    smem = pl.BlockSpec(memory_space=pltpu.SMEM)
    f32 = jnp.float32
    params = pltpu.CompilerParams(vmem_limit_bytes=32 * 1024 * 1024)

    rows = comps * steps + 8
    whole = lambda shape: pl.BlockSpec(shape, lambda i: (0,) * len(shape))
    packed = pl.pallas_call(
        pack_kernel,
        out_shape=jax.ShapeDtypeStruct((groups * rows, nz), f32),
        grid=(1,),
        in_specs=[
            smem,
            whole(forcing.shape),
            whole(start_field.shape),
            pl.BlockSpec((1, comps, planes, ny, nz), lambda i: (steps - 1, 0, 0, 0, 0)),
            whole(region.shape),
        ],
        out_specs=whole((groups * rows, nz)),
        compiler_params=params,
        name="pack",
    )(conductance, forcing, start_field, iterate, region)

    got = lax.all_to_all(packed.reshape(groups, rows, nz), TM, 0, 0, tiled=True)

    spectrum = pl.pallas_call(
        forward_kernel,
        out_shape=jax.ShapeDtypeStruct((half, (2 * comps + 1) * nz), f32),
        in_specs=[smem, vmem, vmem, vmem],
        out_specs=vmem,
        compiler_params=params,
        name="forward",
    )(conductance, got, jnp.asarray(forward_table), region)

    own = lax.all_to_all(spectrum, PAIRS, 0, 0, tiled=True)

    count = lax.axis_size("x")
    x_at = lax.axis_index("x")
    left = lax.ppermute(own, "x", [(i, i + 1) for i in range(count - 1)])
    right = lax.ppermute(own, "x", [(i + 1, i) for i in range(count - 1)])
    part = lax.dynamic_slice_in_dim(
        own, jnp.where(x_at < count // 2, half // 2, 0), half // 2, 0
    )
    far = lax.ppermute(part, "x", [(i, (i + 2) % count) for i in range(count)])

    places = 2 * REACH + BLOCK + 2 * GUARD
    solved = pl.pallas_call(
        solve_kernel,
        out_shape=jax.ShapeDtypeStruct((half, 2 * comps * nz), f32),
        in_specs=[smem, vmem, vmem, vmem, vmem],
        out_specs=vmem,
        scratch_shapes=[
            pltpu.VMEM((places, 6, ny, nz), f32),
            pltpu.VMEM((places, 6, ny, nz), f32),
            pltpu.VMEM((BLOCK, 6, ny, nz), f32),
            pltpu.VMEM((places, ny, nz), f32),
        ],
        compiler_params=params,
        name="solve",
    )(jnp.asarray(pair_table(window)), own, left, right, far)

    back = lax.all_to_all(solved, PAIRS, 0, 0, tiled=True)

    pencil = pl.pallas_call(
        inverse_kernel,
        out_shape=jax.ShapeDtypeStruct((groups, comps * steps, nz), f32),
        in_specs=[vmem, vmem],
        out_specs=vmem,
        compiler_params=params,
        name="inverse",
    )(back, jnp.asarray(inverse_table))

    home = lax.all_to_all(pencil, TM, 0, 0, tiled=True)

    return pl.pallas_call(
        unpack_kernel,
        out_shape=jax.ShapeDtypeStruct(forcing.shape, f32),
        in_specs=[vmem],
        out_specs=vmem,
        compiler_params=params,
        name="unpack",
    )(home.reshape(groups * comps * steps, nz))


def solution(mesh):
    fine = Mesh(mesh.devices.reshape(2, 8, 4, 4, 2), ("yh", "z", "x", "yl", "c"))
    space = ("x", "yl", "c")
    placed = (
        P(TM, None, space, None, None),
        P(None, space, None, None),
        P(TM, None, space, None, None),
        P(space, None, None),
        P(),
    )
    return jax.shard_map(
        per_device,
        mesh=fine,
        in_specs=placed,
        out_specs=P(TM, None, space, None, None),
        check_vma=False,
    )
```

time: 575 us -> 210 us (0.37)
  the two profiles are of different devices: /device:TPU:2 before, /device:TPU:20 now
where the time goes in v1:
time: 210 us; the launch traced here: 209 us
  blocking collectives  104 us (50%)
  Pallas kernels  77 us (37%)
  waiting for transfers between devices  13.4 us (6%)
  starting transfers between devices  8.28 us (4%)
  local copies, waits for them, and re-layouts  6.05 us (3%)
    pallas_call x1, Pallas kernels, per_device(): pl.pallas_call(solve_kernel, out_shape=jax.ShapeDtypeStruct((half, 2 * co...  73.6 us
    all_to_all x1, blocking collectives, per_device(): got = lax.all_to_all(packed.reshape(groups, rows, nz), TM, 0, 0, tiled=True)  33.3 us
    all_to_all x1, blocking collectives, per_device(): own = lax.all_to_all(spectrum, PAIRS, 0, 0, tiled=True)  25.9 us
    all_to_all x1, blocking collectives, per_device(): back = lax.all_to_all(solved, PAIRS, 0, 0, tiled=True)  22.9 us
    all_to_all x1, blocking collectives, per_device(): home = lax.all_to_all(pencil, TM, 0, 0, tiled=True)  22.4 us
    ppermute x1, waiting for transfers between devices, per_device(): far = lax.ppermute(part, 'x', [(i, (i + 2) % count) for i in range(count)])  13.4 us
    unnamed x21, local copies, waits for them, and re-layouts  5.09 us
  transfers between devices with their start and end apart: 3, of which 1 were waited for; matrix products, arithmetic and copies ran while one was open for 0% of the time, Pallas kernels for 0%

profile of v1, /device:TPU:20, one launch (start us, length us, event | category | flops | bytes accessed | tf_op | source)
XLA Modules:
  0.0 209.3 jit_solution(1181862006656804648)
XLA Ops:
  0.0 0.0 copy-start
  0.0 1.0 copy-done
  1.0 1.0 copy-done.1
  2.0 0.0 copy-start.4
  2.0 0.7 copy-done.4
  2.7 0.7 copy-done.6
  3.4 0.7 copy-done.8
  4.1 0.6 pack.1
  4.7 0.0 copy-start.3
  4.7 0.0 copy-start.5
  4.7 33.3 %all_to_all.32.got = f32[16,56,128]{2,1,0:T(8,128)S(1)} all-to-all(f32[16,56,128]{2,1,0:T(8,128)S(1)} %bitcast.17), channel_id=1, replica_groups=mesh['yh'=2,'z'=8,'x'=4,'yl'=4,'c'=2] {'yh','z'}, dimensions={0} | all-to-all | bytes 917504 | tf_op jit(solution)/shard_map/all_to_all | solution.py:366
  38.1 0.0 copy-done.3
  38.1 0.0 copy-done.5
  38.1 1.1 forward.1
  39.2 0.5 copy.9
  39.7 25.9 %all_to_all.33 = f32[128,1,896]{2,1,0:T(1,128)S(1)} all-to-all(f32[128,1,896]{2,1,0:T(1,128)S(1)} %copy.9), channel_id=1, replica_groups=mesh['yh'=2,'z'=8,'x'=4,'yl'=4,'c'=2] {'yl','c','yh','z'}, dimensions={0} | all-to-all | bytes 917504 | tf_op jit(solution)/shard_map/all_to_all | solution.py:377
  65.6 2.4 %collective-permute-start.1 = (f32[128,896]{1,0:T(8,128)S(1)}, f32[128,896]{1,0:T(8,128)S(1)}, u32[]{:S(2)}, u32[]{:S(2)}) collective-permute-start(f32[128,896]{1,0:T(8,128)S(1)} %bitcast.13), channel_id=1, source_target_pairs={{8,0},{16,8},{24,16},{9,1},{17,9},{25,17},{10,2},{18,10},{26,18},{... | collective-permute-start | bytes 1376264 | tf_op jit(solution)/shard_map/ppermute | solution.py:382
  68.0 3.4 %collective-permute-start = (f32[128,896]{1,0:T(8,128)S(1)}, f32[128,896]{1,0:T(8,128)S(1)}, u32[]{:S(2)}, u32[]{:S(2)}) collective-permute-start(f32[128,896]{1,0:T(8,128)S(1)} %bitcast.14), channel_id=1, source_target_pairs={{0,8},{8,16},{16,24},{1,9},{9,17},{17,25},{2,10},{10,18},{18,26},{... | collective-permute-start | bytes 1376264 | tf_op jit(solution)/shard_map/ppermute | solution.py:381
  71.5 0.1 constant_dynamic-slice_fusion
  71.6 0.0 copy-start.7
  71.6 2.4 %collective-permute-start.2 = (f32[64,896]{1,0:T(8,128)S(1)}, f32[64,896]{1,0:T(8,128)S(1)}, u32[]{:S(2)}, u32[]{:S(2)}) collective-permute-start(f32[64,896]{1,0:T(8,128)S(1)} %bitcast.21), channel_id=1, source_target_pairs={{0,16},{8,24},{16,0},{24,8},{1,17},{9,25},{17,1},{25,9},{2,18},{10... | collective-permute-start | bytes 688136 | tf_op jit(solution)/shard_map/ppermute | solution.py:386
  74.0 13.4 %collective-permute-done.2.far = f32[64,896]{1,0:T(8,128)S(1)} collective-permute-done((f32[64,896]{1,0:T(8,128)S(1)}, f32[64,896]{1,0:T(8,128)S(1)}, u32[]{:S(2)}, u32[]{:S(2)}) %collective-permute-start.2) | collective-permute-done | bytes 229408 | tf_op jit(solution)/shard_map/ppermute | solution.py:386
  87.4 0.0 collective-permute-done.1.right
  87.4 0.0 collective-permute-done.left
  87.4 0.0 copy-done.7
  87.5 73.6 %solve.1 = f32[128,768]{1,0:T(8,128)S(1)} custom-call(f32[4,128]{1,0:T(4,128)S(1)} %copy-done.7, f32[128,896]{1,0:T(8,128)S(1)} %bitcast.15, f32[128,896]{1,0:T(8,128)S(1)} %collective-permute-done.left, f32[128,896]{1,0:T(8,128)S(1)} %collective-permute-done.1.right, f32[64,896]{1,0:T(8,128)S(1)} %collective-permute-done.2.far), custom_call_target="tpu_custom_call" | custom-call | tf_op jit(solution)/shard_map/solve/pallas_call | solution.py:389
  161.0 0.4 copy.10
  161.5 22.9 %all_to_all.34 = f32[128,1,768]{2,1,0:T(1,128)S(1)} all-to-all(f32[128,1,768]{2,1,0:T(1,128)S(1)} %copy.10), channel_id=1, replica_groups=mesh['yh'=2,'z'=8,'x'=4,'yl'=4,'c'=2] {'yl','c','yh','z'}, dimensions={0} | all-to-all | bytes 786432 | tf_op jit(solution)/shard_map/all_to_all | solution.py:404
  184.3 0.9 copy-done.2
  185.3 0.8 inverse.1
  186.0 22.4 %all_to_all.35 = f32[16,48,128]{2,1,0:T(8,128)S(1)} all-to-all(f32[16,48,128]{2,1,0:T(8,128)S(1)} %inverse.1), channel_id=1, replica_groups=mesh['yh'=2,'z'=8,'x'=4,'yl'=4,'c'=2] {'yh','z'}, dimensions={0} | all-to-all | bytes 786432 | tf_op jit(solution)/shard_map/all_to_all | solution.py:415
  208.4 0.9 unpack.1
  (7 shorter events, 0.1 us)
Async XLA Ops:
  0.0 1.0 copy-start
  1.0 1.0 copy-start.1
  2.0 0.7 copy-start.4
  2.7 0.7 copy-start.6
  3.4 0.7 copy-start.8
  4.7 33.4 %copy-start.3 = (f32[256,256]{1,0:T(8,128)S(1)}, f32[256,256]{1,0:T(8,128)}, u32[]{:S(2)}) copy-start(f32[256,256]{1,0:T(8,128)} %constant.20.clone.table) | copy-start | bytes 786436
  4.7 33.3 %copy-start.5 = (s32[2,8,128]{2,1,0:T(8,128)S(1)}, s32[2,8,128]{2,1,0:T(8,128)}, u32[]{:S(2)}) copy-start(s32[2,8,128]{2,1,0:T(8,128)} %region.3) | copy-start | bytes 24580
  65.6 21.9 %collective-permute-start.1 = (f32[128,896]{1,0:T(8,128)S(1)}, f32[128,896]{1,0:T(8,128)S(1)}, u32[]{:S(2)}, u32[]{:S(2)}) collective-permute-start(f32[128,896]{1,0:T(8,128)S(1)} %bitcast.13), channel_id=1, source_target_pairs={{8,0},{16,8},{24,16},{9,1},{17,9},{25,17},{10,2},{18,10},{26,18},{... | collective-permute-start | bytes 1376264 | tf_op jit(solution)/shard_map/ppermute | solution.py:382
  68.0 19.4 %collective-permute-start = (f32[128,896]{1,0:T(8,128)S(1)}, f32[128,896]{1,0:T(8,128)S(1)}, u32[]{:S(2)}, u32[]{:S(2)}) collective-permute-start(f32[128,896]{1,0:T(8,128)S(1)} %bitcast.14), channel_id=1, source_target_pairs={{0,8},{8,16},{16,24},{1,9},{9,17},{17,25},{2,10},{10,18},{18,26},{... | collective-permute-start | bytes 1376264 | tf_op jit(solution)/shard_map/ppermute | solution.py:381
  71.6 15.9 %copy-start.7 = (f32[4,128]{1,0:T(4,128)S(1)}, f32[4,128]{1,0:T(4,128)}, u32[]{:S(2)}) copy-start(f32[4,128]{1,0:T(4,128)} %constant.21.clone.terms) | copy-start | bytes 6148
  71.6 15.8 %collective-permute-start.2 = (f32[64,896]{1,0:T(8,128)S(1)}, f32[64,896]{1,0:T(8,128)S(1)}, u32[]{:S(2)}, u32[]{:S(2)}) collective-permute-start(f32[64,896]{1,0:T(8,128)S(1)} %bitcast.21), channel_id=1, source_target_pairs={{0,16},{8,24},{16,0},{24,8},{1,17},{9,25},{17,1},{25,9},{2,18},{10... | collective-permute-start | bytes 688136 | tf_op jit(solution)/shard_map/ppermute | solution.py:386
  184.3 1.0 copy-start.2

commit v2 on v1

v2 whole, which is shorter than its diff:
```python
import functools
import math

import jax
import jax.numpy as jnp
import numpy as np
from jax import lax
from jax.experimental import pallas as pl
from jax.experimental.pallas import tpu as pltpu
from jax.sharding import Mesh
from jax.sharding import PartitionSpec as P

SWEEPS = 12
ALPHA = 0.1
LOWER = 0.02
UPPER = 1.0
SIGMA_TOP = 4.0
CURL_TOP = 12.0

TM = ("yh", "z")
PAIRS = ("yl", "c", "yh", "z")
BLOCK = 16
REACH = 24
GUARD = 1
CHUNK = 8


def tables(window):
    gamma = ALPHA ** (1.0 / window)
    half = window // 2
    pairs = np.arange(half)
    freqs = np.concatenate([pairs, np.where(pairs == 0, half, window - pairs)])
    moments = np.arange(window)
    angle = 2.0 * math.pi * (freqs[:, None] * moments[None, :] % window) / window
    cas = np.cos(angle) + np.sin(angle)
    forward = cas * gamma ** moments[None, :]
    inverse = cas.T * gamma ** (-moments[:, None]) / window
    return forward.astype(np.float32), inverse.astype(np.float32)


def pair_table(window):
    gamma = ALPHA ** (1.0 / window)
    pairs = np.arange(window // 2)
    theta = 2.0 * math.pi * pairs / window
    plain = 1.0 - gamma * np.cos(theta)
    p_plus = np.where(pairs == 0, 1.0 - gamma, plain)
    p_minus = np.where(pairs == 0, 1.0 + gamma, plain)
    q_term = np.where(pairs == 0, 0.0, gamma * np.sin(theta))
    bound = np.sqrt(np.maximum(p_plus, p_minus) ** 2 + q_term**2) * SIGMA_TOP + CURL_TOP
    return np.stack([p_plus, p_minus, q_term, 1.0 / bound**2]).astype(np.float32)


def chebyshev_terms(count):
    center = (UPPER + LOWER) / 2.0
    radius = (UPPER - LOWER) / 2.0
    spread_ratio = center / radius
    weight_now = 1.0 / spread_ratio
    carry_terms, push_terms = ([], [])
    for _ in range(count):
        weight_next = 1.0 / (2.0 * spread_ratio - weight_now)
        carry_terms.append(weight_next * weight_now)
        push_terms.append(2.0 * weight_next / radius)
        weight_now = weight_next
    return (carry_terms, push_terms, center)


def material(region, cond):
    return jnp.where(
        region == 0,
        cond[0],
        jnp.where(region == 1, cond[1], jnp.where(region == 2, cond[2], 0.0)),
    )


def pack_kernel(cond, forcing, start, latest, region, out):
    steps, comps, planes, ny, _ = forcing.shape
    rows = out.shape[0] // (planes * ny)
    is_first = (lax.axis_index("yh") == 0) & (lax.axis_index("z") == 0)
    for p in range(planes):
        sigma = material(region[p], cond)
        base = p * ny * rows
        for c in range(comps):
            head = forcing[0, c, p]
            head = head + jnp.where(is_first, sigma * start[c, p], 0.0)
            out[pl.ds(base + c * steps, ny, stride=rows), :] = head
            for b in range(1, steps):
                out[pl.ds(base + c * steps + b, ny, stride=rows), :] = forcing[b, c, p]
            out[pl.ds(base + comps * steps + c, ny, stride=rows), :] = -ALPHA * (
                sigma * latest[0, c, p]
            )
        for pad in range(comps * steps + comps, rows):
            out[pl.ds(base + pad, ny, stride=rows), :] = jnp.zeros_like(sigma)


def forward_kernel(got, table, out):
    groups, _, nz = got.shape
    window = table.shape[0]
    steps = window // groups
    comps = 3
    half = window // 2
    head = lax.broadcasted_iota(jnp.int32, (window, nz), 0) == 0
    parts = []
    for c in range(comps):
        part = got[:, c * steps : (c + 1) * steps, :].reshape(window, nz)
        row = got[groups - 1, comps * steps + c : comps * steps + c + 1, :]
        parts.append(part + jnp.where(head, row, 0.0))
    spectrum = jnp.dot(
        table[...],
        jnp.concatenate(parts, axis=1),
        precision=lax.Precision.HIGHEST,
        preferred_element_type=jnp.float32,
    )
    width = comps * nz
    out[:, :width] = spectrum[:half]
    out[:, width:] = spectrum[half:]


def inverse_kernel(got, table, out):
    half, wide = got.shape
    groups, rows, nz = out.shape
    steps = table.shape[0] // groups
    width = wide // 2
    dot = functools.partial(
        jnp.dot, precision=lax.Precision.HIGHEST, preferred_element_type=jnp.float32
    )
    result = dot(table[:, :half], got[:, :width]) + dot(table[:, half:], got[:, width:])
    for c in range(rows // steps):
        out[:, c * steps : (c + 1) * steps, :] = result[:, c * nz : (c + 1) * nz].reshape(
            groups, steps, nz
        )


def unpack_kernel(got, out):
    steps, comps, planes, ny, _ = out.shape
    rows = got.shape[0] // (planes * ny)
    for p in range(planes):
        for c in range(comps):
            for b in range(steps):
                out[b, c, p] = got[pl.ds(p * ny * rows + c * steps + b, ny, stride=rows), :]


def solve_kernel(terms, cond, region, own, left, right, far, out, field, first, resid, total, sigma):
    ny, nz = field.shape[2:]
    x_at = lax.axis_index("x")
    pair = lax.axis_index(PAIRS)
    p_plus, p_minus = terms[0, pair], terms[1, pair]
    q_term, inv_scale = terms[2, pair], terms[3, pair]
    carry_terms, push_terms, center = chebyshev_terms(SWEEPS - 1)

    row = lax.broadcasted_iota(jnp.int32, (ny, nz), 0)
    lane = lax.broadcasted_iota(jnp.int32, (ny, nz), 1)
    row_first, row_last = row == 0, row == ny - 1
    lane_first, lane_last = lane == 0, lane == nz - 1
    blank = jnp.zeros((ny, nz), jnp.float32)

    def ahead_y(f):
        return jnp.where(row_last, 0.0, pltpu.roll(f, ny - 1, 0))

    def ahead_z(f):
        return jnp.where(lane_last, 0.0, pltpu.roll(f, nz - 1, 1))

    def behind_y(f):
        return jnp.where(row_first, 0.0, pltpu.roll(f, 1, 0))

    def behind_z(f):
        return jnp.where(lane_first, 0.0, pltpu.roll(f, 1, 1))

    def curls(now, after):
        flux = []
        for f in (0, 3):
            ex, ey, ez = now[f : f + 3]
            _, ey_after, ez_after = after[f : f + 3]
            flux += [
                (ahead_y(ez) - ez) - (ahead_z(ey) - ey),
                (ahead_z(ex) - ex) - (ez_after - ez),
                (ey_after - ey) - (ahead_y(ex) - ex),
            ]
        return flux

    def tails(now, after):
        flux = []
        for f in (0, 3):
            ex, ey, ez = now[f : f + 3]
            _, ey_after, ez_after = after[f : f + 3]
            flux += [
                (ahead_z(ex) - ex) - (ez_after - ez),
                (ey_after - ey) - (ahead_y(ex) - ex),
            ]
        return flux

    def adjoints(flux, before):
        field = []
        for f, g in ((0, 0), (3, 2)):
            bx, by, bz = flux[f : f + 3]
            by_before, bz_before = before[g : g + 2]
            field += [
                (behind_z(by) - by) - (behind_y(bz) - bz),
                (bz_before - bz) - (behind_z(bx) - bx),
                (behind_y(bx) - bx) - (by_before - by),
            ]
        return field

    def add_couple(field, values, weight, sign):
        sp, sm, sq = weight * p_plus, weight * p_minus, weight * (sign * q_term)
        return [
            field[c] + (sp * values[c] - sq * values[3 + c]) for c in range(3)
        ] + [field[3 + c] + (sm * values[3 + c] + sq * values[c]) for c in range(3)]

    def load(ref, at):
        return [ref[at + GUARD, k] for k in range(6)]

    def store(ref, at, values):
        for k in range(6):
            ref[at + GUARD, k] = values[k]

    blocks = lax.axis_size("x")
    width = 2 * REACH + BLOCK
    grid_low = REACH - BLOCK * x_at
    grid_high = grid_low + BLOCK * blocks
    top = jnp.minimum(grid_high, width)

    def fill(source, begin, count):
        def some(t, _):
            for u in range(CHUNK):
                i = t * CHUNK + u
                line = pl.ds(pl.multiple_of(i * ny, ny), ny)
                store(first, begin + i, [source[line, k * nz : (k + 1) * nz] for k in range(6)])
            return 0

        lax.fori_loop(0, count // CHUNK, some, 0)

    extra = far.shape[0] // ny
    low_far, high_far = 0, REACH + 2 * BLOCK
    for at in [*range(-1, extra), *range(high_far, high_far + extra + 1)]:
        store(first, at, [blank] * 6)
    fill(left, REACH - BLOCK, BLOCK)
    fill(own, REACH, BLOCK)
    fill(right, REACH + BLOCK, BLOCK)
    fill(far, jnp.where(x_at < blocks // 2, high_far, low_far), extra)
    store(field, top, [blank] * 6)
    store(field, -1, [blank] * 6)

    def bounds(margin):
        margin = -(-margin // CHUNK) * CHUNK
        low = jnp.maximum(grid_low, REACH - margin)
        high = jnp.minimum(grid_high, REACH + BLOCK + margin)
        return low, high

    def run(margin, source, sign, finish):
        low, high = bounds(margin)

        def some(t, _):
            begin = low + t * CHUNK
            now = load(source, begin)
            before = tails(load(source, begin - 1), now)
            before = [jnp.where(begin > grid_low, v, 0.0) for v in before]
            for u in range(CHUNK):
                i = begin + u
                after = load(source, i + 1)
                flux = curls(now, after)
                value = adjoints(flux, before)
                finish(i, add_couple(value, now, sigma[i + GUARD], sign))
                now, before = after, [flux[1], flux[2], flux[4], flux[5]]
            return 0

        lax.fori_loop(0, (high - low) // CHUNK, some, 0)

    low, high = bounds(REACH)

    def fill_sigma(t, _):
        for u in range(CHUNK):
            i = low + t * CHUNK + u
            sigma[i + GUARD] = material(region[i - grid_low], cond)
        return 0

    lax.fori_loop(0, (high - low) // CHUNK, fill_sigma, 0)

    def begin_with(i, value):
        store(resid, i, value)
        store(field, i, [v * (inv_scale * (1.0 / center)) for v in value])

    run(2 * (SWEEPS - 1), first, -1.0, begin_with)

    for s in range(SWEEPS - 1):
        margin = 2 * (SWEEPS - 2 - s)
        carry_term, push_term = carry_terms[s], push_terms[s] * inv_scale

        def add_total(t, _):
            for u in range(CHUNK):
                i = t * CHUNK + u
                for k in range(6):
                    step = field[i + REACH + GUARD, k]
                    total[i, k] = step if s == 0 else total[i, k] + step
            return 0

        lax.fori_loop(0, BLOCK // CHUNK, add_total, 0)

        def keep_first(i, value):
            store(first, i, value)

        def update(i, value):
            rest = [r - v for r, v in zip(load(resid, i), value)]
            store(resid, i, rest)
            store(
                field,
                i,
                [carry_term * d + push_term * r for d, r in zip(load(field, i), rest)],
            )

        run(margin + 1, field, 1.0, keep_first)
        run(margin, first, -1.0, update)

    def write(t, _):
        for u in range(CHUNK):
            i = t * CHUNK + u
            line = pl.ds(pl.multiple_of(i * ny, ny), ny)
            for k in range(6):
                out[line, k * nz : (k + 1) * nz] = total[i, k] + field[i + REACH + GUARD, k]
        return 0

    lax.fori_loop(0, BLOCK // CHUNK, write, 0)


def per_device(forcing, start_field, iterate, region, conductance):
    steps, comps, planes, ny, nz = forcing.shape
    groups = lax.axis_size(TM)
    window = steps * groups
    half = window // 2
    forward_table, inverse_table = tables(window)
    vmem = pl.BlockSpec(memory_space=pltpu.VMEM)
    smem = pl.BlockSpec(memory_space=pltpu.SMEM)
    f32 = jnp.float32
    params = pltpu.CompilerParams(vmem_limit_bytes=12 * 1024 * 1024)
    materials = lax.all_gather(region, ("x", "yl", "c"), axis=0, tiled=True)

    rows = comps * steps + 8
    whole = lambda shape: pl.BlockSpec(shape, lambda i: (0,) * len(shape))
    packed = pl.pallas_call(
        pack_kernel,
        out_shape=jax.ShapeDtypeStruct((groups * rows, nz), f32),
        grid=(1,),
        in_specs=[
            smem,
            whole(forcing.shape),
            whole(start_field.shape),
            pl.BlockSpec((1, comps, planes, ny, nz), lambda i: (steps - 1, 0, 0, 0, 0)),
            whole(region.shape),
        ],
        out_specs=whole((groups * rows, nz)),
        compiler_params=pltpu.CompilerParams(vmem_limit_bytes=60 * 1024 * 1024),
        name="pack",
    )(conductance, forcing, start_field, iterate, region)

    got = lax.all_to_all(packed.reshape(groups, rows, nz), TM, 0, 0, tiled=True)

    spectrum = pl.pallas_call(
        forward_kernel,
        out_shape=jax.ShapeDtypeStruct((half, 2 * comps * nz), f32),
        in_specs=[vmem, vmem],
        out_specs=vmem,
        compiler_params=params,
        name="forward",
    )(got, jnp.asarray(forward_table))

    own = lax.all_to_all(spectrum, PAIRS, 0, 0, tiled=True)
    own, materials = lax.optimization_barrier((own, materials))

    count = lax.axis_size("x")
    x_at = lax.axis_index("x")
    left = lax.ppermute(own, "x", [(i, i + 1) for i in range(count - 1)])
    right = lax.ppermute(own, "x", [(i + 1, i) for i in range(count - 1)])
    part = lax.dynamic_slice_in_dim(
        own, jnp.where(x_at < count // 2, half // 2, 0), half // 2, 0
    )
    far = lax.ppermute(part, "x", [(i, (i + 2) % count) for i in range(count)])

    places = 2 * REACH + BLOCK + 2 * GUARD
    solved = pl.pallas_call(
        solve_kernel,
        out_shape=jax.ShapeDtypeStruct((half, 2 * comps * nz), f32),
        in_specs=[smem, smem, vmem, vmem, vmem, vmem, vmem],
        out_specs=vmem,
        scratch_shapes=[
            pltpu.VMEM((places, 6, ny, nz), f32),
            pltpu.VMEM((places, 6, ny, nz), f32),
            pltpu.VMEM((places, 6, ny, nz), f32),
            pltpu.VMEM((BLOCK, 6, ny, nz), f32),
            pltpu.VMEM((places, ny, nz), f32),
        ],
        compiler_params=params,
        name="solve",
    )(jnp.asarray(pair_table(window)), conductance, materials, own, left, right, far)

    back = lax.all_to_all(solved, PAIRS, 0, 0, tiled=True)

    pencil = pl.pallas_call(
        inverse_kernel,
        out_shape=jax.ShapeDtypeStruct((groups, comps * steps, nz), f32),
        in_specs=[vmem, vmem],
        out_specs=vmem,
        compiler_params=params,
        name="inverse",
    )(back, jnp.asarray(inverse_table))

    home = lax.all_to_all(pencil, TM, 0, 0, tiled=True)

    return pl.pallas_call(
        unpack_kernel,
        out_shape=jax.ShapeDtypeStruct(forcing.shape, f32),
        in_specs=[vmem],
        out_specs=vmem,
        compiler_params=params,
        name="unpack",
    )(home.reshape(groups * comps * steps, nz))


def solution(mesh):
    fine = Mesh(mesh.devices.reshape(2, 8, 4, 4, 2), ("yh", "z", "x", "yl", "c"))
    space = ("x", "yl", "c")
    placed = (
        P(TM, None, space, None, None),
        P(None, space, None, None),
        P(TM, None, space, None, None),
        P(space, None, None),
        P(),
    )
    return jax.shard_map(
        per_device,
        mesh=fine,
        in_specs=placed,
        out_specs=P(TM, None, space, None, None),
        check_vma=False,
    )
```

time: 210 us -> 190 us (0.905)
  Pallas kernels: 77 us -> 28.3 us
  blocking collectives: 104 us -> 126 us
  starting transfers between devices: 8.28 us -> 21.2 us
  local copies, waits for them, and re-layouts: 6.05 us -> 2.57 us
    pallas_call x1, Pallas kernels: 73.6 us -> 24.2 us  [per_device(): pl.pallas_call(solve_kernel, out_shape=jax.ShapeDtypeStruct((half, 2 * co...]
    all_gather x0 -> x1, blocking collectives: none -> 35.8 us  [per_device(): materials = lax.all_gather(region, ('x', 'yl', 'c'), axis=0, tiled=True)]
    all_to_all x1 -> x0, blocking collectives: 25.9 us -> none  [per_device(): own = lax.all_to_all(spectrum, PAIRS, 0, 0, tiled=True)]
    all_to_all x1, blocking collectives: 22.9 us -> 34.6 us  [per_device(): back = lax.all_to_all(solved, PAIRS, 0, 0, tiled=True)]
    all_to_all x0 -> x1, starting transfers between devices: none -> 8.28 us  [per_device(): own = lax.all_to_all(spectrum, PAIRS, 0, 0, tiled=True)]
    unnamed x21 -> x12, local copies, waits for them, and re-layouts: 5.09 us -> 0.99 us
    ppermute x1, starting transfers between devices: 2.41 us -> 4.84 us  [per_device(): far = lax.ppermute(part, 'x', [(i, (i + 2) % count) for i in range(count)])]
    ppermute x1, starting transfers between devices: 3.43 us -> 5.68 us  [per_device(): left = lax.ppermute(own, 'x', [(i, i + 1) for i in range(count - 1)])]
  transfers between devices with their start and end apart: 3 -> 4, of which waited for: 1 -> 1; matrix products, arithmetic and copies ran while one was open for 0% -> 0% of each run, Pallas kernels for 0% -> 0%
where the time goes in v2:
time: 190 us
  blocking collectives  126 us (66%)
  Pallas kernels  28.3 us (15%)
  starting transfers between devices  21.2 us (11%)
  waiting for transfers between devices  11.3 us (6%)
  local copies, waits for them, and re-layouts  2.57 us (1%)
    all_gather x1, blocking collectives, per_device(): materials = lax.all_gather(region, ('x', 'yl', 'c'), axis=0, tiled=True)  35.8 us
    all_to_all x1, blocking collectives, per_device(): back = lax.all_to_all(solved, PAIRS, 0, 0, tiled=True)  34.6 us
    all_to_all x1, blocking collectives, per_device(): got = lax.all_to_all(packed.reshape(groups, rows, nz), TM, 0, 0, tiled=True)  33.5 us
    pallas_call x1, Pallas kernels, per_device(): pl.pallas_call(solve_kernel, out_shape=jax.ShapeDtypeStruct((half, 2 * co...  24.2 us
    all_to_all x1, blocking collectives, per_device(): home = lax.all_to_all(pencil, TM, 0, 0, tiled=True)  22.4 us
    ppermute x1, waiting for transfers between devices, per_device(): far = lax.ppermute(part, 'x', [(i, (i + 2) % count) for i in range(count)])  11.3 us
    all_to_all x1, starting transfers between devices, per_device(): own = lax.all_to_all(spectrum, PAIRS, 0, 0, tiled=True)  8.28 us
    ppermute x1, starting transfers between devices, per_device(): left = lax.ppermute(own, 'x', [(i, i + 1) for i in range(count - 1)])  5.68 us
  transfers between devices with their start and end apart: 4, of which 1 were waited for; matrix products, arithmetic and copies ran while one was open for 0% of the time, Pallas kernels for 0%

profile of v2, /device:TPU:20, one launch (start us, length us, event | category | flops | bytes accessed | tf_op | source)
XLA Modules:
  0.0 189.8 jit_solution(6628251624302365672)
XLA Ops:
  0.0 1.9 pack.1
  1.9 0.0 copy-start
  1.9 33.5 %all_to_all.33.got = f32[16,56,128]{2,1,0:T(8,128)S(1)} all-to-all(f32[16,56,128]{2,1,0:T(8,128)} %bitcast.18), channel_id=1, replica_groups=mesh['yh'=2,'z'=8,'x'=4,'yl'=4,'c'=2] {'yh','z'}, dimensions={0} | all-to-all | bytes 917504 | tf_op jit(solution)/shard_map/all_to_all | solution.py:354
  35.4 0.0 copy-done
  35.4 0.6 forward.1
  36.0 1.2 copy.9
  37.1 0.0 copy-start.4
  37.1 8.3 %all-to-all-start.1 = ((f32[128,1,768]{2,1,0:T(1,128)}), f32[128,1,768]{2,1,0:T(1,128)S(1)}, u32[]{:S(2)}, u32[]{:S(2)}) async-start(f32[128,1,768]{2,1,0:T(1,128)} %copy.9), calls=%async_computation.1 | async-start | bytes 786432 | tf_op jit(solution)/shard_map/all_to_all | solution.py:365
  45.4 0.0 copy-done.4
  45.4 35.8 %all_gather.3.region = s32[64,8,128]{2,1,0:T(8,128)S(1)} all-gather(s32[2,8,128]{2,1,0:T(8,128)S(1)} %copy-done.4), channel_id=1, replica_groups=mesh['yh'=2,'z'=8,'x'=4,'yl'=4,'c'=2] {'x','yl','c'}, dimensions={0}, use_global_device_ids=true | all-gather | bytes 270336 | tf_op jit(solution)/shard_map/all_gather | solution.py:334
  81.2 0.0 all-to-all-done.1
  81.3 2.4 %collective-permute-start.1 = (f32[128,768]{1,0:T(8,128)S(1)}, f32[128,768]{1,0:T(8,128)S(1)}, u32[]{:S(2)}, u32[]{:S(2)}) collective-permute-start(f32[128,768]{1,0:T(8,128)S(1)} %bitcast.10), channel_id=1, source_target_pairs={{8,0},{16,8},{24,16},{9,1},{17,9},{25,17},{10,2},{18,10},{26,18},{... | collective-permute-start | bytes 1179656 | tf_op jit(solution)/shard_map/ppermute | solution.py:371
  83.6 5.7 %collective-permute-start = (f32[128,768]{1,0:T(8,128)S(1)}, f32[128,768]{1,0:T(8,128)S(1)}, u32[]{:S(2)}, u32[]{:S(2)}) collective-permute-start(f32[128,768]{1,0:T(8,128)S(1)} %bitcast.11), channel_id=1, source_target_pairs={{0,8},{8,16},{16,24},{1,9},{9,17},{17,25},{2,10},{10,18},{18,26},{... | collective-permute-start | bytes 1179656 | tf_op jit(solution)/shard_map/ppermute | solution.py:370
  89.3 0.0 copy-start.2
  89.4 0.0 copy-start.3
  89.4 4.8 %collective-permute-start.2 = (f32[64,768]{1,0:T(8,128)S(1)}, f32[64,768]{1,0:T(8,128)S(1)}, u32[]{:S(2)}, u32[]{:S(2)}) collective-permute-start(f32[64,768]{1,0:T(8,128)S(1)} %constant_dynamic-slice_fusion), channel_id=1, source_target_pairs={{0,16},{8,24},{16,0},{24,8},{1,17},{9,25},{17,1},{25,9},{2,18},{10... | collective-permute-start | bytes 589832 | tf_op jit(solution)/shard_map/ppermute | solution.py:375
  94.2 11.3 %collective-permute-done.2.far = f32[64,768]{1,0:T(8,128)S(1)} collective-permute-done((f32[64,768]{1,0:T(8,128)S(1)}, f32[64,768]{1,0:T(8,128)S(1)}, u32[]{:S(2)}, u32[]{:S(2)}) %collective-permute-start.2) | collective-permute-done | bytes 196640 | tf_op jit(solution)/shard_map/ppermute | solution.py:375
  105.5 0.0 collective-permute-done.1.right
  105.5 0.0 collective-permute-done.left
  105.5 0.0 copy-done.2
  105.5 0.0 copy-done.3
  105.5 24.2 %solve.1 = f32[128,768]{1,0:T(8,128)S(1)} custom-call(f32[4,128]{1,0:T(4,128)S(1)} %copy-done.2, f32[3]{0:T(128)S(1)} %copy-done.3, s32[64,8,128]{2,1,0:T(8,128)S(1)} %all_gather.3.region, f32[128,768]{1,0:T(8,128)S(1)} %bitcast.13, f32[128,768]{1,0:T(8,128)S(1)} %collective-permute-done.left, f32[128,768]{1,0:T(8,128)S(1)} %collective-permute-done.1.right, ...), custom_call_target="tpu_custom_call" | custom-call | tf_op jit(solution)/shard_map/solve/pallas_call | solution.py:378
  129.7 0.4 copy.10
  130.2 34.6 %all_to_all.34 = f32[128,1,768]{2,1,0:T(1,128)S(1)} all-to-all(f32[128,1,768]{2,1,0:T(1,128)S(1)} %copy.10), channel_id=1, replica_groups=mesh['yh'=2,'z'=8,'x'=4,'yl'=4,'c'=2] {'yl','c','yh','z'}, dimensions={0} | all-to-all | bytes 786432 | tf_op jit(solution)/shard_map/all_to_all | solution.py:394
  164.8 0.0 copy-start.1
  164.8 0.9 copy-done.1
  165.7 0.8 inverse.1
  166.5 22.4 %all_to_all.35 = f32[16,48,128]{2,1,0:T(8,128)S(1)} all-to-all(f32[16,48,128]{2,1,0:T(8,128)S(1)} %inverse.1), channel_id=1, replica_groups=mesh['yh'=2,'z'=8,'x'=4,'yl'=4,'c'=2] {'yh','z'}, dimensions={0} | all-to-all | bytes 786432 | tf_op jit(solution)/shard_map/all_to_all | solution.py:405
  188.9 0.9 unpack.1
  (3 shorter events, 0.1 us)
Async XLA Ops:
  1.9 33.5 %copy-start = (f32[256,256]{1,0:T(8,128)S(1)}, f32[256,256]{1,0:T(8,128)}, u32[]{:S(2)}) copy-start(f32[256,256]{1,0:T(8,128)} %constant.19.clone.table) | copy-start | bytes 786436
  37.1 8.3 %copy-start.4 = (s32[2,8,128]{2,1,0:T(8,128)S(1)}, s32[2,8,128]{2,1,0:T(8,128)}, u32[]{:S(2)}) copy-start(s32[2,8,128]{2,1,0:T(8,128)} %region.1) | copy-start | bytes 24580
  37.1 44.1 %all-to-all-start.1 = ((f32[128,1,768]{2,1,0:T(1,128)}), f32[128,1,768]{2,1,0:T(1,128)S(1)}, u32[]{:S(2)}, u32[]{:S(2)}) async-start(f32[128,1,768]{2,1,0:T(1,128)} %copy.9), calls=%async_computation.1 | async-start | bytes 786432 | tf_op jit(solution)/shard_map/all_to_all | solution.py:365
  81.3 24.2 %collective-permute-start.1 = (f32[128,768]{1,0:T(8,128)S(1)}, f32[128,768]{1,0:T(8,128)S(1)}, u32[]{:S(2)}, u32[]{:S(2)}) collective-permute-start(f32[128,768]{1,0:T(8,128)S(1)} %bitcast.10), channel_id=1, source_target_pairs={{8,0},{16,8},{24,16},{9,1},{17,9},{25,17},{10,2},{18,10},{26,18},{... | collective-permute-start | bytes 1179656 | tf_op jit(solution)/shard_map/ppermute | solution.py:371
  83.6 21.9 %collective-permute-start = (f32[128,768]{1,0:T(8,128)S(1)}, f32[128,768]{1,0:T(8,128)S(1)}, u32[]{:S(2)}, u32[]{:S(2)}) collective-permute-start(f32[128,768]{1,0:T(8,128)S(1)} %bitcast.11), channel_id=1, source_target_pairs={{0,8},{8,16},{16,24},{1,9},{9,17},{17,25},{2,10},{10,18},{18,26},{... | collective-permute-start | bytes 1179656 | tf_op jit(solution)/shard_map/ppermute | solution.py:370
  89.3 16.2 %copy-start.2 = (f32[4,128]{1,0:T(4,128)S(1)}, f32[4,128]{1,0:T(4,128)}, u32[]{:S(2)}) copy-start(f32[4,128]{1,0:T(4,128)} %constant.20.clone.terms) | copy-start | bytes 6148
  89.4 16.2 %copy-start.3 = (f32[3]{0:T(128)S(1)}, f32[3]{0:T(128)}, u32[]{:S(2)}) copy-start(f32[3]{0:T(128)} %cond.3) | copy-start | bytes 40
  89.4 16.1 %collective-permute-start.2 = (f32[64,768]{1,0:T(8,128)S(1)}, f32[64,768]{1,0:T(8,128)S(1)}, u32[]{:S(2)}, u32[]{:S(2)}) collective-permute-start(f32[64,768]{1,0:T(8,128)S(1)} %constant_dynamic-slice_fusion), channel_id=1, source_target_pairs={{0,16},{8,24},{16,0},{24,8},{1,17},{9,25},{17,1},{25,9},{2,18},{10... | collective-permute-start | bytes 589832 | tf_op jit(solution)/shard_map/ppermute | solution.py:375
  164.8 1.0 copy-start.1

commit v3 on v2

--- a/solution.py
+++ b/solution.py
@@ -23,6 +23,8 @@
 REACH = 24
 GUARD = 1
 CHUNK = 8
+LONG = 16
+SHORT = (8,)
 
 
 def tables(window):
@@ -92,7 +94,7 @@
             out[pl.ds(base + pad, ny, stride=rows), :] = jnp.zeros_like(sigma)
 
 
-def forward_kernel(got, table, out):
+def forward_kernel(cond, got, table, region, out):
     groups, _, nz = got.shape
     window = table.shape[0]
     steps = window // groups
@@ -112,7 +114,9 @@
     )
     width = comps * nz
     out[:, :width] = spectrum[:half]
-    out[:, width:] = spectrum[half:]
+    out[:, width : 2 * width] = spectrum[half:]
+    line = region[lax.axis_index("yh"), pl.ds(lax.axis_index("z"), 1), :]
+    out[:, 2 * width :] = jnp.broadcast_to(material(line, cond), (half, nz))
 
 
 def inverse_kernel(got, table, out):
@@ -139,13 +143,13 @@
                 out[b, c, p] = got[pl.ds(p * ny * rows + c * steps + b, ny, stride=rows), :]
 
 
-def solve_kernel(terms, cond, region, own, left, right, far, out, field, first, resid, total, sigma):
+def solve_kernel(terms, weights, own, far, left, right, out, field, first, resid, total, sigma):
     ny, nz = field.shape[2:]
     x_at = lax.axis_index("x")
     pair = lax.axis_index(PAIRS)
     p_plus, p_minus = terms[0, pair], terms[1, pair]
     q_term, inv_scale = terms[2, pair], terms[3, pair]
-    carry_terms, push_terms, center = chebyshev_terms(SWEEPS - 1)
+    _, _, center = chebyshev_terms(SWEEPS - 1)
 
     row = lax.broadcasted_iota(jnp.int32, (ny, nz), 0)
     lane = lax.broadcasted_iota(jnp.int32, (ny, nz), 1)
@@ -220,18 +224,14 @@
     top = jnp.minimum(grid_high, width)
 
     def fill(source, begin, count):
-        def some(t, _):
-            for u in range(CHUNK):
-                i = t * CHUNK + u
-                line = pl.ds(pl.multiple_of(i * ny, ny), ny)
-                store(first, begin + i, [source[line, k * nz : (k + 1) * nz] for k in range(6)])
-            return 0
-
-        lax.fori_loop(0, count // CHUNK, some, 0)
+        for i in range(count):
+            line = slice(i * ny, (i + 1) * ny)
+            store(first, begin + i, [source[line, k * nz : (k + 1) * nz] for k in range(6)])
+            sigma[begin + i + GUARD] = source[line, 6 * nz :]
 
     extra = far.shape[0] // ny
-    low_far, high_far = 0, REACH + 2 * BLOCK
-    for at in [*range(-1, extra), *range(high_far, high_far + extra + 1)]:
+    low_far, high_far = REACH - BLOCK - extra, REACH + 2 * BLOCK
+    for at in [*range(-1, low_far + extra), *range(high_far, width + 1)]:
         store(first, at, [blank] * 6)
     fill(left, REACH - BLOCK, BLOCK)
     fill(own, REACH, BLOCK)
@@ -241,39 +241,39 @@
     store(field, -1, [blank] * 6)
 
     def bounds(margin):
-        margin = -(-margin // CHUNK) * CHUNK
         low = jnp.maximum(grid_low, REACH - margin)
         high = jnp.minimum(grid_high, REACH + BLOCK + margin)
-        return low, high
+        length = (high - low + CHUNK - 1) // CHUNK * CHUNK
+        high = jnp.minimum(top, low + length)
+        return high - length, length
 
     def run(margin, source, sign, finish):
-        low, high = bounds(margin)
-
-        def some(t, _):
-            begin = low + t * CHUNK
+        low, length = bounds(margin)
+
+        def some(begin, planes):
             now = load(source, begin)
             before = tails(load(source, begin - 1), now)
             before = [jnp.where(begin > grid_low, v, 0.0) for v in before]
-            for u in range(CHUNK):
+            for u in range(planes):
                 i = begin + u
                 after = load(source, i + 1)
                 flux = curls(now, after)
                 value = adjoints(flux, before)
                 finish(i, add_couple(value, now, sigma[i + GUARD], sign))
                 now, before = after, [flux[1], flux[2], flux[4], flux[5]]
+
+        many = length // LONG
+
+        def step(t, _):
+            some(low + t * LONG, LONG)
             return 0
 
-        lax.fori_loop(0, (high - low) // CHUNK, some, 0)
-
-    low, high = bounds(REACH)
-
-    def fill_sigma(t, _):
-        for u in range(CHUNK):
-            i = low + t * CHUNK + u
-            sigma[i + GUARD] = material(region[i - grid_low], cond)
-        return 0
-
-    lax.fori_loop(0, (high - low) // CHUNK, fill_sigma, 0)
+        lax.fori_loop(0, many, step, 0)
+        for planes in SHORT:
+
+            @pl.when((length - many * LONG) == planes)
+            def _():
+                some(low + many * LONG, planes)
 
     def begin_with(i, value):
         store(resid, i, value)
@@ -281,16 +281,23 @@
 
     run(2 * (SWEEPS - 1), first, -1.0, begin_with)
 
-    for s in range(SWEEPS - 1):
+    def clear(t, _):
+        for u in range(CHUNK):
+            for k in range(6):
+                total[t * CHUNK + u, k] = blank
+        return 0
+
+    lax.fori_loop(0, BLOCK // CHUNK, clear, 0)
+
+    def sweep(s, _):
         margin = 2 * (SWEEPS - 2 - s)
-        carry_term, push_term = carry_terms[s], push_terms[s] * inv_scale
+        carry_term, push_term = weights[0, s], weights[1, s] * inv_scale
 
         def add_total(t, _):
             for u in range(CHUNK):
                 i = t * CHUNK + u
                 for k in range(6):
-                    step = field[i + REACH + GUARD, k]
-                    total[i, k] = step if s == 0 else total[i, k] + step
+                    total[i, k] = total[i, k] + field[i + REACH + GUARD, k]
             return 0
 
         lax.fori_loop(0, BLOCK // CHUNK, add_total, 0)
@@ -309,6 +316,9 @@
 
         run(margin + 1, field, 1.0, keep_first)
         run(margin, first, -1.0, update)
+        return 0
+
+    lax.fori_loop(0, SWEEPS - 1, sweep, 0)
 
     def write(t, _):
         for u in range(CHUNK):
@@ -331,7 +341,6 @@
     smem = pl.BlockSpec(memory_space=pltpu.SMEM)
     f32 = jnp.float32
     params = pltpu.CompilerParams(vmem_limit_bytes=12 * 1024 * 1024)
-    materials = lax.all_gather(region, ("x", "yl", "c"), axis=0, tiled=True)
 
     rows = comps * steps + 8
     whole = lambda shape: pl.BlockSpec(shape, lambda i: (0,) * len(shape))
@@ -355,30 +364,31 @@
 
     spectrum = pl.pallas_call(
         forward_kernel,
-        out_shape=jax.ShapeDtypeStruct((half, 2 * comps * nz), f32),
-        in_specs=[vmem, vmem],
+        out_shape=jax.ShapeDtypeStruct((half, (2 * comps + 1) * nz), f32),
+        in_specs=[smem, vmem, vmem, vmem],
         out_specs=vmem,
         compiler_params=params,
         name="forward",
-    )(got, jnp.asarray(forward_table))
+    )(conductance, got, jnp.asarray(forward_table), region)
 
     own = lax.all_to_all(spectrum, PAIRS, 0, 0, tiled=True)
-    own, materials = lax.optimization_barrier((own, materials))
 
     count = lax.axis_size("x")
     x_at = lax.axis_index("x")
+    extra = (2 * SWEEPS - 1 - BLOCK) * ny
+    part = lax.dynamic_slice_in_dim(
+        own, jnp.where(x_at < count // 2, half - extra, 0), extra, 0
+    )
+    own, part = lax.optimization_barrier((own, part))
+    far = lax.ppermute(part, "x", [(i, (i + 2) % count) for i in range(count)])
     left = lax.ppermute(own, "x", [(i, i + 1) for i in range(count - 1)])
     right = lax.ppermute(own, "x", [(i + 1, i) for i in range(count - 1)])
-    part = lax.dynamic_slice_in_dim(
-        own, jnp.where(x_at < count // 2, half // 2, 0), half // 2, 0
-    )
-    far = lax.ppermute(part, "x", [(i, (i + 2) % count) for i in range(count)])
 
     places = 2 * REACH + BLOCK + 2 * GUARD
     solved = pl.pallas_call(
         solve_kernel,
         out_shape=jax.ShapeDtypeStruct((half, 2 * comps * nz), f32),
-        in_specs=[smem, smem, vmem, vmem, vmem, vmem, vmem],
+        in_specs=[smem, smem, vmem, vmem, vmem, vmem],
         out_specs=vmem,
         scratch_shapes=[
             pltpu.VMEM((places, 6, ny, nz), f32),
@@ -389,7 +399,14 @@
         ],
         compiler_params=params,
         name="solve",
-    )(jnp.asarray(pair_table(window)), conductance, materials, own, left, right, far)
+    )(
+        jnp.asarray(pair_table(window)),
+        jnp.asarray(np.array(chebyshev_terms(SWEEPS - 1)[:2], np.float32)),
+        own,
+        far,
+        left,
+        right,
+    )
 
     back = lax.all_to_all(solved, PAIRS, 0, 0, tiled=True)
 

time: 190 us -> 153 us (0.81)
  blocking collectives: 126 us -> 78.8 us
  waiting for transfers between devices: 11.3 us -> 30.9 us
  starting transfers between devices: 21.2 us -> 16.4 us
  Pallas kernels: 28.3 us -> 24 us
    all_gather x1 -> x0, blocking collectives: 35.8 us -> none  [per_device(): materials = lax.all_gather(region, ('x', 'yl', 'c'), axis=0, tiled=True)]
    all_to_all x1, waiting for transfers between devices: 0.01 us -> 17.9 us  [per_device(): own = lax.all_to_all(spectrum, PAIRS, 0, 0, tiled=True)]
    all_to_all x1, blocking collectives: 34.6 us -> 22.9 us  [per_device(): back = lax.all_to_all(solved, PAIRS, 0, 0, tiled=True)]
    pallas_call x1, Pallas kernels: 24.2 us -> 19.3 us  [per_device(): pl.pallas_call(solve_kernel, out_shape=jax.ShapeDtypeStruct((half, 2 * co...]
    ppermute x1, starting transfers between devices: 4.84 us -> 2.42 us  [per_device(): far = lax.ppermute(part, 'x', [(i, (i + 2) % count) for i in range(count)])]
    ppermute x1, starting transfers between devices: 5.68 us -> 3.42 us  [per_device(): left = lax.ppermute(own, 'x', [(i, i + 1) for i in range(count - 1)])]
  transfers between devices with their start and end apart: 4 -> 4, of which waited for: 1 -> 2; matrix products, arithmetic and copies ran while one was open for 0% -> 0% of each run, Pallas kernels for 0% -> 0%
where the time goes in v3:
time: 153 us
  blocking collectives  78.8 us (52%)
  waiting for transfers between devices  30.9 us (20%)
  Pallas kernels  24 us (16%)
  starting transfers between devices  16.4 us (11%)
  local copies, waits for them, and re-layouts  2.72 us (2%)
    all_to_all x1, blocking collectives, per_device(): got = lax.all_to_all(packed.reshape(groups, rows, nz), TM, 0, 0, tiled=True)  33.5 us
    all_to_all x1, blocking collectives, per_device(): back = lax.all_to_all(solved, PAIRS, 0, 0, tiled=True)  22.9 us
    all_to_all x1, blocking collectives, per_device(): home = lax.all_to_all(pencil, TM, 0, 0, tiled=True)  22.4 us
    pallas_call x1, Pallas kernels, per_device(): pl.pallas_call(solve_kernel, out_shape=jax.ShapeDtypeStruct((half, 2 * co...  19.3 us
    all_to_all x1, waiting for transfers between devices, per_device(): own = lax.all_to_all(spectrum, PAIRS, 0, 0, tiled=True)  17.9 us
    ppermute x1, waiting for transfers between devices, per_device(): far = lax.ppermute(part, 'x', [(i, (i + 2) % count) for i in range(count)])  12.9 us
    all_to_all x1, starting transfers between devices, per_device(): own = lax.all_to_all(spectrum, PAIRS, 0, 0, tiled=True)  8.15 us
    ppermute x1, starting transfers between devices, per_device(): left = lax.ppermute(own, 'x', [(i, i + 1) for i in range(count - 1)])  3.42 us
  transfers between devices with their start and end apart: 4, of which 2 were waited for; matrix products, arithmetic and copies ran while one was open for 0% of the time, Pallas kernels for 0%

profile of v3, /device:TPU:20, one launch (start us, length us, event | category | flops | bytes accessed | tf_op | source)
XLA Modules:
  0.0 152.9 jit_solution(18137830598610747882)
XLA Ops:
  0.0 1.9 %pack.1 = f32[896,128]{1,0:T(8,128)} custom-call(f32[3]{0:T(128)} %cond.3, f32[16,3,2,8,128]{4,3,2,1,0:T(8,128)} %forcing.1, f32[3,2,8,128]{3,2,1,0:T(8,128)} %start.1, f32[16,3,2,8,128]{4,3,2,1,0:T(8,128)} %latest.1, s32[2,8,128]{2,1,0:T(8,128)} %region.3), custom_call_target="tpu_custom_call" | custom-call | tf_op jit(solution)/shard_map/pack/pallas_call | solution.py:347
  1.9 0.0 copy-start.1
  1.9 0.0 copy-start.2
  1.9 0.0 copy-start.3
  1.9 33.5 %all_to_all.33.got = f32[16,56,128]{2,1,0:T(8,128)S(1)} all-to-all(f32[16,56,128]{2,1,0:T(8,128)} %bitcast.20), channel_id=1, replica_groups=mesh['yh'=2,'z'=8,'x'=4,'yl'=4,'c'=2] {'yh','z'}, dimensions={0} | all-to-all | bytes 917504 | tf_op jit(solution)/shard_map/all_to_all | solution.py:363
  35.4 0.0 copy-done.1
  35.4 0.0 copy-done.2
  35.4 0.0 copy-done.3
  35.4 1.1 forward.1
  36.6 1.2 copy.10
  37.8 8.1 %all-to-all-start.1 = ((f32[128,1,896]{2,1,0:T(1,128)}), f32[128,1,896]{2,1,0:T(1,128)S(1)}, u32[]{:S(2)}, u32[]{:S(2)}) async-start(f32[128,1,896]{2,1,0:T(1,128)} %copy.10), calls=%async_computation.1 | async-start | bytes 917504 | tf_op jit(solution)/shard_map/all_to_all | solution.py:374
  46.0 17.9 %all-to-all-done.1 = f32[128,1,896]{2,1,0:T(1,128)S(1)} async-done(((f32[128,1,896]{2,1,0:T(1,128)}), f32[128,1,896]{2,1,0:T(1,128)S(1)}, u32[]{:S(2)}, u32[]{:S(2)}) %all-to-all-start.1) | async-done | bytes 458784 | tf_op jit(solution)/shard_map/all_to_all | solution.py:374
  63.9 0.1 constant_dynamic-slice_fusion
  64.0 0.0 copy-start.4
  64.0 0.0 copy-start.5
  64.0 2.4 %collective-permute-start.2 = (f32[128,896]{1,0:T(8,128)S(1)}, f32[128,896]{1,0:T(8,128)S(1)}, u32[]{:S(2)}, u32[]{:S(2)}) collective-permute-start(f32[128,896]{1,0:T(8,128)S(1)} %bitcast.13), channel_id=1, source_target_pairs={{8,0},{16,8},{24,16},{9,1},{17,9},{25,17},{10,2},{18,10},{26,18},{... | collective-permute-start | bytes 1376264 | tf_op jit(solution)/shard_map/ppermute | solution.py:385
  66.5 3.4 %collective-permute-start.1 = (f32[128,896]{1,0:T(8,128)S(1)}, f32[128,896]{1,0:T(8,128)S(1)}, u32[]{:S(2)}, u32[]{:S(2)}) collective-permute-start(f32[128,896]{1,0:T(8,128)S(1)} %bitcast.14), channel_id=1, source_target_pairs={{0,8},{8,16},{16,24},{1,9},{9,17},{17,25},{2,10},{10,18},{18,26},{... | collective-permute-start | bytes 1376264 | tf_op jit(solution)/shard_map/ppermute | solution.py:384
  69.9 2.4 %collective-permute-start = (f32[56,896]{1,0:T(8,128)S(1)}, f32[56,896]{1,0:T(8,128)S(1)}, u32[]{:S(2)}, u32[]{:S(2)}) collective-permute-start(f32[56,896]{1,0:T(8,128)S(1)} %bitcast.21), channel_id=1, source_target_pairs={{0,16},{8,24},{16,0},{24,8},{1,17},{9,25},{17,1},{25,9},{2,18},{10... | collective-permute-start | bytes 602120 | tf_op jit(solution)/shard_map/ppermute | solution.py:383
  72.3 12.9 %collective-permute-done.far = f32[56,896]{1,0:T(8,128)S(1)} collective-permute-done((f32[56,896]{1,0:T(8,128)S(1)}, f32[56,896]{1,0:T(8,128)S(1)}, u32[]{:S(2)}, u32[]{:S(2)}) %collective-permute-start) | collective-permute-done | bytes 200736 | tf_op jit(solution)/shard_map/ppermute | solution.py:383
  85.3 0.0 collective-permute-done.2.right
  85.3 0.0 collective-permute-done.1.left
  85.3 0.0 copy-done.4
  85.3 0.0 copy-done.5
  85.3 19.3 %solve.1 = f32[128,768]{1,0:T(8,128)S(1)} custom-call(f32[4,128]{1,0:T(4,128)S(1)} %copy-done.4, f32[2,11]{1,0:T(2,128)S(1)} %copy-done.5, f32[128,896]{1,0:T(8,128)S(1)} %bitcast.15, f32[56,896]{1,0:T(8,128)S(1)} %collective-permute-done.far, f32[128,896]{1,0:T(8,128)S(1)} %collective-permute-done.1.left, f32[128,896]{1,0:T(8,128)S(1)} %collective-permute-done.2.right), custom_call_target="tpu_custom_call" | custom-call | tf_op jit(solution)/shard_map/solve/pallas_call | solution.py:388
  104.6 0.4 copy.11
  105.0 22.9 %all_to_all.34 = f32[128,1,768]{2,1,0:T(1,128)S(1)} all-to-all(f32[128,1,768]{2,1,0:T(1,128)S(1)} %copy.11), channel_id=1, replica_groups=mesh['yh'=2,'z'=8,'x'=4,'yl'=4,'c'=2] {'yl','c','yh','z'}, dimensions={0} | all-to-all | bytes 786432 | tf_op jit(solution)/shard_map/all_to_all | solution.py:411
  127.9 0.0 copy-start
  127.9 0.9 copy-done
  128.9 0.8 inverse.1
  129.6 22.4 %all_to_all.35 = f32[16,48,128]{2,1,0:T(8,128)S(1)} all-to-all(f32[16,48,128]{2,1,0:T(8,128)S(1)} %inverse.1), channel_id=1, replica_groups=mesh['yh'=2,'z'=8,'x'=4,'yl'=4,'c'=2] {'yh','z'}, dimensions={0} | all-to-all | bytes 786432 | tf_op jit(solution)/shard_map/all_to_all | solution.py:422
  152.0 0.9 unpack.1
  (3 shorter events, 0.1 us)
Async XLA Ops:
  1.9 33.5 %copy-start.1 = (f32[256,256]{1,0:T(8,128)S(1)}, f32[256,256]{1,0:T(8,128)}, u32[]{:S(2)}) copy-start(f32[256,256]{1,0:T(8,128)} %constant.22.clone.table) | copy-start | bytes 786436
  1.9 33.5 %copy-start.2 = (s32[2,8,128]{2,1,0:T(8,128)S(1)}, s32[2,8,128]{2,1,0:T(8,128)}, u32[]{:S(2)}) copy-start(s32[2,8,128]{2,1,0:T(8,128)} %region.3) | copy-start | bytes 24580
  1.9 33.5 %copy-start.3 = (f32[3]{0:T(128)S(1)}, f32[3]{0:T(128)}, u32[]{:S(2)}) copy-start(f32[3]{0:T(128)} %cond.3) | copy-start | bytes 40
  37.8 26.1 %all-to-all-start.1 = ((f32[128,1,896]{2,1,0:T(1,128)}), f32[128,1,896]{2,1,0:T(1,128)S(1)}, u32[]{:S(2)}, u32[]{:S(2)}) async-start(f32[128,1,896]{2,1,0:T(1,128)} %copy.10), calls=%async_computation.1 | async-start | bytes 917504 | tf_op jit(solution)/shard_map/all_to_all | solution.py:374
  64.0 21.3 %copy-start.4 = (f32[4,128]{1,0:T(4,128)S(1)}, f32[4,128]{1,0:T(4,128)}, u32[]{:S(2)}) copy-start(f32[4,128]{1,0:T(4,128)} %constant.23.clone.terms) | copy-start | bytes 6148
  64.0 21.3 %copy-start.5 = (f32[2,11]{1,0:T(2,128)S(1)}, f32[2,11]{1,0:T(2,128)}, u32[]{:S(2)}) copy-start(f32[2,11]{1,0:T(2,128)} %constant.24.clone.weights) | copy-start | bytes 268
  64.0 21.2 %collective-permute-start.2 = (f32[128,896]{1,0:T(8,128)S(1)}, f32[128,896]{1,0:T(8,128)S(1)}, u32[]{:S(2)}, u32[]{:S(2)}) collective-permute-start(f32[128,896]{1,0:T(8,128)S(1)} %bitcast.13), channel_id=1, source_target_pairs={{8,0},{16,8},{24,16},{9,1},{17,9},{25,17},{10,2},{18,10},{26,18},{... | collective-permute-start | bytes 1376264 | tf_op jit(solution)/shard_map/ppermute | solution.py:385
  66.5 18.8 %collective-permute-start.1 = (f32[128,896]{1,0:T(8,128)S(1)}, f32[128,896]{1,0:T(8,128)S(1)}, u32[]{:S(2)}, u32[]{:S(2)}) collective-permute-start(f32[128,896]{1,0:T(8,128)S(1)} %bitcast.14), channel_id=1, source_target_pairs={{0,8},{8,16},{16,24},{1,9},{9,17},{17,25},{2,10},{10,18},{18,26},{... | collective-permute-start | bytes 1376264 | tf_op jit(solution)/shard_map/ppermute | solution.py:384
  69.9 15.4 %collective-permute-start = (f32[56,896]{1,0:T(8,128)S(1)}, f32[56,896]{1,0:T(8,128)S(1)}, u32[]{:S(2)}, u32[]{:S(2)}) collective-permute-start(f32[56,896]{1,0:T(8,128)S(1)} %bitcast.21), channel_id=1, source_target_pairs={{0,16},{8,24},{16,0},{24,8},{1,17},{9,25},{17,1},{25,9},{2,18},{10... | collective-permute-start | bytes 602120 | tf_op jit(solution)/shard_map/ppermute | solution.py:383
  127.9 1.0 copy-start

commit v4 on v3

--- a/solution.py
+++ b/solution.py
@@ -18,13 +18,28 @@
 CURL_TOP = 12.0
 
 TM = ("yh", "z")
-PAIRS = ("yl", "c", "yh", "z")
-BLOCK = 16
+GROUP = ("xl", "yl", "yh", "z")
+HALF = 32
 REACH = 24
+STRIPE = 2
 GUARD = 1
-CHUNK = 8
-LONG = 16
-SHORT = (8,)
+CHUNK = 14
+
+
+def pair_rows(count):
+    flip = lax.axis_index("xh")
+    size = count // 2
+    return tuple(
+        pl.ds(pl.multiple_of(at * size, size), size) for at in (flip, 1 - flip)
+    )
+
+
+def pair_index():
+    half_at, low_at, *rest = (lax.axis_index(name) for name in ("xh",) + GROUP)
+    index = (half_at + low_at) % 2
+    for name, at in zip(GROUP[1:], rest):
+        index = index * lax.axis_size(name) + at
+    return index
 
 
 def tables(window):
@@ -113,8 +128,10 @@
         preferred_element_type=jnp.float32,
     )
     width = comps * nz
-    out[:, :width] = spectrum[:half]
-    out[:, width : 2 * width] = spectrum[half:]
+    for at, rows in enumerate(pair_rows(half)):
+        lines = slice(at * (half // 2), (at + 1) * (half // 2))
+        out[rows, :width] = spectrum[:half][lines]
+        out[rows, width : 2 * width] = spectrum[half:][lines]
     line = region[lax.axis_index("yh"), pl.ds(lax.axis_index("z"), 1), :]
     out[:, 2 * width :] = jnp.broadcast_to(material(line, cond), (half, nz))
 
@@ -127,7 +144,8 @@
     dot = functools.partial(
         jnp.dot, precision=lax.Precision.HIGHEST, preferred_element_type=jnp.float32
     )
-    result = dot(table[:, :half], got[:, :width]) + dot(table[:, half:], got[:, width:])
+    solved = jnp.concatenate([got[rows, :] for rows in pair_rows(half)], axis=0)
+    result = dot(table[:, :half], solved[:, :width]) + dot(table[:, half:], solved[:, width:])
     for c in range(rows // steps):
         out[:, c * steps : (c + 1) * steps, :] = result[:, c * nz : (c + 1) * nz].reshape(
             groups, steps, nz
@@ -143,10 +161,11 @@
                 out[b, c, p] = got[pl.ds(p * ny * rows + c * steps + b, ny, stride=rows), :]
 
 
-def solve_kernel(terms, weights, own, far, left, right, out, field, first, resid, total, sigma):
+def solve_kernel(terms, weights, mine, mate, part, part_mate, out, field, first, resid, total, sigma, flux_a, flux_b):
     ny, nz = field.shape[2:]
-    x_at = lax.axis_index("x")
-    pair = lax.axis_index(PAIRS)
+    half_at = lax.axis_index("xh")
+    core_at = lax.axis_index("c")
+    pair = pair_index()
     p_plus, p_minus = terms[0, pair], terms[1, pair]
     q_term, inv_scale = terms[2, pair], terms[3, pair]
     _, _, center = chebyshev_terms(SWEEPS - 1)
@@ -217,90 +236,87 @@
         for k in range(6):
             ref[at + GUARD, k] = values[k]
 
-    blocks = lax.axis_size("x")
-    width = 2 * REACH + BLOCK
-    grid_low = REACH - BLOCK * x_at
-    grid_high = grid_low + BLOCK * blocks
-    top = jnp.minimum(grid_high, width)
-
-    def fill(source, begin, count):
-        for i in range(count):
-            line = slice(i * ny, (i + 1) * ny)
-            store(first, begin + i, [source[line, k * nz : (k + 1) * nz] for k in range(6)])
-            sigma[begin + i + GUARD] = source[line, 6 * nz :]
-
-    extra = far.shape[0] // ny
-    low_far, high_far = REACH - BLOCK - extra, REACH + 2 * BLOCK
-    for at in [*range(-1, low_far + extra), *range(high_far, width + 1)]:
-        store(first, at, [blank] * 6)
-    fill(left, REACH - BLOCK, BLOCK)
-    fill(own, REACH, BLOCK)
-    fill(right, REACH + BLOCK, BLOCK)
-    fill(far, jnp.where(x_at < blocks // 2, high_far, low_far), extra)
-    store(field, top, [blank] * 6)
-    store(field, -1, [blank] * 6)
+    own_low = REACH * half_at
+    halo_low = HALF * (1 - half_at)
+    grid_low = -(HALF - REACH) * half_at
+    grid_high = grid_low + 2 * HALF
+    width = HALF + REACH
+
+    def fill(source, begin):
+        for at in range(source.shape[0] // ny):
+            i = begin + (at // STRIPE) * (2 * STRIPE) + at % STRIPE
+            line = slice(at * ny, (at + 1) * ny)
+            store(first, i, [source[line, k * nz : (k + 1) * nz] for k in range(6)])
+            sigma[i + GUARD] = source[line, 6 * nz :]
+
+    for ref in (first, field):
+        store(ref, -1, [blank] * 6)
+        store(ref, width, [blank] * 6)
+    mine_at, mate_at = STRIPE * core_at, STRIPE * (1 - core_at)
+    fill(mine, own_low + mine_at)
+    fill(mate, own_low + mate_at)
+    fill(part, halo_low + mine_at)
+    fill(part_mate, halo_low + mate_at)
 
     def bounds(margin):
-        low = jnp.maximum(grid_low, REACH - margin)
-        high = jnp.minimum(grid_high, REACH + BLOCK + margin)
+        low = jnp.maximum(grid_low, own_low - margin)
+        high = jnp.minimum(grid_high, own_low + HALF + margin)
         length = (high - low + CHUNK - 1) // CHUNK * CHUNK
-        high = jnp.minimum(top, low + length)
-        return high - length, length
-
-    def run(margin, source, sign, finish):
-        low, length = bounds(margin)
-
-        def some(begin, planes):
-            now = load(source, begin)
-            before = tails(load(source, begin - 1), now)
-            before = [jnp.where(begin > grid_low, v, 0.0) for v in before]
-            for u in range(planes):
-                i = begin + u
-                after = load(source, i + 1)
-                flux = curls(now, after)
-                value = adjoints(flux, before)
-                finish(i, add_couple(value, now, sigma[i + GUARD], sign))
-                now, before = after, [flux[1], flux[2], flux[4], flux[5]]
-
-        many = length // LONG
+        high = jnp.minimum(width, low + length)
+        return high - length, length // CHUNK
+
+    def lift(flux, source, begin):
+        now = load(source, begin)
+        before = tails(load(source, begin - 1), now)
+        for k, v in zip((1, 2, 4, 5), before):
+            flux[0, k] = jnp.where(begin > grid_low, v, 0.0)
+        for u in range(CHUNK):
+            after = load(source, begin + u + 1)
+            for k, v in enumerate(curls(now, after)):
+                flux[u + 1, k] = v
+            now = after
+
+    def drop(flux, source, begin, sign, finish):
+        before = [flux[0, k] for k in (1, 2, 4, 5)]
+        for u in range(CHUNK):
+            i = begin + u
+            now = [flux[u + 1, k] for k in range(6)]
+            value = adjoints(now, before)
+            finish(i, add_couple(value, load(source, i), sigma[i + GUARD], sign))
+            before = [now[k] for k in (1, 2, 4, 5)]
+
+    def run(margin, flux, source, sign, finish, other_margin, other_flux, other_source):
+        low, count = bounds(margin)
 
         def step(t, _):
-            some(low + t * LONG, LONG)
+            begin = low + t * CHUNK
+            drop(flux, source, begin, sign, finish)
+            lift(flux, source, begin + CHUNK)
             return 0
 
-        lax.fori_loop(0, many, step, 0)
-        for planes in SHORT:
-
-            @pl.when((length - many * LONG) == planes)
-            def _():
-                some(low + many * LONG, planes)
+        lax.fori_loop(0, count - 1, step, 0)
+        lift(other_flux, other_source, bounds(other_margin)[0])
+        drop(flux, source, low + (count - 1) * CHUNK, sign, finish)
 
     def begin_with(i, value):
         store(resid, i, value)
         store(field, i, [v * (inv_scale * (1.0 / center)) for v in value])
 
-    run(2 * (SWEEPS - 1), first, -1.0, begin_with)
-
-    def clear(t, _):
-        for u in range(CHUNK):
+    reach = 2 * (SWEEPS - 1)
+    lift(flux_b, first, bounds(reach)[0])
+    run(reach, flux_b, first, -1.0, begin_with, reach - 1, flux_a, field)
+
+    own_planes = [(at // STRIPE) * (2 * STRIPE) + at % STRIPE for at in range(HALF // 2)]
+    own_begin = own_low + mine_at
+
+    def sweep(s, _):
+        margin = reach - 2 - 2 * s
+        carry_term, push_term = weights[0, s], weights[1, s] * inv_scale
+
+        for at, h in enumerate(own_planes):
             for k in range(6):
-                total[t * CHUNK + u, k] = blank
-        return 0
-
-    lax.fori_loop(0, BLOCK // CHUNK, clear, 0)
-
-    def sweep(s, _):
-        margin = 2 * (SWEEPS - 2 - s)
-        carry_term, push_term = weights[0, s], weights[1, s] * inv_scale
-
-        def add_total(t, _):
-            for u in range(CHUNK):
-                i = t * CHUNK + u
-                for k in range(6):
-                    total[i, k] = total[i, k] + field[i + REACH + GUARD, k]
-            return 0
-
-        lax.fori_loop(0, BLOCK // CHUNK, add_total, 0)
+                step = field[own_begin + h + GUARD, k]
+                total[at, k] = jnp.where(s == 0, step, total[at, k] + step)
 
         def keep_first(i, value):
             store(first, i, value)
@@ -314,21 +330,17 @@
                 [carry_term * d + push_term * r for d, r in zip(load(field, i), rest)],
             )
 
-        run(margin + 1, field, 1.0, keep_first)
-        run(margin, first, -1.0, update)
+        run(margin + 1, flux_a, field, 1.0, keep_first, margin, flux_b, first)
+        run(margin, flux_b, first, -1.0, update, jnp.maximum(margin - 1, 0), flux_a, field)
         return 0
 
     lax.fori_loop(0, SWEEPS - 1, sweep, 0)
 
-    def write(t, _):
-        for u in range(CHUNK):
-            i = t * CHUNK + u
-            line = pl.ds(pl.multiple_of(i * ny, ny), ny)
-            for k in range(6):
-                out[line, k * nz : (k + 1) * nz] = total[i, k] + field[i + REACH + GUARD, k]
-        return 0
-
-    lax.fori_loop(0, BLOCK // CHUNK, write, 0)
+    for at, h in enumerate(own_planes):
+        for k in range(6):
+            out[at * ny : (at + 1) * ny, k * nz : (k + 1) * nz] = (
+                total[at, k] + field[own_begin + h + GUARD, k]
+            )
 
 
 def per_device(forcing, start_field, iterate, region, conductance):
@@ -371,44 +383,46 @@
         name="forward",
     )(conductance, got, jnp.asarray(forward_table), region)
 
-    own = lax.all_to_all(spectrum, PAIRS, 0, 0, tiled=True)
-
-    count = lax.axis_size("x")
-    x_at = lax.axis_index("x")
-    extra = (2 * SWEEPS - 1 - BLOCK) * ny
+    mine = lax.all_to_all(spectrum, GROUP, 0, 0, tiled=True)
+
+    rows_sent = half * REACH // HALF
     part = lax.dynamic_slice_in_dim(
-        own, jnp.where(x_at < count // 2, half - extra, 0), extra, 0
-    )
-    own, part = lax.optimization_barrier((own, part))
-    far = lax.ppermute(part, "x", [(i, (i + 2) % count) for i in range(count)])
-    left = lax.ppermute(own, "x", [(i, i + 1) for i in range(count - 1)])
-    right = lax.ppermute(own, "x", [(i + 1, i) for i in range(count - 1)])
-
-    places = 2 * REACH + BLOCK + 2 * GUARD
+        mine, (1 - lax.axis_index("xh")) * (half - rows_sent), rows_sent, 0
+    )
+    blocks = lax.axis_size(("xh", "xl"))
+    part = lax.ppermute(part, ("xh", "xl"), [(i, blocks - 1 - i) for i in range(blocks)])
+    mate = lax.ppermute(mine, "c", [(0, 1), (1, 0)])
+    part_mate = lax.ppermute(part, "c", [(0, 1), (1, 0)])
+
+    places = HALF + REACH + 2 * GUARD
+    window_shape = pltpu.VMEM((places, 2 * comps, ny, nz), f32)
+    flux_shape = pltpu.VMEM((CHUNK + 1, 2 * comps, ny, nz), f32)
     solved = pl.pallas_call(
         solve_kernel,
         out_shape=jax.ShapeDtypeStruct((half, 2 * comps * nz), f32),
         in_specs=[smem, smem, vmem, vmem, vmem, vmem],
         out_specs=vmem,
         scratch_shapes=[
-            pltpu.VMEM((places, 6, ny, nz), f32),
-            pltpu.VMEM((places, 6, ny, nz), f32),
-            pltpu.VMEM((places, 6, ny, nz), f32),
-            pltpu.VMEM((BLOCK, 6, ny, nz), f32),
+            window_shape,
+            window_shape,
+            window_shape,
+            pltpu.VMEM((HALF // 2, 2 * comps, ny, nz), f32),
             pltpu.VMEM((places, ny, nz), f32),
+            flux_shape,
+            flux_shape,
         ],
         compiler_params=params,
         name="solve",
     )(
         jnp.asarray(pair_table(window)),
         jnp.asarray(np.array(chebyshev_terms(SWEEPS - 1)[:2], np.float32)),
-        own,
-        far,
-        left,
-        right,
-    )
-
-    back = lax.all_to_all(solved, PAIRS, 0, 0, tiled=True)
+        mine,
+        mate,
+        part,
+        part_mate,
+    )
+
+    back = lax.all_to_all(solved, GROUP, 0, 0, tiled=True)
 
     pencil = pl.pallas_call(
         inverse_kernel,
@@ -432,8 +446,9 @@
 
 
 def solution(mesh):
-    fine = Mesh(mesh.devices.reshape(2, 8, 4, 4, 2), ("yh", "z", "x", "yl", "c"))
-    space = ("x", "yl", "c")
+    names = ("yh", "z", "xh", "xl", "yl", "c")
+    fine = Mesh(mesh.devices.reshape(2, 8, 2, 2, 4, 2), names)
+    space = ("xh", "xl", "yl", "c")
     placed = (
         P(TM, None, space, None, None),
         P(None, space, None, None),

time: 153 us -> 149 us (0.974)
  the two profiles are of different devices: /device:TPU:20 before, /device:TPU:8 now
where the time goes in v4:
time: 149 us; the launch traced here: 148 us
  blocking collectives  80.6 us (54%)
  waiting for transfers between devices  24.3 us (16%)
  Pallas kernels  23.6 us (16%)
  starting transfers between devices  16.8 us (11%)
  local copies, waits for them, and re-layouts  2.77 us (2%)
    all_to_all x1, blocking collectives, per_device(): got = lax.all_to_all(packed.reshape(groups, rows, nz), TM, 0, 0, tiled=True)  34.2 us
    all_to_all x1, blocking collectives, per_device(): back = lax.all_to_all(solved, GROUP, 0, 0, tiled=True)  25 us
    all_to_all x1, blocking collectives, per_device(): home = lax.all_to_all(pencil, TM, 0, 0, tiled=True)  21.4 us
    pallas_call x1, Pallas kernels, per_device(): pl.pallas_call(solve_kernel, out_shape=jax.ShapeDtypeStruct((half, 2 * co...  19 us
    all_to_all x1, waiting for transfers between devices, per_device(): mine = lax.all_to_all(spectrum, GROUP, 0, 0, tiled=True)  18.2 us
    all_to_all x1, starting transfers between devices, per_device(): mine = lax.all_to_all(spectrum, GROUP, 0, 0, tiled=True)  8.18 us
    ppermute x1, starting transfers between devices, per_device(): lax.ppermute(part, ('xh', 'xl'), [(i, blocks - 1 - i) for i in range(bloc...  4.82 us
    ppermute x1, waiting for transfers between devices, per_device(): lax.ppermute(part, ('xh', 'xl'), [(i, blocks - 1 - i) for i in range(bloc...  4.56 us
  transfers between devices with their start and end apart: 4, of which 3 were waited for; matrix products, arithmetic and copies ran while one was open for 0% of the time, Pallas kernels for 0%

profile of v4, /device:TPU:8, one launch (start us, length us, event | category | flops | bytes accessed | tf_op | source)
XLA Modules:
  0.0 148.3 jit_solution(11780680897729853888)
XLA Ops:
  0.0 1.9 %pack.1 = f32[896,128]{1,0:T(8,128)} custom-call(f32[3]{0:T(128)} %cond.3, f32[16,3,2,8,128]{4,3,2,1,0:T(8,128)} %forcing.1, f32[3,2,8,128]{3,2,1,0:T(8,128)} %start.1, f32[16,3,2,8,128]{4,3,2,1,0:T(8,128)} %latest.1, s32[2,8,128]{2,1,0:T(8,128)} %region.3), custom_call_target="tpu_custom_call" | custom-call | tf_op jit(solution)/shard_map/pack/pallas_call | solution.py:359
  1.9 0.0 copy-start.1
  1.9 0.0 copy-start.2
  1.9 0.0 copy-start.3
  1.9 34.2 %all_to_all.32.got = f32[16,56,128]{2,1,0:T(8,128)S(1)} all-to-all(f32[16,56,128]{2,1,0:T(8,128)} %bitcast.19), channel_id=1, replica_groups=mesh['yh'=2,'z'=8,'xh'=2,'xl'=2,'yl'=4,'c'=2] {'yh','z'}, dimensions={0} | all-to-all | bytes 917504 | tf_op jit(solution)/shard_map/all_to_all | solution.py:375
  36.1 0.0 copy-done.1
  36.1 0.0 copy-done.2
  36.1 0.0 copy-done.3
  36.1 1.1 forward.1
  37.3 1.2 copy.10
  38.5 8.2 %all-to-all-start.1 = ((f32[128,1,896]{2,1,0:T(1,128)}), f32[128,1,896]{2,1,0:T(1,128)S(1)}, u32[]{:S(2)}, u32[]{:S(2)}) async-start(f32[128,1,896]{2,1,0:T(1,128)} %copy.10), calls=%async_computation.1 | async-start | bytes 917504 | tf_op jit(solution)/shard_map/all_to_all | solution.py:386
  46.7 18.2 %all-to-all-done.1 = f32[128,1,896]{2,1,0:T(1,128)S(1)} async-done(((f32[128,1,896]{2,1,0:T(1,128)}), f32[128,1,896]{2,1,0:T(1,128)S(1)}, u32[]{:S(2)}, u32[]{:S(2)}) %all-to-all-start.1) | async-done | bytes 458784 | tf_op jit(solution)/shard_map/all_to_all | solution.py:386
  64.9 0.1 constant_dynamic-slice_fusion
  65.0 4.8 %collective-permute-start.1 = (f32[96,896]{1,0:T(8,128)S(1)}, f32[96,896]{1,0:T(8,128)S(1)}, u32[]{:S(2)}, u32[]{:S(2)}) collective-permute-start(f32[96,896]{1,0:T(8,128)S(1)} %bitcast.20), channel_id=1, source_target_pairs={{0,24},{8,16},{16,8},{24,0},{1,25},{9,17},{17,9},{25,1},{2,26},{10... | collective-permute-start | bytes 1032200 | tf_op jit(solution)/shard_map/ppermute | solution.py:393
  69.8 0.0 copy-start.4
  69.9 0.0 copy-start.5
  69.9 1.9 %collective-permute-start = (f32[128,896]{1,0:T(8,128)S(1)}, f32[128,896]{1,0:T(8,128)S(1)}, u32[]{:S(2)}, u32[]{:S(2)}) collective-permute-start(f32[128,896]{1,0:T(8,128)S(1)} %bitcast.13), channel_id=1, source_target_pairs={{0,1},{1,0},{2,3},{3,2},{4,5},{5,4},{6,7},{7,6},{8,9},{9,8},{10,11... | collective-permute-start | bytes 1376264 | tf_op jit(solution)/shard_map/ppermute | solution.py:394
  71.8 4.6 %collective-permute-done.1.part = f32[96,896]{1,0:T(8,128)S(1)} collective-permute-done((f32[96,896]{1,0:T(8,128)S(1)}, f32[96,896]{1,0:T(8,128)S(1)}, u32[]{:S(2)}, u32[]{:S(2)}) %collective-permute-start.1) | collective-permute-done | bytes 344096 | tf_op jit(solution)/shard_map/ppermute | solution.py:393
  76.4 1.9 %collective-permute-start.2 = (f32[96,896]{1,0:T(8,128)S(1)}, f32[96,896]{1,0:T(8,128)S(1)}, u32[]{:S(2)}, u32[]{:S(2)}) collective-permute-start(f32[96,896]{1,0:T(8,128)S(1)} %collective-permute-done.1.part), channel_id=1, source_target_pairs={{0,1},{1,0},{2,3},{3,2},{4,5},{5,4},{6,7},{7,6},{8,9},{9,8},{10,11... | collective-permute-start | bytes 1032200 | tf_op jit(solution)/shard_map/ppermute | solution.py:395
  78.3 0.0 collective-permute-done.mate
  78.3 1.6 %collective-permute-done.2.part_mate = f32[96,896]{1,0:T(8,128)S(1)} collective-permute-done((f32[96,896]{1,0:T(8,128)S(1)}, f32[96,896]{1,0:T(8,128)S(1)}, u32[]{:S(2)}, u32[]{:S(2)}) %collective-permute-start.2) | collective-permute-done | bytes 344096 | tf_op jit(solution)/shard_map/ppermute | solution.py:395
  79.9 0.0 copy-done.4
  79.9 0.0 copy-done.5
  79.9 19.0 %solve.1 = f32[128,768]{1,0:T(8,128)S(1)} custom-call(f32[4,128]{1,0:T(4,128)S(1)} %copy-done.4, f32[2,11]{1,0:T(2,128)S(1)} %copy-done.5, f32[128,896]{1,0:T(8,128)S(1)} %bitcast.14, f32[128,896]{1,0:T(8,128)S(1)} %collective-permute-done.mate, f32[96,896]{1,0:T(8,128)S(1)} %collective-permute-done.1.part, f32[96,896]{1,0:T(8,128)S(1)} %collective-permute-done.2.part_mate), custom_call_target="tpu_custom_call" | custom-call | tf_op jit(solution)/shard_map/solve/pallas_call | solution.py:400
  98.9 0.4 copy.11
  99.3 25.0 %all_to_all.33 = f32[128,1,768]{2,1,0:T(1,128)S(1)} all-to-all(f32[128,1,768]{2,1,0:T(1,128)S(1)} %copy.11), channel_id=1, replica_groups=mesh['yh'=2,'z'=8,'xh'=2,'xl'=2,'yl'=4,'c'=2] {'xl','yl','yh','z'}, dimensions={0} | all-to-all | bytes 786432 | tf_op jit(solution)/shard_map/all_to_all | solution.py:425
  124.3 0.0 copy-start
  124.4 0.9 copy-done
  125.3 0.8 inverse.1
  126.1 21.4 %all_to_all.34 = f32[16,48,128]{2,1,0:T(8,128)S(1)} all-to-all(f32[16,48,128]{2,1,0:T(8,128)S(1)} %inverse.1), channel_id=1, replica_groups=mesh['yh'=2,'z'=8,'xh'=2,'xl'=2,'yl'=4,'c'=2] {'yh','z'}, dimensions={0} | all-to-all | bytes 786432 | tf_op jit(solution)/shard_map/all_to_all | solution.py:436
  147.4 0.9 unpack.1
  (3 shorter events, 0.1 us)
Async XLA Ops:
  1.9 34.2 %copy-start.1 = (f32[256,256]{1,0:T(8,128)S(1)}, f32[256,256]{1,0:T(8,128)}, u32[]{:S(2)}) copy-start(f32[256,256]{1,0:T(8,128)} %constant.23.clone.table) | copy-start | bytes 786436
  1.9 34.2 %copy-start.2 = (s32[2,8,128]{2,1,0:T(8,128)S(1)}, s32[2,8,128]{2,1,0:T(8,128)}, u32[]{:S(2)}) copy-start(s32[2,8,128]{2,1,0:T(8,128)} %region.3) | copy-start | bytes 24580
  1.9 34.2 %copy-start.3 = (f32[3]{0:T(128)S(1)}, f32[3]{0:T(128)}, u32[]{:S(2)}) copy-start(f32[3]{0:T(128)} %cond.3) | copy-start | bytes 40
  38.5 26.4 %all-to-all-start.1 = ((f32[128,1,896]{2,1,0:T(1,128)}), f32[128,1,896]{2,1,0:T(1,128)S(1)}, u32[]{:S(2)}, u32[]{:S(2)}) async-start(f32[128,1,896]{2,1,0:T(1,128)} %copy.10), calls=%async_computation.1 | async-start | bytes 917504 | tf_op jit(solution)/shard_map/all_to_all | solution.py:386
  65.0 11.4 %collective-permute-start.1 = (f32[96,896]{1,0:T(8,128)S(1)}, f32[96,896]{1,0:T(8,128)S(1)}, u32[]{:S(2)}, u32[]{:S(2)}) collective-permute-start(f32[96,896]{1,0:T(8,128)S(1)} %bitcast.20), channel_id=1, source_target_pairs={{0,24},{8,16},{16,8},{24,0},{1,25},{9,17},{17,9},{25,1},{2,26},{10... | collective-permute-start | bytes 1032200 | tf_op jit(solution)/shard_map/ppermute | solution.py:393
  69.8 10.1 %copy-start.4 = (f32[4,128]{1,0:T(4,128)S(1)}, f32[4,128]{1,0:T(4,128)}, u32[]{:S(2)}) copy-start(f32[4,128]{1,0:T(4,128)} %constant.24.clone.terms) | copy-start | bytes 6148
  69.9 10.0 %copy-start.5 = (f32[2,11]{1,0:T(2,128)S(1)}, f32[2,11]{1,0:T(2,128)}, u32[]{:S(2)}) copy-start(f32[2,11]{1,0:T(2,128)} %constant.25.clone.weights) | copy-start | bytes 268
  69.9 8.4 %collective-permute-start = (f32[128,896]{1,0:T(8,128)S(1)}, f32[128,896]{1,0:T(8,128)S(1)}, u32[]{:S(2)}, u32[]{:S(2)}) collective-permute-start(f32[128,896]{1,0:T(8,128)S(1)} %bitcast.13), channel_id=1, source_target_pairs={{0,1},{1,0},{2,3},{3,2},{4,5},{5,4},{6,7},{7,6},{8,9},{9,8},{10,11... | collective-permute-start | bytes 1376264 | tf_op jit(solution)/shard_map/ppermute | solution.py:394
  76.4 3.5 %collective-permute-start.2 = (f32[96,896]{1,0:T(8,128)S(1)}, f32[96,896]{1,0:T(8,128)S(1)}, u32[]{:S(2)}, u32[]{:S(2)}) collective-permute-start(f32[96,896]{1,0:T(8,128)S(1)} %collective-permute-done.1.part), channel_id=1, source_target_pairs={{0,1},{1,0},{2,3},{3,2},{4,5},{5,4},{6,7},{7,6},{8,9},{9,8},{10,11... | collective-permute-start | bytes 1032200 | tf_op jit(solution)/shard_map/ppermute | solution.py:395
  124.3 1.0 copy-start

commit v5 on v4

--- a/solution.py
+++ b/solution.py
@@ -24,14 +24,6 @@
 STRIPE = 2
 GUARD = 1
 CHUNK = 14
-
-
-def pair_rows(count):
-    flip = lax.axis_index("xh")
-    size = count // 2
-    return tuple(
-        pl.ds(pl.multiple_of(at * size, size), size) for at in (flip, 1 - flip)
-    )
 
 
 def pair_index():
@@ -90,28 +82,24 @@
 
 
 def pack_kernel(cond, forcing, start, latest, region, out):
-    steps, comps, planes, ny, _ = forcing.shape
-    rows = out.shape[0] // (planes * ny)
+    steps, comps, _, ny, _ = forcing.shape
+    rows = out.shape[0] // ny
     is_first = (lax.axis_index("yh") == 0) & (lax.axis_index("z") == 0)
-    for p in range(planes):
-        sigma = material(region[p], cond)
-        base = p * ny * rows
-        for c in range(comps):
-            head = forcing[0, c, p]
-            head = head + jnp.where(is_first, sigma * start[c, p], 0.0)
-            out[pl.ds(base + c * steps, ny, stride=rows), :] = head
-            for b in range(1, steps):
-                out[pl.ds(base + c * steps + b, ny, stride=rows), :] = forcing[b, c, p]
-            out[pl.ds(base + comps * steps + c, ny, stride=rows), :] = -ALPHA * (
-                sigma * latest[0, c, p]
-            )
-        for pad in range(comps * steps + comps, rows):
-            out[pl.ds(base + pad, ny, stride=rows), :] = jnp.zeros_like(sigma)
-
-
-def forward_kernel(cond, got, table, region, out):
+    sigma = material(region[0], cond)
+    for c in range(comps):
+        head = forcing[0, c, 0]
+        head = head + jnp.where(is_first, sigma * start[c, 0], 0.0)
+        out[pl.ds(c * steps, ny, stride=rows), :] = head
+        for b in range(1, steps):
+            out[pl.ds(c * steps + b, ny, stride=rows), :] = forcing[b, c, 0]
+        out[pl.ds(comps * steps + c, ny, stride=rows), :] = -ALPHA * (sigma * latest[0, c, 0])
+    for pad in range(comps * steps + comps, rows):
+        out[pl.ds(pad, ny, stride=rows), :] = jnp.zeros_like(sigma)
+
+
+def forward_kernel(cond, got, tables, region, out):
     groups, _, nz = got.shape
-    window = table.shape[0]
+    window = tables.shape[1]
     steps = window // groups
     comps = 3
     half = window // 2
@@ -122,30 +110,54 @@
         row = got[groups - 1, comps * steps + c : comps * steps + c + 1, :]
         parts.append(part + jnp.where(head, row, 0.0))
     spectrum = jnp.dot(
-        table[...],
+        tables[0],
         jnp.concatenate(parts, axis=1),
         precision=lax.Precision.HIGHEST,
         preferred_element_type=jnp.float32,
     )
     width = comps * nz
-    for at, rows in enumerate(pair_rows(half)):
-        lines = slice(at * (half // 2), (at + 1) * (half // 2))
-        out[rows, :width] = spectrum[:half][lines]
-        out[rows, width : 2 * width] = spectrum[half:][lines]
+    flip = lax.axis_index("xh")
     line = region[lax.axis_index("yh"), pl.ds(lax.axis_index("z"), 1), :]
-    out[:, 2 * width :] = jnp.broadcast_to(material(line, cond), (half, nz))
-
-
-def inverse_kernel(got, table, out):
-    half, wide = got.shape
+    weight = jnp.broadcast_to(material(line, cond), (8, nz))
+    cols = out.shape[0] // half
+    for at in range(half // 8):
+        lower = at < half // 16
+        begin = at * 8 + (flip if lower else -flip) * (half // 2)
+        for k in range(2 * comps):
+            block = spectrum[
+                k // comps * half + at * 8 : k // comps * half + at * 8 + 8,
+                k % comps * nz : (k % comps + 1) * nz,
+            ]
+            out[pl.ds(begin * cols + k, 8, stride=cols), :] = block
+        out[pl.ds(begin * cols + 2 * comps, 8, stride=cols), :] = weight
+
+
+def inverse_kernel(got, tables, out):
     groups, rows, nz = out.shape
-    steps = table.shape[0] // groups
-    width = wide // 2
+    _, window, _ = tables.shape
+    half = window // 2
+    steps = window // groups
+    cols = got.shape[0] // half
     dot = functools.partial(
         jnp.dot, precision=lax.Precision.HIGHEST, preferred_element_type=jnp.float32
     )
-    solved = jnp.concatenate([got[rows, :] for rows in pair_rows(half)], axis=0)
-    result = dot(table[:, :half], solved[:, :width]) + dot(table[:, half:], solved[:, width:])
+    flip = lax.axis_index("xh")
+    size = half // 2
+
+    def member(f):
+        return jnp.concatenate(
+            [
+                jnp.concatenate(
+                    [got[pl.ds(at * size * cols + k, size, stride=cols), :] for at in (flip, 1 - flip)],
+                    axis=0,
+                )
+                for k in range(f * cols // 2, (f + 1) * cols // 2)
+            ],
+            axis=1,
+        )
+
+    table = tables.at[1]
+    result = dot(table[:, :half], member(0)) + dot(table[:, half:], member(1))
     for c in range(rows // steps):
         out[:, c * steps : (c + 1) * steps, :] = result[:, c * nz : (c + 1) * nz].reshape(
             groups, steps, nz
@@ -153,12 +165,11 @@
 
 
 def unpack_kernel(got, out):
-    steps, comps, planes, ny, _ = out.shape
-    rows = got.shape[0] // (planes * ny)
-    for p in range(planes):
-        for c in range(comps):
-            for b in range(steps):
-                out[b, c, p] = got[pl.ds(p * ny * rows + c * steps + b, ny, stride=rows), :]
+    steps, comps, _, ny, _ = out.shape
+    rows = got.shape[0] // ny
+    for c in range(comps):
+        for b in range(steps):
+            out[b, c, 0] = got[pl.ds(c * steps + b, ny, stride=rows), :]
 
 
 def solve_kernel(terms, weights, mine, mate, part, part_mate, out, field, first, resid, total, sigma, flux_a, flux_b):
@@ -243,11 +254,11 @@
     width = HALF + REACH
 
     def fill(source, begin):
-        for at in range(source.shape[0] // ny):
+        for at in range(source.shape[0] // (7 * ny)):
             i = begin + (at // STRIPE) * (2 * STRIPE) + at % STRIPE
-            line = slice(at * ny, (at + 1) * ny)
-            store(first, i, [source[line, k * nz : (k + 1) * nz] for k in range(6)])
-            sigma[i + GUARD] = source[line, 6 * nz :]
+            parts = [source[pl.ds(at * 7 * ny + k, ny, stride=7), :] for k in range(7)]
+            store(first, i, parts[:6])
+            sigma[i + GUARD] = parts[6]
 
     for ref in (first, field):
         store(ref, -1, [blank] * 6)
@@ -338,7 +349,7 @@
 
     for at, h in enumerate(own_planes):
         for k in range(6):
-            out[at * ny : (at + 1) * ny, k * nz : (k + 1) * nz] = (
+            out[pl.ds(at * 6 * ny + k, ny, stride=6), :] = (
                 total[at, k] + field[own_begin + h + GUARD, k]
             )
 
@@ -348,26 +359,26 @@
     groups = lax.axis_size(TM)
     window = steps * groups
     half = window // 2
-    forward_table, inverse_table = tables(window)
+    both = jnp.asarray(np.stack(tables(window)))
     vmem = pl.BlockSpec(memory_space=pltpu.VMEM)
     smem = pl.BlockSpec(memory_space=pltpu.SMEM)
     f32 = jnp.float32
     params = pltpu.CompilerParams(vmem_limit_bytes=12 * 1024 * 1024)
 
     rows = comps * steps + 8
-    whole = lambda shape: pl.BlockSpec(shape, lambda i: (0,) * len(shape))
+    plane_of = pl.BlockSpec((steps, comps, 1, ny, nz), lambda p: (0, 0, p, 0, 0))
     packed = pl.pallas_call(
         pack_kernel,
         out_shape=jax.ShapeDtypeStruct((groups * rows, nz), f32),
-        grid=(1,),
+        grid=(planes,),
         in_specs=[
             smem,
-            whole(forcing.shape),
-            whole(start_field.shape),
-            pl.BlockSpec((1, comps, planes, ny, nz), lambda i: (steps - 1, 0, 0, 0, 0)),
-            whole(region.shape),
+            plane_of,
+            pl.BlockSpec((comps, 1, ny, nz), lambda p: (0, p, 0, 0)),
+            pl.BlockSpec((1, comps, 1, ny, nz), lambda p: (steps - 1, 0, p, 0, 0)),
+            pl.BlockSpec((1, ny, nz), lambda p: (p, 0, 0)),
         ],
-        out_specs=whole((groups * rows, nz)),
+        out_specs=pl.BlockSpec((ny * rows, nz), lambda p: (p, 0)),
         compiler_params=pltpu.CompilerParams(vmem_limit_bytes=60 * 1024 * 1024),
         name="pack",
     )(conductance, forcing, start_field, iterate, region)
@@ -376,19 +387,22 @@
 
     spectrum = pl.pallas_call(
         forward_kernel,
-        out_shape=jax.ShapeDtypeStruct((half, (2 * comps + 1) * nz), f32),
+        out_shape=jax.ShapeDtypeStruct((half * (2 * comps + 1), nz), f32),
         in_specs=[smem, vmem, vmem, vmem],
         out_specs=vmem,
         compiler_params=params,
         name="forward",
-    )(conductance, got, jnp.asarray(forward_table), region)
-
-    mine = lax.all_to_all(spectrum, GROUP, 0, 0, tiled=True)
+    )(conductance, got, both, region)
+
+    mine = lax.all_to_all(
+        spectrum.reshape(half, 1, (2 * comps + 1) * nz), GROUP, 0, 0, tiled=True
+    )
 
     rows_sent = half * REACH // HALF
     part = lax.dynamic_slice_in_dim(
         mine, (1 - lax.axis_index("xh")) * (half - rows_sent), rows_sent, 0
-    )
+    ).reshape(rows_sent * (2 * comps + 1), nz)
+    mine = mine.reshape(half * (2 * comps + 1), nz)
     blocks = lax.axis_size(("xh", "xl"))
     part = lax.ppermute(part, ("xh", "xl"), [(i, blocks - 1 - i) for i in range(blocks)])
     mate = lax.ppermute(mine, "c", [(0, 1), (1, 0)])
@@ -399,7 +413,7 @@
     flux_shape = pltpu.VMEM((CHUNK + 1, 2 * comps, ny, nz), f32)
     solved = pl.pallas_call(
         solve_kernel,
-        out_shape=jax.ShapeDtypeStruct((half, 2 * comps * nz), f32),
+        out_shape=jax.ShapeDtypeStruct((half * 2 * comps, nz), f32),
         in_specs=[smem, smem, vmem, vmem, vmem, vmem],
         out_specs=vmem,
         scratch_shapes=[
@@ -422,7 +436,9 @@
         part_mate,
     )
 
-    back = lax.all_to_all(solved, GROUP, 0, 0, tiled=True)
+    back = lax.all_to_all(
+        solved.reshape(half, 1, 2 * comps * nz), GROUP, 0, 0, tiled=True
+    ).reshape(half * 2 * comps, nz)
 
     pencil = pl.pallas_call(
         inverse_kernel,
@@ -431,15 +447,16 @@
         out_specs=vmem,
         compiler_params=params,
         name="inverse",
-    )(back, jnp.asarray(inverse_table))
+    )(back, both)
 
     home = lax.all_to_all(pencil, TM, 0, 0, tiled=True)
 
     return pl.pallas_call(
         unpack_kernel,
         out_shape=jax.ShapeDtypeStruct(forcing.shape, f32),
-        in_specs=[vmem],
-        out_specs=vmem,
+        grid=(planes,),
+        in_specs=[pl.BlockSpec((ny * comps * steps, nz), lambda p: (p, 0))],
+        out_specs=plane_of,
         compiler_params=params,
         name="unpack",
     )(home.reshape(groups * comps * steps, nz))

time: 149 us -> 147 us (0.987)
  local copies, waits for them, and re-layouts: 2.77 us -> 0.13 us
    all_to_all x2 -> x0, local copies, waits for them, and re-layouts: 1.64 us -> none  [the longest x1 1.24 us: per_device(): mine = lax.all_to_all(spectrum, GROUP, 0, 0, tiled=True)]
where the time goes in v5:
time: 147 us; the launch traced here: 146 us
  blocking collectives  80.6 us (55%)
  waiting for transfers between devices  24.4 us (17%)
  Pallas kernels  24.3 us (17%)
  starting transfers between devices  16.8 us (11%)
    all_to_all x1, blocking collectives, per_device(): got = lax.all_to_all(packed.reshape(groups, rows, nz), TM, 0, 0, tiled=True)  34.2 us
    all_to_all x1, blocking collectives, per_device(): lax.all_to_all(solved.reshape(half, 1, 2 * comps * nz), GROUP, 0, 0, tile...  25 us
    all_to_all x1, blocking collectives, per_device(): home = lax.all_to_all(pencil, TM, 0, 0, tiled=True)  21.4 us
    pallas_call x1, Pallas kernels, per_device(): pl.pallas_call(solve_kernel, out_shape=jax.ShapeDtypeStruct((half * 2 * c...  19 us
    all_to_all x1, waiting for transfers between devices, per_device(): lax.all_to_all(spectrum.reshape(half, 1, (2 * comps + 1) * nz), GROUP, 0,...  18.2 us
    all_to_all x1, starting transfers between devices, per_device(): lax.all_to_all(spectrum.reshape(half, 1, (2 * comps + 1) * nz), GROUP, 0,...  8.18 us
    ppermute x1, starting transfers between devices, per_device(): lax.ppermute(part, ('xh', 'xl'), [(i, blocks - 1 - i) for i in range(bloc...  4.81 us
    ppermute x1, waiting for transfers between devices, per_device(): lax.ppermute(part, ('xh', 'xl'), [(i, blocks - 1 - i) for i in range(bloc...  4.63 us
  transfers between devices with their start and end apart: 4, of which 3 were waited for; matrix products, arithmetic and copies ran while one was open for 0% of the time, Pallas kernels for 0%

profile of v5, /device:TPU:8, one launch (start us, length us, event | category | flops | bytes accessed | tf_op | source)
XLA Modules:
  0.0 146.4 jit_solution(13008781784792010465)
XLA Ops:
  0.0 1.8 %pack.1 = f32[896,128]{1,0:T(8,128)} custom-call(f32[3]{0:T(128)} %cond.3, f32[16,3,2,8,128]{4,3,2,1,0:T(8,128)} %forcing.1, f32[3,2,8,128]{3,2,1,0:T(8,128)} %start.1, f32[16,3,2,8,128]{4,3,2,1,0:T(8,128)} %latest.1, s32[2,8,128]{2,1,0:T(8,128)} %region.3), custom_call_target="tpu_custom_call" | custom-call | tf_op jit(solution)/shard_map/pack/pallas_call | solution.py:370
  1.8 0.0 copy-start
  1.8 0.0 copy-start.1
  1.8 0.0 copy-start.2
  1.9 34.2 %all_to_all.20.got = f32[16,56,128]{2,1,0:T(8,128)S(1)} all-to-all(f32[16,56,128]{2,1,0:T(8,128)} %bitcast.12), channel_id=1, replica_groups=mesh['yh'=2,'z'=8,'xh'=2,'xl'=2,'yl'=4,'c'=2] {'yh','z'}, dimensions={0} | all-to-all | bytes 917504 | tf_op jit(solution)/shard_map/all_to_all | solution.py:386
  36.1 0.0 copy-done
  36.1 0.0 copy-done.1
  36.1 0.0 copy-done.2
  36.1 1.9 %forward.1 = f32[896,128]{1,0:T(8,128)} custom-call(f32[3]{0:T(128)S(1)} %copy-done.2, f32[16,56,128]{2,1,0:T(8,128)S(1)} %all_to_all.20.got, f32[2,256,256]{2,1,0:T(8,128)S(1)} %copy-done, s32[2,8,128]{2,1,0:T(8,128)S(1)} %copy-done.1), custom_call_target="tpu_custom_call" | custom-call | tf_op jit(solution)/shard_map/forward/pallas_call | solution.py:388
  38.0 8.2 %all-to-all-start.1 = ((f32[128,1,896]{2,1,0:T(1,128)}), f32[128,1,896]{2,1,0:T(1,128)S(1)}, u32[]{:S(2)}, u32[]{:S(2)}) async-start(f32[128,1,896]{2,1,0:T(1,128)} %bitcast.1), calls=%async_computation.1 | async-start | bytes 917504 | tf_op jit(solution)/shard_map/all_to_all | solution.py:397
  46.2 18.2 %all-to-all-done.1 = f32[128,1,896]{2,1,0:T(1,128)S(1)} async-done(((f32[128,1,896]{2,1,0:T(1,128)}), f32[128,1,896]{2,1,0:T(1,128)S(1)}, u32[]{:S(2)}, u32[]{:S(2)}) %all-to-all-start.1) | async-done | bytes 458784 | tf_op jit(solution)/shard_map/all_to_all | solution.py:397
  64.4 0.1 constant_dynamic-slice_fusion
  64.5 0.0 copy-start.3
  64.5 0.0 copy-start.4
  64.5 4.8 %collective-permute-start.1 = (f32[672,128]{1,0:T(8,128)S(1)}, f32[672,128]{1,0:T(8,128)S(1)}, u32[]{:S(2)}, u32[]{:S(2)}) collective-permute-start(f32[672,128]{1,0:T(8,128)S(1)} %bitcast.13), channel_id=1, source_target_pairs={{0,24},{8,16},{16,8},{24,0},{1,25},{9,17},{17,9},{25,1},{2,26},{10... | collective-permute-start | bytes 1032200 | tf_op jit(solution)/shard_map/ppermute | solution.py:407
  69.3 1.9 %collective-permute-start = (f32[896,128]{1,0:T(8,128)S(1)}, f32[896,128]{1,0:T(8,128)S(1)}, u32[]{:S(2)}, u32[]{:S(2)}) collective-permute-start(f32[896,128]{1,0:T(8,128)S(1)} %bitcast.7), channel_id=1, source_target_pairs={{0,1},{1,0},{2,3},{3,2},{4,5},{5,4},{6,7},{7,6},{8,9},{9,8},{10,11... | collective-permute-start | bytes 1376264 | tf_op jit(solution)/shard_map/ppermute | solution.py:408
  71.2 4.6 %collective-permute-done.1.part = f32[672,128]{1,0:T(8,128)S(1)} collective-permute-done((f32[672,128]{1,0:T(8,128)S(1)}, f32[672,128]{1,0:T(8,128)S(1)}, u32[]{:S(2)}, u32[]{:S(2)}) %collective-permute-start.1) | collective-permute-done | bytes 344096 | tf_op jit(solution)/shard_map/ppermute | solution.py:407
  75.9 1.9 %collective-permute-start.2 = (f32[672,128]{1,0:T(8,128)S(1)}, f32[672,128]{1,0:T(8,128)S(1)}, u32[]{:S(2)}, u32[]{:S(2)}) collective-permute-start(f32[672,128]{1,0:T(8,128)S(1)} %collective-permute-done.1.part), channel_id=1, source_target_pairs={{0,1},{1,0},{2,3},{3,2},{4,5},{5,4},{6,7},{7,6},{8,9},{9,8},{10,11... | collective-permute-start | bytes 1032200 | tf_op jit(solution)/shard_map/ppermute | solution.py:409
  77.8 0.0 collective-permute-done.mate
  77.8 1.6 %collective-permute-done.2.part_mate = f32[672,128]{1,0:T(8,128)S(1)} collective-permute-done((f32[672,128]{1,0:T(8,128)S(1)}, f32[672,128]{1,0:T(8,128)S(1)}, u32[]{:S(2)}, u32[]{:S(2)}) %collective-permute-start.2) | collective-permute-done | bytes 344096 | tf_op jit(solution)/shard_map/ppermute | solution.py:409
  79.4 0.0 copy-done.3
  79.4 0.0 copy-done.4
  79.4 19.0 %solve.1 = f32[768,128]{1,0:T(8,128)S(1)} custom-call(f32[4,128]{1,0:T(4,128)S(1)} %copy-done.3, f32[2,11]{1,0:T(2,128)S(1)} %copy-done.4, f32[896,128]{1,0:T(8,128)S(1)} %bitcast.8, f32[896,128]{1,0:T(8,128)S(1)} %collective-permute-done.mate, f32[672,128]{1,0:T(8,128)S(1)} %collective-permute-done.1.part, f32[672,128]{1,0:T(8,128)S(1)} %collective-permute-done.2.part_mate), custom_call_target="tpu_custom_call" | custom-call | tf_op jit(solution)/shard_map/solve/pallas_call | solution.py:414
  98.4 25.0 %all_to_all.21 = f32[128,1,768]{2,1,0:T(1,128)S(1)} all-to-all(f32[128,1,768]{2,1,0:T(1,128)S(1)} %bitcast.10), channel_id=1, replica_groups=mesh['yh'=2,'z'=8,'xh'=2,'xl'=2,'yl'=4,'c'=2] {'xl','yl','yh','z'}, dimensions={0} | all-to-all | bytes 786432 | tf_op jit(solution)/shard_map/all_to_all | solution.py:439
  123.4 0.8 inverse.1
  124.2 21.4 %all_to_all.22 = f32[16,48,128]{2,1,0:T(8,128)S(1)} all-to-all(f32[16,48,128]{2,1,0:T(8,128)S(1)} %inverse.1), channel_id=1, replica_groups=mesh['yh'=2,'z'=8,'xh'=2,'xl'=2,'yl'=4,'c'=2] {'yh','z'}, dimensions={0} | all-to-all | bytes 786432 | tf_op jit(solution)/shard_map/all_to_all | solution.py:452
  145.6 0.8 unpack.1
Async XLA Ops:
  1.8 34.3 %copy-start = (f32[2,256,256]{2,1,0:T(8,128)S(1)}, f32[2,256,256]{2,1,0:T(8,128)}, u32[]{:S(2)}) copy-start(f32[2,256,256]{2,1,0:T(8,128)} %constant.20.clone.tables) | copy-start | bytes 1572868
  1.8 34.3 %copy-start.1 = (s32[2,8,128]{2,1,0:T(8,128)S(1)}, s32[2,8,128]{2,1,0:T(8,128)}, u32[]{:S(2)}) copy-start(s32[2,8,128]{2,1,0:T(8,128)} %region.3) | copy-start | bytes 24580
  1.8 34.3 %copy-start.2 = (f32[3]{0:T(128)S(1)}, f32[3]{0:T(128)}, u32[]{:S(2)}) copy-start(f32[3]{0:T(128)} %cond.3) | copy-start | bytes 40
  38.0 26.4 %all-to-all-start.1 = ((f32[128,1,896]{2,1,0:T(1,128)}), f32[128,1,896]{2,1,0:T(1,128)S(1)}, u32[]{:S(2)}, u32[]{:S(2)}) async-start(f32[128,1,896]{2,1,0:T(1,128)} %bitcast.1), calls=%async_computation.1 | async-start | bytes 917504 | tf_op jit(solution)/shard_map/all_to_all | solution.py:397
  64.5 14.9 %copy-start.3 = (f32[4,128]{1,0:T(4,128)S(1)}, f32[4,128]{1,0:T(4,128)}, u32[]{:S(2)}) copy-start(f32[4,128]{1,0:T(4,128)} %constant.21.clone.terms) | copy-start | bytes 6148
  64.5 14.9 %copy-start.4 = (f32[2,11]{1,0:T(2,128)S(1)}, f32[2,11]{1,0:T(2,128)}, u32[]{:S(2)}) copy-start(f32[2,11]{1,0:T(2,128)} %constant.22.clone.weights) | copy-start | bytes 268
  64.5 11.4 %collective-permute-start.1 = (f32[672,128]{1,0:T(8,128)S(1)}, f32[672,128]{1,0:T(8,128)S(1)}, u32[]{:S(2)}, u32[]{:S(2)}) collective-permute-start(f32[672,128]{1,0:T(8,128)S(1)} %bitcast.13), channel_id=1, source_target_pairs={{0,24},{8,16},{16,8},{24,0},{1,25},{9,17},{17,9},{25,1},{2,26},{10... | collective-permute-start | bytes 1032200 | tf_op jit(solution)/shard_map/ppermute | solution.py:407
  69.3 8.5 %collective-permute-start = (f32[896,128]{1,0:T(8,128)S(1)}, f32[896,128]{1,0:T(8,128)S(1)}, u32[]{:S(2)}, u32[]{:S(2)}) collective-permute-start(f32[896,128]{1,0:T(8,128)S(1)} %bitcast.7), channel_id=1, source_target_pairs={{0,1},{1,0},{2,3},{3,2},{4,5},{5,4},{6,7},{7,6},{8,9},{9,8},{10,11... | collective-permute-start | bytes 1376264 | tf_op jit(solution)/shard_map/ppermute | solution.py:408
  75.9 3.5 %collective-permute-start.2 = (f32[672,128]{1,0:T(8,128)S(1)}, f32[672,128]{1,0:T(8,128)S(1)}, u32[]{:S(2)}, u32[]{:S(2)}) collective-permute-start(f32[672,128]{1,0:T(8,128)S(1)} %collective-permute-done.1.part), channel_id=1, source_target_pairs={{0,1},{1,0},{2,3},{3,2},{4,5},{5,4},{6,7},{7,6},{8,9},{9,8},{10,11... | collective-permute-start | bytes 1032200 | tf_op jit(solution)/shard_map/ppermute | solution.py:409

commit v6 on v5

--- a/solution.py
+++ b/solution.py
@@ -23,7 +23,8 @@
 REACH = 24
 STRIPE = 2
 GUARD = 1
-CHUNK = 14
+INNER = 8
+OUTER = 12
 
 
 def pair_index():
@@ -172,20 +173,15 @@
             out[b, c, 0] = got[pl.ds(c * steps + b, ny, stride=rows), :]
 
 
-def solve_kernel(terms, weights, mine, mate, part, part_mate, out, field, first, resid, total, sigma, flux_a, flux_b):
-    ny, nz = field.shape[2:]
-    half_at = lax.axis_index("xh")
-    core_at = lax.axis_index("c")
+def operator(terms, sigma):
+    ny, nz = sigma.shape[1:]
     pair = pair_index()
-    p_plus, p_minus = terms[0, pair], terms[1, pair]
-    q_term, inv_scale = terms[2, pair], terms[3, pair]
-    _, _, center = chebyshev_terms(SWEEPS - 1)
+    p_plus, p_minus, q_term = terms[0, pair], terms[1, pair], terms[2, pair]
 
     row = lax.broadcasted_iota(jnp.int32, (ny, nz), 0)
     lane = lax.broadcasted_iota(jnp.int32, (ny, nz), 1)
     row_first, row_last = row == 0, row == ny - 1
     lane_first, lane_last = lane == 0, lane == nz - 1
-    blank = jnp.zeros((ny, nz), jnp.float32)
 
     def ahead_y(f):
         return jnp.where(row_last, 0.0, pltpu.roll(f, ny - 1, 0))
@@ -240,48 +236,12 @@
             field[c] + (sp * values[c] - sq * values[3 + c]) for c in range(3)
         ] + [field[3 + c] + (sm * values[3 + c] + sq * values[c]) for c in range(3)]
 
-    def load(ref, at):
-        return [ref[at + GUARD, k] for k in range(6)]
-
-    def store(ref, at, values):
-        for k in range(6):
-            ref[at + GUARD, k] = values[k]
-
-    own_low = REACH * half_at
-    halo_low = HALF * (1 - half_at)
-    grid_low = -(HALF - REACH) * half_at
-    grid_high = grid_low + 2 * HALF
-    width = HALF + REACH
-
-    def fill(source, begin):
-        for at in range(source.shape[0] // (7 * ny)):
-            i = begin + (at // STRIPE) * (2 * STRIPE) + at % STRIPE
-            parts = [source[pl.ds(at * 7 * ny + k, ny, stride=7), :] for k in range(7)]
-            store(first, i, parts[:6])
-            sigma[i + GUARD] = parts[6]
-
-    for ref in (first, field):
-        store(ref, -1, [blank] * 6)
-        store(ref, width, [blank] * 6)
-    mine_at, mate_at = STRIPE * core_at, STRIPE * (1 - core_at)
-    fill(mine, own_low + mine_at)
-    fill(mate, own_low + mate_at)
-    fill(part, halo_low + mine_at)
-    fill(part_mate, halo_low + mate_at)
-
-    def bounds(margin):
-        low = jnp.maximum(grid_low, own_low - margin)
-        high = jnp.minimum(grid_high, own_low + HALF + margin)
-        length = (high - low + CHUNK - 1) // CHUNK * CHUNK
-        high = jnp.minimum(width, low + length)
-        return high - length, length // CHUNK
-
-    def lift(flux, source, begin):
+    def lift(flux, source, begin, edge):
         now = load(source, begin)
         before = tails(load(source, begin - 1), now)
         for k, v in zip((1, 2, 4, 5), before):
-            flux[0, k] = jnp.where(begin > grid_low, v, 0.0)
-        for u in range(CHUNK):
+            flux[0, k] = v if edge is None else jnp.where(edge, 0.0, v)
+        for u in range(flux.shape[0] - 1):
             after = load(source, begin + u + 1)
             for k, v in enumerate(curls(now, after)):
                 flux[u + 1, k] = v
@@ -289,69 +249,182 @@
 
     def drop(flux, source, begin, sign, finish):
         before = [flux[0, k] for k in (1, 2, 4, 5)]
-        for u in range(CHUNK):
+        for u in range(flux.shape[0] - 1):
             i = begin + u
             now = [flux[u + 1, k] for k in range(6)]
             value = adjoints(now, before)
             finish(i, add_couple(value, load(source, i), sigma[i + GUARD], sign))
             before = [now[k] for k in (1, 2, 4, 5)]
 
-    def run(margin, flux, source, sign, finish, other_margin, other_flux, other_source):
-        low, count = bounds(margin)
+    return lift, drop
+
+
+def load(ref, at):
+    return [ref[at + GUARD, k] for k in range(6)]
+
+
+def store(ref, at, values):
+    for k in range(6):
+        ref[at + GUARD, k] = values[k]
+
+
+def finishers(terms, field, first, resid, total, place):
+    inv_scale = terms[3, pair_index()]
+    center = chebyshev_terms(SWEEPS - 1)[2]
+
+    def begin_with(i, value):
+        step = [v * (inv_scale * (1.0 / center)) for v in value]
+        store(resid, place(i), value)
+        store(field, place(i), step)
+        store(total, place(i), step)
+
+    def keep_first(i, value):
+        store(first, place(i), value)
+
+    def update(carry_term, push_term):
+        push_term = push_term * inv_scale
+
+        def do(i, value):
+            rest = [r - v for r, v in zip(load(resid, i), value)]
+            step = [carry_term * d + push_term * r for d, r in zip(load(field, i), rest)]
+            store(resid, place(i), rest)
+            store(field, place(i), step)
+            store(total, place(i), [x + d for x, d in zip(load(total, i), step)])
+
+        return do
+
+    return begin_with, keep_first, update
+
+
+def fill(first, sigma, source, begin):
+    ny, nz = sigma.shape[1:]
+    cols = 7
+    for at in range(source.shape[0] // (cols * ny)):
+        i = begin + (at // STRIPE) * (2 * STRIPE) + at % STRIPE
+        parts = [source[pl.ds(at * cols * ny + k, ny, stride=cols), :] for k in range(cols)]
+        store(first, i, parts[:6])
+        sigma[i + GUARD] = parts[6]
+
+
+def inner_kernel(terms, weights, mine, mate, field, first, resid, total, sigma, flux_a, flux_b):
+    ny, nz = sigma.shape[1:]
+    blank = jnp.zeros((ny, nz), jnp.float32)
+    half_at, core_at = lax.axis_index("xh"), lax.axis_index("c")
+    lift, drop = operator(terms, sigma)
+    size = flux_a.shape[0] - 1
+
+    for ref in (first, field):
+        store(ref, -1, [blank] * 6)
+        store(ref, HALF, [blank] * 6)
+    fill(first, sigma, mine, STRIPE * core_at)
+    fill(first, sigma, mate, STRIPE * (1 - core_at))
+
+    def begin_of(level):
+        count = (HALF - level + size - 1) // size
+        return half_at * (HALF - count * size), count
+
+    def run(level, flux, source, sign, finish, other_flux, other_source, beside):
+        low, count = begin_of(level)
+        other_low, _ = begin_of(level + 1)
+
+        def at_edge(begin):
+            return (begin == 0) & (half_at == 0)
 
         def step(t, _):
-            begin = low + t * CHUNK
+            begin = low + t * size
             drop(flux, source, begin, sign, finish)
-            lift(flux, source, begin + CHUNK)
+            lift(flux, source, begin + size, None)
             return 0
 
         lax.fori_loop(0, count - 1, step, 0)
-        lift(other_flux, other_source, bounds(other_margin)[0])
-        drop(flux, source, low + (count - 1) * CHUNK, sign, finish)
-
-    def begin_with(i, value):
-        store(resid, i, value)
-        store(field, i, [v * (inv_scale * (1.0 / center)) for v in value])
-
-    reach = 2 * (SWEEPS - 1)
-    lift(flux_b, first, bounds(reach)[0])
-    run(reach, flux_b, first, -1.0, begin_with, reach - 1, flux_a, field)
-
-    own_planes = [(at // STRIPE) * (2 * STRIPE) + at % STRIPE for at in range(HALF // 2)]
-    own_begin = own_low + mine_at
+        if beside:
+            lift(other_flux, other_source, other_low, at_edge(other_low))
+        drop(flux, source, low + (count - 1) * size, sign, finish)
+        if not beside:
+            lift(other_flux, other_source, other_low, at_edge(other_low))
+
+    def placed(level):
+        low, high = half_at * level, HALF - level + half_at * level
+        return lambda i: jnp.where((i >= low) & (i < high), i, HALF + 1)
+
+    begin_with, _, _ = finishers(terms, field, first, resid, total, placed(1))
+    lift(flux_b, first, begin_of(1)[0], half_at == 0)
+    run(1, flux_b, first, -1.0, begin_with, flux_a, field, True)
+
+    def sweep(s, beside):
+        _, keep_first, _ = finishers(terms, field, first, resid, total, placed(2 + 2 * s))
+        _, _, update = finishers(terms, field, first, resid, total, placed(3 + 2 * s))
+        run(2 + 2 * s, flux_a, field, 1.0, keep_first, flux_b, first, beside)
+        run(
+            3 + 2 * s,
+            flux_b,
+            first,
+            -1.0,
+            update(weights[0, s], weights[1, s]),
+            flux_a,
+            field,
+            beside,
+        )
+
+    def early(s, _):
+        sweep(s, True)
+        return 0
+
+    def late(s, _):
+        sweep(s, False)
+        return 0
+
+    apart = max(s for s in range(SWEEPS) if (HALF - 4 - 2 * s + size - 1) // size >= 3) + 1
+    lax.fori_loop(0, apart, early, 0)
+    lax.fori_loop(apart, SWEEPS - 1, late, 0)
+
+
+def outer_kernel(
+    terms, weights, part, part_mate, *refs
+):
+    given, out, state, (flux_a, flux_b) = refs[:5], refs[5], refs[6:11], refs[11:]
+    field, first, resid, total, sigma = state
+    ny, nz = sigma.shape[1:]
+    half_at, core_at = lax.axis_index("xh"), lax.axis_index("c")
+    lift, drop = operator(terms, sigma)
+    size = flux_a.shape[0] - 1
+
+    own_low = REACH * half_at
+    for ref, old in zip(state[:4], given[:4]):
+        for i in range(HALF):
+            store(ref, own_low + i, load(old, i))
+    for i in range(HALF):
+        sigma[own_low + i + GUARD] = given[4][i + GUARD]
+    halo_low = HALF * (1 - half_at)
+    fill(first, sigma, part, halo_low + STRIPE * core_at)
+    fill(first, sigma, part_mate, halo_low + STRIPE * (1 - core_at))
+
+    def begin_of(level, turn):
+        low = jnp.where(half_at == 0, HALF - level, level)
+        return low + jnp.where(half_at == 0, turn, 1 - turn) * size
+
+    def run(level, source, sign, finish, other_source):
+        lift(flux_b, source, begin_of(level, 1), None)
+        drop(flux_a, source, begin_of(level, 0), sign, finish)
+        lift(flux_a, other_source, begin_of(level + 1, 0), None)
+        drop(flux_b, source, begin_of(level, 1), sign, finish)
+
+    begin_with, keep_first, update = finishers(terms, field, first, resid, total, lambda i: i)
+    lift(flux_a, first, begin_of(1, 0), None)
+    run(1, first, -1.0, begin_with, field)
 
     def sweep(s, _):
-        margin = reach - 2 - 2 * s
-        carry_term, push_term = weights[0, s], weights[1, s] * inv_scale
-
-        for at, h in enumerate(own_planes):
-            for k in range(6):
-                step = field[own_begin + h + GUARD, k]
-                total[at, k] = jnp.where(s == 0, step, total[at, k] + step)
-
-        def keep_first(i, value):
-            store(first, i, value)
-
-        def update(i, value):
-            rest = [r - v for r, v in zip(load(resid, i), value)]
-            store(resid, i, rest)
-            store(
-                field,
-                i,
-                [carry_term * d + push_term * r for d, r in zip(load(field, i), rest)],
-            )
-
-        run(margin + 1, flux_a, field, 1.0, keep_first, margin, flux_b, first)
-        run(margin, flux_b, first, -1.0, update, jnp.maximum(margin - 1, 0), flux_a, field)
+        run(2 + 2 * s, field, 1.0, keep_first, first)
+        run(3 + 2 * s, first, -1.0, update(weights[0, s], weights[1, s]), field)
         return 0
 
     lax.fori_loop(0, SWEEPS - 1, sweep, 0)
 
-    for at, h in enumerate(own_planes):
-        for k in range(6):
-            out[pl.ds(at * 6 * ny + k, ny, stride=6), :] = (
-                total[at, k] + field[own_begin + h + GUARD, k]
-            )
+    own_begin = own_low + STRIPE * core_at
+    for at in range(HALF // 2):
+        i = own_begin + (at // STRIPE) * (2 * STRIPE) + at % STRIPE
+        for k, v in enumerate(load(total, i)):
+            out[pl.ds(at * 6 * ny + k, ny, stride=6), :] = v
 
 
 def per_device(forcing, start_field, iterate, region, conductance):
@@ -363,7 +436,7 @@
     vmem = pl.BlockSpec(memory_space=pltpu.VMEM)
     smem = pl.BlockSpec(memory_space=pltpu.SMEM)
     f32 = jnp.float32
-    params = pltpu.CompilerParams(vmem_limit_bytes=12 * 1024 * 1024)
+    params = pltpu.CompilerParams(vmem_limit_bytes=14 * 1024 * 1024)
 
     rows = comps * steps + 8
     plane_of = pl.BlockSpec((steps, comps, 1, ny, nz), lambda p: (0, 0, p, 0, 0))
@@ -403,38 +476,46 @@
         mine, (1 - lax.axis_index("xh")) * (half - rows_sent), rows_sent, 0
     ).reshape(rows_sent * (2 * comps + 1), nz)
     mine = mine.reshape(half * (2 * comps + 1), nz)
-    blocks = lax.axis_size(("xh", "xl"))
-    part = lax.ppermute(part, ("xh", "xl"), [(i, blocks - 1 - i) for i in range(blocks)])
+    blocks, cores = lax.axis_size(("xh", "xl")), lax.axis_size("c")
+    chips = [(i, blocks - 1 - i) for i in range(blocks)]
+    across = [
+        (i * cores + c, j * cores + cores - 1 - c) for i, j in chips for c in range(cores)
+    ]
+    part_mate = lax.ppermute(part, ("xh", "xl", "c"), across)
+    part = lax.ppermute(part, ("xh", "xl"), chips)
     mate = lax.ppermute(mine, "c", [(0, 1), (1, 0)])
-    part_mate = lax.ppermute(part, "c", [(0, 1), (1, 0)])
-
-    places = HALF + REACH + 2 * GUARD
-    window_shape = pltpu.VMEM((places, 2 * comps, ny, nz), f32)
-    flux_shape = pltpu.VMEM((CHUNK + 1, 2 * comps, ny, nz), f32)
+
+    terms = jnp.asarray(pair_table(window))
+    weights = jnp.asarray(np.array(chebyshev_terms(SWEEPS - 1)[:2], np.float32))
+
+    def state(places):
+        return [(places, 2 * comps, ny, nz)] * 4 + [(places, ny, nz)]
+
+    def flux(planes):
+        return pltpu.VMEM((planes + 1, 2 * comps, ny, nz), f32)
+
+    inner = pl.pallas_call(
+        inner_kernel,
+        out_shape=[jax.ShapeDtypeStruct(shape, f32) for shape in state(HALF + 3 * GUARD)],
+        in_specs=[smem, smem, vmem, vmem],
+        out_specs=[vmem] * 5,
+        scratch_shapes=[flux(INNER)] * 2,
+        compiler_params=params,
+        cost_estimate=pl.CostEstimate(
+            flops=10**10, bytes_accessed=2 * 10**7, transcendentals=0
+        ),
+        name="inner",
+    )(terms, weights, mine, mate)
     solved = pl.pallas_call(
-        solve_kernel,
+        outer_kernel,
         out_shape=jax.ShapeDtypeStruct((half * 2 * comps, nz), f32),
-        in_specs=[smem, smem, vmem, vmem, vmem, vmem],
+        in_specs=[smem, smem] + [vmem] * 7,
         out_specs=vmem,
-        scratch_shapes=[
-            window_shape,
-            window_shape,
-            window_shape,
-            pltpu.VMEM((HALF // 2, 2 * comps, ny, nz), f32),
-            pltpu.VMEM((places, ny, nz), f32),
-            flux_shape,
-            flux_shape,
-        ],
+        scratch_shapes=[pltpu.VMEM(shape, f32) for shape in state(HALF + REACH + 2 * GUARD)]
+        + [flux(OUTER)] * 2,
         compiler_params=params,
-        name="solve",
-    )(
-        jnp.asarray(pair_table(window)),
-        jnp.asarray(np.array(chebyshev_terms(SWEEPS - 1)[:2], np.float32)),
-        mine,
-        mate,
-        part,
-        part_mate,
-    )
+        name="outer",
+    )(terms, weights, part, part_mate, *inner)
 
     back = lax.all_to_all(
         solved.reshape(half, 1, 2 * comps * nz), GROUP, 0, 0, tiled=True

time: 147 us -> 145 us (0.986)
  blocking collectives: 80.6 us -> 106 us
  waiting for transfers between devices: 24.4 us -> 1.14 us
  starting transfers between devices: 16.8 us -> 8.78 us
  Pallas kernels: 24.3 us -> 28.7 us
    all_to_all x0 -> x1, blocking collectives: none -> 26.2 us  [per_device(): lax.all_to_all(spectrum.reshape(half, 1, (2 * comps + 1) * nz), GROUP, 0,...]
    all_to_all x1 -> x0, waiting for transfers between devices: 18.2 us -> none  [per_device(): lax.all_to_all(spectrum.reshape(half, 1, (2 * comps + 1) * nz), GROUP, 0,...]
    all_to_all x1 -> x0, starting transfers between devices: 8.18 us -> none  [per_device(): lax.all_to_all(spectrum.reshape(half, 1, (2 * comps + 1) * nz), GROUP, 0,...]
    pallas_call x1 -> x2, Pallas kernels: 19 us -> 24.1 us  [the longest x1 12.5 us: per_device(): pl.pallas_call(inner_kernel, out_shape=[jax.ShapeDtypeStruct(shape, f32)...]
    ppermute x2, waiting for transfers between devices: 6.23 us -> 1.14 us  [the longest x1 1.13 us: per_device(): part_mate = lax.ppermute(part, ('xh', 'xl', 'c'), across)]
  transfers between devices with their start and end apart: 4 -> 3, of which waited for: 3 -> 1; matrix products, arithmetic and copies ran while one was open for 0% -> 0% of each run, Pallas kernels for 0% -> 9%
where the time goes in v6:
time: 145 us
  blocking collectives  106 us (73%)
  Pallas kernels  28.7 us (20%)
  starting transfers between devices  8.78 us (6%)
    all_to_all x1, blocking collectives, per_device(): got = lax.all_to_all(packed.reshape(groups, rows, nz), TM, 0, 0, tiled=True)  34.2 us
    all_to_all x1, blocking collectives, per_device(): lax.all_to_all(spectrum.reshape(half, 1, (2 * comps + 1) * nz), GROUP, 0,...  26.2 us
    all_to_all x1, blocking collectives, per_device(): lax.all_to_all(solved.reshape(half, 1, 2 * comps * nz), GROUP, 0, 0, tile...  23.9 us
    all_to_all x1, blocking collectives, per_device(): home = lax.all_to_all(pencil, TM, 0, 0, tiled=True)  21.5 us
    pallas_call x1, Pallas kernels, per_device(): pl.pallas_call(inner_kernel, out_shape=[jax.ShapeDtypeStruct(shape, f32)...  12.5 us
    pallas_call x1, Pallas kernels, per_device(): pl.pallas_call(outer_kernel, out_shape=jax.ShapeDtypeStruct((half * 2 * c...  11.6 us
    ppermute x1, starting transfers between devices, per_device(): part = lax.ppermute(part, ('xh', 'xl'), chips)  4.82 us
  transfers between devices with their start and end apart: 3, of which 1 were waited for; matrix products, arithmetic and copies ran while one was open for 0% of the time, Pallas kernels for 9%

profile of v6, /device:TPU:8, one launch (start us, length us, event | category | flops | bytes accessed | tf_op | source)
XLA Modules:
  0.0 144.6 jit_solution(7618998832359934169)
XLA Ops:
  0.0 1.8 %pack.1 = f32[896,128]{1,0:T(8,128)} custom-call(f32[3]{0:T(128)} %cond.3, f32[16,3,2,8,128]{4,3,2,1,0:T(8,128)} %forcing.1, f32[3,2,8,128]{3,2,1,0:T(8,128)} %start.1, f32[16,3,2,8,128]{4,3,2,1,0:T(8,128)} %latest.1, s32[2,8,128]{2,1,0:T(8,128)} %region.3), custom_call_target="tpu_custom_call" | custom-call | tf_op jit(solution)/shard_map/pack/pallas_call | solution.py:443
  1.8 0.0 copy-start
  1.8 0.0 copy-start.1
  1.8 0.0 copy-start.3
  1.9 34.2 %all_to_all.20.got = f32[16,56,128]{2,1,0:T(8,128)S(1)} all-to-all(f32[16,56,128]{2,1,0:T(8,128)} %bitcast.13), channel_id=1, replica_groups=mesh['yh'=2,'z'=8,'xh'=2,'xl'=2,'yl'=4,'c'=2] {'yh','z'}, dimensions={0} | all-to-all | bytes 917504 | tf_op jit(solution)/shard_map/all_to_all | solution.py:459
  36.1 0.0 copy-done
  36.1 0.0 copy-done.1
  36.1 0.0 copy-done.3
  36.1 1.1 forward.1
  37.2 26.2 %all_to_all.21 = f32[128,1,896]{2,1,0:T(1,128)S(1)} all-to-all(f32[128,1,896]{2,1,0:T(1,128)S(1)} %bitcast.7), channel_id=1, replica_groups=mesh['yh'=2,'z'=8,'xh'=2,'xl'=2,'yl'=4,'c'=2] {'xl','yl','yh','z'}, dimensions={0} | all-to-all | bytes 917504 | tf_op jit(solution)/shard_map/all_to_all | solution.py:470
  63.4 1.9 %collective-permute-start.2 = (f32[896,128]{1,0:T(8,128)S(1)}, f32[896,128]{1,0:T(8,128)S(1)}, u32[]{:S(2)}, u32[]{:S(2)}) collective-permute-start(f32[896,128]{1,0:T(8,128)S(1)} %bitcast.11), channel_id=1, source_target_pairs={{0,1},{1,0},{2,3},{3,2},{4,5},{5,4},{6,7},{7,6},{8,9},{9,8},{10,11... | collective-permute-start | bytes 1376264 | tf_op jit(solution)/shard_map/ppermute | solution.py:486
  65.3 0.0 copy-start.2
  65.3 0.1 constant_dynamic-slice_fusion
  65.5 0.0 copy-start.4
  65.5 4.8 %collective-permute-start = (f32[672,128]{1,0:T(8,128)S(1)}, f32[672,128]{1,0:T(8,128)S(1)}, u32[]{:S(2)}, u32[]{:S(2)}) collective-permute-start(f32[672,128]{1,0:T(8,128)S(1)} %bitcast.14), channel_id=1, source_target_pairs={{0,24},{8,16},{16,8},{24,0},{1,25},{9,17},{17,9},{25,1},{2,26},{10... | collective-permute-start | bytes 1032200 | tf_op jit(solution)/shard_map/ppermute | solution.py:485
  70.3 2.1 %collective-permute-start.1 = (f32[672,128]{1,0:T(8,128)S(1)}, f32[672,128]{1,0:T(8,128)S(1)}, u32[]{:S(2)}, u32[]{:S(2)}) collective-permute-start(f32[672,128]{1,0:T(8,128)S(1)} %bitcast.15), channel_id=1, source_target_pairs={{0,25},{1,24},{8,17},{9,16},{16,9},{17,8},{24,1},{25,0},{2,27},{3,... | collective-permute-start | bytes 1032200 | tf_op jit(solution)/shard_map/ppermute | solution.py:484
  72.4 0.0 collective-permute-done.2.mate
  72.4 0.0 copy-done.2
  72.4 0.0 copy-done.4
  72.4 12.5 %inner.1 = (f32[35,6,8,128]{3,2,1,0:T(8,128)S(1)}, f32[35,6,8,128]{3,2,1,0:T(8,128)S(1)}, f32[35,6,8,128]{3,2,1,0:T(8,128)S(1)}, f32[35,6,8,128]{3,2,1,0:T(8,128)S(1)}, f32[35,8,128]{2,1,0:T(8,128)S(1)}) custom-call(f32[4,128]{1,0:T(4,128)S(1)} %copy-done.2, f32[2,11]{1,0:T(2,128)S(1)} %copy-done.4, f32[896,128]{1,0:T(8,128)S(1)} %bitcast.12, ...), custom_call_target="tpu_custom_call" | custom-call | flops 10000000000 | bytes 20000000 | tf_op jit(solution)/shard_map/inner/pallas_call | solution.py:497
  84.9 0.0 collective-permute-done.part
  84.9 1.1 collective-permute-done.1.part_mate
  86.0 11.6 %outer.1 = f32[768,128]{1,0:T(8,128)S(1)} custom-call(f32[4,128]{1,0:T(4,128)S(1)} %copy-done.2, f32[2,11]{1,0:T(2,128)S(1)} %copy-done.4, f32[672,128]{1,0:T(8,128)S(1)} %collective-permute-done.part, f32[672,128]{1,0:T(8,128)S(1)} %collective-permute-done.1.part_mate, f32[35,6,8,128]{3,2,1,0:T(8,128)S(1)} %get-tuple-element.10.refs_0_, ...), custom_call_target="tpu_custom_call" | custom-call | tf_op jit(solution)/shard_map/outer/pallas_call | solution.py:509
  97.6 23.9 %all_to_all.22 = f32[128,1,768]{2,1,0:T(1,128)S(1)} all-to-all(f32[128,1,768]{2,1,0:T(1,128)S(1)} %bitcast.10), channel_id=1, replica_groups=mesh['yh'=2,'z'=8,'xh'=2,'xl'=2,'yl'=4,'c'=2] {'xl','yl','yh','z'}, dimensions={0} | all-to-all | bytes 786432 | tf_op jit(solution)/shard_map/all_to_all | solution.py:520
  121.5 0.8 inverse.1
  122.3 21.5 %all_to_all.23 = f32[16,48,128]{2,1,0:T(8,128)S(1)} all-to-all(f32[16,48,128]{2,1,0:T(8,128)S(1)} %inverse.1), channel_id=1, replica_groups=mesh['yh'=2,'z'=8,'xh'=2,'xl'=2,'yl'=4,'c'=2] {'yh','z'}, dimensions={0} | all-to-all | bytes 786432 | tf_op jit(solution)/shard_map/all_to_all | solution.py:533
  143.8 0.8 unpack.1
Async XLA Ops:
  1.8 34.3 %copy-start = (f32[2,256,256]{2,1,0:T(8,128)S(1)}, f32[2,256,256]{2,1,0:T(8,128)}, u32[]{:S(2)}) copy-start(f32[2,256,256]{2,1,0:T(8,128)} %constant.20.clone.tables) | copy-start | bytes 1572868
  1.8 34.3 %copy-start.1 = (s32[2,8,128]{2,1,0:T(8,128)S(1)}, s32[2,8,128]{2,1,0:T(8,128)}, u32[]{:S(2)}) copy-start(s32[2,8,128]{2,1,0:T(8,128)} %region.3) | copy-start | bytes 24580
  1.8 34.3 %copy-start.3 = (f32[3]{0:T(128)S(1)}, f32[3]{0:T(128)}, u32[]{:S(2)}) copy-start(f32[3]{0:T(128)} %cond.3) | copy-start | bytes 40
  63.4 9.0 %collective-permute-start.2 = (f32[896,128]{1,0:T(8,128)S(1)}, f32[896,128]{1,0:T(8,128)S(1)}, u32[]{:S(2)}, u32[]{:S(2)}) collective-permute-start(f32[896,128]{1,0:T(8,128)S(1)} %bitcast.11), channel_id=1, source_target_pairs={{0,1},{1,0},{2,3},{3,2},{4,5},{5,4},{6,7},{7,6},{8,9},{9,8},{10,11... | collective-permute-start | bytes 1376264 | tf_op jit(solution)/shard_map/ppermute | solution.py:486
  65.3 7.0 %copy-start.2 = (f32[4,128]{1,0:T(4,128)S(1)}, f32[4,128]{1,0:T(4,128)}, u32[]{:S(2)}) copy-start(f32[4,128]{1,0:T(4,128)} %constant.21.clone.terms) | copy-start | bytes 6148
  65.5 6.9 %copy-start.4 = (f32[2,11]{1,0:T(2,128)S(1)}, f32[2,11]{1,0:T(2,128)}, u32[]{:S(2)}) copy-start(f32[2,11]{1,0:T(2,128)} %constant.22.clone.weights) | copy-start | bytes 268
  65.5 19.4 %collective-permute-start = (f32[672,128]{1,0:T(8,128)S(1)}, f32[672,128]{1,0:T(8,128)S(1)}, u32[]{:S(2)}, u32[]{:S(2)}) collective-permute-start(f32[672,128]{1,0:T(8,128)S(1)} %bitcast.14), channel_id=1, source_target_pairs={{0,24},{8,16},{16,8},{24,0},{1,25},{9,17},{17,9},{25,1},{2,26},{10... | collective-permute-start | bytes 1032200 | tf_op jit(solution)/shard_map/ppermute | solution.py:485
  70.3 15.7 %collective-permute-start.1 = (f32[672,128]{1,0:T(8,128)S(1)}, f32[672,128]{1,0:T(8,128)S(1)}, u32[]{:S(2)}, u32[]{:S(2)}) collective-permute-start(f32[672,128]{1,0:T(8,128)S(1)} %bitcast.15), channel_id=1, source_target_pairs={{0,25},{1,24},{8,17},{9,16},{16,9},{17,8},{24,1},{25,0},{2,27},{3,... | collective-permute-start | bytes 1032200 | tf_op jit(solution)/shard_map/ppermute | solution.py:484

commit v7 on v6

--- a/solution.py
+++ b/solution.py
@@ -1,4 +1,3 @@
-import functools
 import math
 
 import jax
@@ -46,6 +45,19 @@
     forward = cas * gamma ** moments[None, :]
     inverse = cas.T * gamma ** (-moments[:, None]) / window
     return forward.astype(np.float32), inverse.astype(np.float32)
+
+
+def product(table, values):
+    def parts(array):
+        high = array.astype(jnp.bfloat16)
+        return high, (array - high.astype(jnp.float32)).astype(jnp.bfloat16)
+
+    (table_high, table_low), (high, low) = parts(table), parts(values)
+    return jnp.dot(
+        jnp.concatenate([table_high, table_low, table_high], axis=1),
+        jnp.concatenate([high, high, low], axis=0),
+        preferred_element_type=jnp.float32,
+    )
 
 
 def pair_table(window):
@@ -110,12 +122,7 @@
         part = got[:, c * steps : (c + 1) * steps, :].reshape(window, nz)
         row = got[groups - 1, comps * steps + c : comps * steps + c + 1, :]
         parts.append(part + jnp.where(head, row, 0.0))
-    spectrum = jnp.dot(
-        tables[0],
-        jnp.concatenate(parts, axis=1),
-        precision=lax.Precision.HIGHEST,
-        preferred_element_type=jnp.float32,
-    )
+    spectrum = product(tables[0], jnp.concatenate(parts, axis=1))
     width = comps * nz
     flip = lax.axis_index("xh")
     line = region[lax.axis_index("yh"), pl.ds(lax.axis_index("z"), 1), :]
@@ -139,9 +146,6 @@
     half = window // 2
     steps = window // groups
     cols = got.shape[0] // half
-    dot = functools.partial(
-        jnp.dot, precision=lax.Precision.HIGHEST, preferred_element_type=jnp.float32
-    )
     flip = lax.axis_index("xh")
     size = half // 2
 
@@ -157,8 +161,7 @@
             axis=1,
         )
 
-    table = tables.at[1]
-    result = dot(table[:, :half], member(0)) + dot(table[:, half:], member(1))
+    result = product(tables[1], jnp.concatenate([member(0), member(1)], axis=0))
     for c in range(rows // steps):
         out[:, c * steps : (c + 1) * steps, :] = result[:, c * nz : (c + 1) * nz].reshape(
             groups, steps, nz
@@ -404,8 +407,8 @@
         return low + jnp.where(half_at == 0, turn, 1 - turn) * size
 
     def run(level, source, sign, finish, other_source):
+        drop(flux_a, source, begin_of(level, 0), sign, finish)
         lift(flux_b, source, begin_of(level, 1), None)
-        drop(flux_a, source, begin_of(level, 0), sign, finish)
         lift(flux_a, other_source, begin_of(level + 1, 0), None)
         drop(flux_b, source, begin_of(level, 1), sign, finish)
 

time: 145 us -> 143 us (0.986)
  Pallas kernels: 28.7 us -> 26.6 us
where the time goes in v7:
time: 143 us
  blocking collectives  106 us (74%)
  Pallas kernels  26.6 us (19%)
  starting transfers between devices  8.78 us (6%)
    all_to_all x1, blocking collectives, per_device(): got = lax.all_to_all(packed.reshape(groups, rows, nz), TM, 0, 0, tiled=True)  34.2 us
    all_to_all x1, blocking collectives, per_device(): lax.all_to_all(spectrum.reshape(half, 1, (2 * comps + 1) * nz), GROUP, 0,...  26.2 us
    all_to_all x1, blocking collectives, per_device(): lax.all_to_all(solved.reshape(half, 1, 2 * comps * nz), GROUP, 0, 0, tile...  23.9 us
    all_to_all x1, blocking collectives, per_device(): home = lax.all_to_all(pencil, TM, 0, 0, tiled=True)  21.5 us
    pallas_call x1, Pallas kernels, per_device(): pl.pallas_call(inner_kernel, out_shape=[jax.ShapeDtypeStruct(shape, f32)...  12.5 us
    pallas_call x1, Pallas kernels, per_device(): pl.pallas_call(outer_kernel, out_shape=jax.ShapeDtypeStruct((half * 2 * c...  10.2 us
    ppermute x1, starting transfers between devices, per_device(): part = lax.ppermute(part, ('xh', 'xl'), chips)  4.82 us
  transfers between devices with their start and end apart: 3, of which 1 were waited for; matrix products, arithmetic and copies ran while one was open for 0% of the time, Pallas kernels for 9%

profile of v7, /device:TPU:8, one launch (start us, length us, event | category | flops | bytes accessed | tf_op | source)
XLA Modules:
  0.0 142.5 jit_solution(17888024800256377178)
XLA Ops:
  0.0 1.8 %pack.1 = f32[896,128]{1,0:T(8,128)} custom-call(f32[3]{0:T(128)} %cond.3, f32[16,3,2,8,128]{4,3,2,1,0:T(8,128)} %forcing.1, f32[3,2,8,128]{3,2,1,0:T(8,128)} %start.1, f32[16,3,2,8,128]{4,3,2,1,0:T(8,128)} %latest.1, s32[2,8,128]{2,1,0:T(8,128)} %region.3), custom_call_target="tpu_custom_call" | custom-call | tf_op jit(solution)/shard_map/pack/pallas_call | solution.py:446
  1.8 0.0 copy-start
  1.8 0.0 copy-start.1
  1.8 0.0 copy-start.3
  1.9 34.2 %all_to_all.20.got = f32[16,56,128]{2,1,0:T(8,128)S(1)} all-to-all(f32[16,56,128]{2,1,0:T(8,128)} %bitcast.13), channel_id=1, replica_groups=mesh['yh'=2,'z'=8,'xh'=2,'xl'=2,'yl'=4,'c'=2] {'yh','z'}, dimensions={0} | all-to-all | bytes 917504 | tf_op jit(solution)/shard_map/all_to_all | solution.py:462
  36.1 0.0 copy-done
  36.1 0.0 copy-done.1
  36.1 0.0 copy-done.3
  36.1 0.9 forward.1
  37.0 26.2 %all_to_all.21 = f32[128,1,896]{2,1,0:T(1,128)S(1)} all-to-all(f32[128,1,896]{2,1,0:T(1,128)S(1)} %bitcast.7), channel_id=1, replica_groups=mesh['yh'=2,'z'=8,'xh'=2,'xl'=2,'yl'=4,'c'=2] {'xl','yl','yh','z'}, dimensions={0} | all-to-all | bytes 917504 | tf_op jit(solution)/shard_map/all_to_all | solution.py:473
  63.2 1.9 %collective-permute-start.2 = (f32[896,128]{1,0:T(8,128)S(1)}, f32[896,128]{1,0:T(8,128)S(1)}, u32[]{:S(2)}, u32[]{:S(2)}) collective-permute-start(f32[896,128]{1,0:T(8,128)S(1)} %bitcast.11), channel_id=1, source_target_pairs={{0,1},{1,0},{2,3},{3,2},{4,5},{5,4},{6,7},{7,6},{8,9},{9,8},{10,11... | collective-permute-start | bytes 1376264 | tf_op jit(solution)/shard_map/ppermute | solution.py:489
  65.1 0.0 copy-start.2
  65.1 0.1 constant_dynamic-slice_fusion
  65.2 0.0 copy-start.4
  65.2 4.8 %collective-permute-start = (f32[672,128]{1,0:T(8,128)S(1)}, f32[672,128]{1,0:T(8,128)S(1)}, u32[]{:S(2)}, u32[]{:S(2)}) collective-permute-start(f32[672,128]{1,0:T(8,128)S(1)} %bitcast.14), channel_id=1, source_target_pairs={{0,24},{8,16},{16,8},{24,0},{1,25},{9,17},{17,9},{25,1},{2,26},{10... | collective-permute-start | bytes 1032200 | tf_op jit(solution)/shard_map/ppermute | solution.py:488
  70.1 2.1 %collective-permute-start.1 = (f32[672,128]{1,0:T(8,128)S(1)}, f32[672,128]{1,0:T(8,128)S(1)}, u32[]{:S(2)}, u32[]{:S(2)}) collective-permute-start(f32[672,128]{1,0:T(8,128)S(1)} %bitcast.15), channel_id=1, source_target_pairs={{0,25},{1,24},{8,17},{9,16},{16,9},{17,8},{24,1},{25,0},{2,27},{3,... | collective-permute-start | bytes 1032200 | tf_op jit(solution)/shard_map/ppermute | solution.py:487
  72.1 0.0 collective-permute-done.2.mate
  72.1 0.0 copy-done.2
  72.1 0.0 copy-done.4
  72.2 12.5 %inner.1 = (f32[35,6,8,128]{3,2,1,0:T(8,128)S(1)}, f32[35,6,8,128]{3,2,1,0:T(8,128)S(1)}, f32[35,6,8,128]{3,2,1,0:T(8,128)S(1)}, f32[35,6,8,128]{3,2,1,0:T(8,128)S(1)}, f32[35,8,128]{2,1,0:T(8,128)S(1)}) custom-call(f32[4,128]{1,0:T(4,128)S(1)} %copy-done.2, f32[2,11]{1,0:T(2,128)S(1)} %copy-done.4, f32[896,128]{1,0:T(8,128)S(1)} %bitcast.12, ...), custom_call_target="tpu_custom_call" | custom-call | flops 10000000000 | bytes 20000000 | tf_op jit(solution)/shard_map/inner/pallas_call | solution.py:500
  84.6 0.0 collective-permute-done.part
  84.6 1.1 collective-permute-done.1.part_mate
  85.8 10.2 %outer.1 = f32[768,128]{1,0:T(8,128)S(1)} custom-call(f32[4,128]{1,0:T(4,128)S(1)} %copy-done.2, f32[2,11]{1,0:T(2,128)S(1)} %copy-done.4, f32[672,128]{1,0:T(8,128)S(1)} %collective-permute-done.part, f32[672,128]{1,0:T(8,128)S(1)} %collective-permute-done.1.part_mate, f32[35,6,8,128]{3,2,1,0:T(8,128)S(1)} %get-tuple-element.10.refs_0_, ...), custom_call_target="tpu_custom_call" | custom-call | tf_op jit(solution)/shard_map/outer/pallas_call | solution.py:512
  96.0 23.9 %all_to_all.22 = f32[128,1,768]{2,1,0:T(1,128)S(1)} all-to-all(f32[128,1,768]{2,1,0:T(1,128)S(1)} %bitcast.10), channel_id=1, replica_groups=mesh['yh'=2,'z'=8,'xh'=2,'xl'=2,'yl'=4,'c'=2] {'xl','yl','yh','z'}, dimensions={0} | all-to-all | bytes 786432 | tf_op jit(solution)/shard_map/all_to_all | solution.py:523
  119.9 0.4 inverse.1
  120.2 21.5 %all_to_all.23 = f32[16,48,128]{2,1,0:T(8,128)S(1)} all-to-all(f32[16,48,128]{2,1,0:T(8,128)S(1)} %inverse.1), channel_id=1, replica_groups=mesh['yh'=2,'z'=8,'xh'=2,'xl'=2,'yl'=4,'c'=2] {'yh','z'}, dimensions={0} | all-to-all | bytes 786432 | tf_op jit(solution)/shard_map/all_to_all | solution.py:536
  141.7 0.8 unpack.1
Async XLA Ops:
  1.8 34.3 %copy-start = (f32[2,256,256]{2,1,0:T(8,128)S(1)}, f32[2,256,256]{2,1,0:T(8,128)}, u32[]{:S(2)}) copy-start(f32[2,256,256]{2,1,0:T(8,128)} %constant.20.clone.tables) | copy-start | bytes 1572868
  1.8 34.3 %copy-start.1 = (s32[2,8,128]{2,1,0:T(8,128)S(1)}, s32[2,8,128]{2,1,0:T(8,128)}, u32[]{:S(2)}) copy-start(s32[2,8,128]{2,1,0:T(8,128)} %region.3) | copy-start | bytes 24580
  1.8 34.3 %copy-start.3 = (f32[3]{0:T(128)S(1)}, f32[3]{0:T(128)}, u32[]{:S(2)}) copy-start(f32[3]{0:T(128)} %cond.3) | copy-start | bytes 40
  63.2 9.0 %collective-permute-start.2 = (f32[896,128]{1,0:T(8,128)S(1)}, f32[896,128]{1,0:T(8,128)S(1)}, u32[]{:S(2)}, u32[]{:S(2)}) collective-permute-start(f32[896,128]{1,0:T(8,128)S(1)} %bitcast.11), channel_id=1, source_target_pairs={{0,1},{1,0},{2,3},{3,2},{4,5},{5,4},{6,7},{7,6},{8,9},{9,8},{10,11... | collective-permute-start | bytes 1376264 | tf_op jit(solution)/shard_map/ppermute | solution.py:489
  65.1 7.0 %copy-start.2 = (f32[4,128]{1,0:T(4,128)S(1)}, f32[4,128]{1,0:T(4,128)}, u32[]{:S(2)}) copy-start(f32[4,128]{1,0:T(4,128)} %constant.21.clone.terms) | copy-start | bytes 6148
  65.2 6.9 %copy-start.4 = (f32[2,11]{1,0:T(2,128)S(1)}, f32[2,11]{1,0:T(2,128)}, u32[]{:S(2)}) copy-start(f32[2,11]{1,0:T(2,128)} %constant.22.clone.weights) | copy-start | bytes 268
  65.2 19.4 %collective-permute-start = (f32[672,128]{1,0:T(8,128)S(1)}, f32[672,128]{1,0:T(8,128)S(1)}, u32[]{:S(2)}, u32[]{:S(2)}) collective-permute-start(f32[672,128]{1,0:T(8,128)S(1)} %bitcast.14), channel_id=1, source_target_pairs={{0,24},{8,16},{16,8},{24,0},{1,25},{9,17},{17,9},{25,1},{2,26},{10... | collective-permute-start | bytes 1032200 | tf_op jit(solution)/shard_map/ppermute | solution.py:488
  70.1 15.7 %collective-permute-start.1 = (f32[672,128]{1,0:T(8,128)S(1)}, f32[672,128]{1,0:T(8,128)S(1)}, u32[]{:S(2)}, u32[]{:S(2)}) collective-permute-start(f32[672,128]{1,0:T(8,128)S(1)} %bitcast.15), channel_id=1, source_target_pairs={{0,25},{1,24},{8,17},{9,16},{16,9},{17,8},{24,1},{25,0},{2,27},{3,... | collective-permute-start | bytes 1032200 | tf_op jit(solution)/shard_map/ppermute | solution.py:487

commit v8 on v7

--- a/solution.py
+++ b/solution.py
@@ -1,3 +1,4 @@
+import itertools
 import math
 
 import jax
@@ -17,7 +18,7 @@
 CURL_TOP = 12.0
 
 TM = ("yh", "z")
-GROUP = ("xl", "yl", "yh", "z")
+GROUP = ("yl", "yh", "xl", "z")
 HALF = 32
 REACH = 24
 STRIPE = 2
@@ -27,11 +28,18 @@
 
 
 def pair_index():
-    half_at, low_at, *rest = (lax.axis_index(name) for name in ("xh",) + GROUP)
-    index = (half_at + low_at) % 2
-    for name, at in zip(GROUP[1:], rest):
+    index = 0
+    for name in GROUP:
+        at = lax.axis_index(name)
+        if name == "xl":
+            at = (at + lax.axis_index("xh")) % 2
         index = index * lax.axis_size(name) + at
     return index
+
+
+def place_of(block):
+    flip = lax.axis_index("xh")
+    return block + (flip if block % 2 == 0 else -flip)
 
 
 def tables(window):
@@ -124,13 +132,11 @@
         parts.append(part + jnp.where(head, row, 0.0))
     spectrum = product(tables[0], jnp.concatenate(parts, axis=1))
     width = comps * nz
-    flip = lax.axis_index("xh")
     line = region[lax.axis_index("yh"), pl.ds(lax.axis_index("z"), 1), :]
     weight = jnp.broadcast_to(material(line, cond), (8, nz))
     cols = out.shape[0] // half
     for at in range(half // 8):
-        lower = at < half // 16
-        begin = at * 8 + (flip if lower else -flip) * (half // 2)
+        begin = place_of(at) * 8
         for k in range(2 * comps):
             block = spectrum[
                 k // comps * half + at * 8 : k // comps * half + at * 8 + 8,
@@ -146,14 +152,14 @@
     half = window // 2
     steps = window // groups
     cols = got.shape[0] // half
-    flip = lax.axis_index("xh")
-    size = half // 2
-
     def member(f):
         return jnp.concatenate(
             [
                 jnp.concatenate(
-                    [got[pl.ds(at * size * cols + k, size, stride=cols), :] for at in (flip, 1 - flip)],
+                    [
+                        got[pl.ds(place_of(at) * 8 * cols + k, 8, stride=cols), :]
+                        for at in range(half // 8)
+                    ],
                     axis=0,
                 )
                 for k in range(f * cols // 2, (f + 1) * cols // 2)
@@ -299,14 +305,25 @@
     return begin_with, keep_first, update
 
 
-def fill(first, sigma, source, begin):
+def fill(first, sigma, source, rows, begins):
     ny, nz = sigma.shape[1:]
     cols = 7
-    for at in range(source.shape[0] // (cols * ny)):
-        i = begin + (at // STRIPE) * (2 * STRIPE) + at % STRIPE
-        parts = [source[pl.ds(at * cols * ny + k, ny, stride=cols), :] for k in range(cols)]
+    for row, (x_at, y_at, p) in rows:
+        i = begins[x_at] + 2 * STRIPE * y_at + p
+        parts = [source[pl.ds(row * cols * ny + k, ny, stride=cols), :] for k in range(cols)]
         store(first, i, parts[:6])
         sigma[i + GUARD] = parts[6]
+
+
+def brick_rows():
+    order = itertools.product(range(4), range(STRIPE), range(2))
+    return [(row, (x_at, y_at, p)) for row, (y_at, p, x_at) in enumerate(order)]
+
+
+def halo_rows():
+    order = [(0, y_at, p) for y_at in range(4) for p in range(STRIPE)]
+    order += [(1, y_at, p) for y_at in range(2) for p in range(STRIPE)]
+    return list(enumerate(order))
 
 
 def inner_kernel(terms, weights, mine, mate, field, first, resid, total, sigma, flux_a, flux_b):
@@ -319,8 +336,9 @@
     for ref in (first, field):
         store(ref, -1, [blank] * 6)
         store(ref, HALF, [blank] * 6)
-    fill(first, sigma, mine, STRIPE * core_at)
-    fill(first, sigma, mate, STRIPE * (1 - core_at))
+    for source, core in ((mine, core_at), (mate, 1 - core_at)):
+        begin = STRIPE * core
+        fill(first, sigma, source, brick_rows(), (begin, begin + HALF // 2))
 
     def begin_of(level):
         count = (HALF - level + size - 1) // size
@@ -399,8 +417,11 @@
     for i in range(HALF):
         sigma[own_low + i + GUARD] = given[4][i + GUARD]
     halo_low = HALF * (1 - half_at)
-    fill(first, sigma, part, halo_low + STRIPE * core_at)
-    fill(first, sigma, part_mate, halo_low + STRIPE * (1 - core_at))
+    for source, core in ((part, core_at), (part_mate, 1 - core_at)):
+        begin = halo_low + STRIPE * core
+        whole_x = begin + (REACH - HALF // 2) * half_at
+        half_x = begin + HALF // 2 * (1 - half_at)
+        fill(first, sigma, source, halo_rows(), (whole_x, half_x))
 
     def begin_of(level, turn):
         low = jnp.where(half_at == 0, HALF - level, level)
@@ -424,10 +445,10 @@
     lax.fori_loop(0, SWEEPS - 1, sweep, 0)
 
     own_begin = own_low + STRIPE * core_at
-    for at in range(HALF // 2):
-        i = own_begin + (at // STRIPE) * (2 * STRIPE) + at % STRIPE
+    for row, (x_at, y_at, p) in brick_rows():
+        i = own_begin + HALF // 2 * x_at + 2 * STRIPE * y_at + p
         for k, v in enumerate(load(total, i)):
-            out[pl.ds(at * 6 * ny + k, ny, stride=6), :] = v
+            out[pl.ds(row * 6 * ny + k, ny, stride=6), :] = v
 
 
 def per_device(forcing, start_field, iterate, region, conductance):
@@ -474,10 +495,13 @@
         spectrum.reshape(half, 1, (2 * comps + 1) * nz), GROUP, 0, 0, tiled=True
     )
 
-    rows_sent = half * REACH // HALF
-    part = lax.dynamic_slice_in_dim(
-        mine, (1 - lax.axis_index("xh")) * (half - rows_sent), rows_sent, 0
-    ).reshape(rows_sent * (2 * comps + 1), nz)
+    half_at = lax.axis_index("xh")
+    bricks = mine.reshape(4, planes, 2, ny * (2 * comps + 1), nz)
+    near = lax.dynamic_index_in_dim(bricks, 1 - half_at, 2, keepdims=False)
+    beyond = lax.dynamic_slice(
+        bricks, (2 * (1 - half_at), 0, half_at, 0, 0), (2, planes, 1) + bricks.shape[3:]
+    )
+    part = jnp.concatenate([near, beyond[:, :, 0]], axis=0).reshape(-1, nz)
     mine = mine.reshape(half * (2 * comps + 1), nz)
     blocks, cores = lax.axis_size(("xh", "xl")), lax.axis_size("c")
     chips = [(i, blocks - 1 - i) for i in range(blocks)]

time: 143 us -> 141 us (0.986)
  the two profiles are of different devices: /device:TPU:8 before, /device:TPU:16 now
where the time goes in v8:
time: 141 us
  blocking collectives  104 us (74%)
  Pallas kernels  26.6 us (19%)
  starting transfers between devices  9.06 us (6%)
    all_to_all x1, blocking collectives, per_device(): got = lax.all_to_all(packed.reshape(groups, rows, nz), TM, 0, 0, tiled=True)  33.5 us
    all_to_all x1, blocking collectives, per_device(): lax.all_to_all(spectrum.reshape(half, 1, (2 * comps + 1) * nz), GROUP, 0,...  26.9 us
    all_to_all x1, blocking collectives, per_device(): lax.all_to_all(solved.reshape(half, 1, 2 * comps * nz), GROUP, 0, 0, tile...  22.6 us
    all_to_all x1, blocking collectives, per_device(): home = lax.all_to_all(pencil, TM, 0, 0, tiled=True)  20.6 us
    pallas_call x1, Pallas kernels, per_device(): pl.pallas_call(inner_kernel, out_shape=[jax.ShapeDtypeStruct(shape, f32)...  12.5 us
    pallas_call x1, Pallas kernels, per_device(): pl.pallas_call(outer_kernel, out_shape=jax.ShapeDtypeStruct((half * 2 * c...  10.2 us
    ppermute x1, starting transfers between devices, per_device(): part = lax.ppermute(part, ('xh', 'xl'), chips)  4.22 us
    ppermute x1, starting transfers between devices, per_device(): part_mate = lax.ppermute(part, ('xh', 'xl', 'c'), across)  2.94 us
  transfers between devices with their start and end apart: 3, of which 1 were waited for; matrix products, arithmetic and copies ran while one was open for 0% of the time, Pallas kernels for 9%

profile of v8, /device:TPU:16, one launch (start us, length us, event | category | flops | bytes accessed | tf_op | source)
XLA Modules:
  0.0 140.6 jit_solution(6215675960416744926)
XLA Ops:
  0.0 1.8 %pack.1 = f32[896,128]{1,0:T(8,128)} custom-call(f32[3]{0:T(128)} %cond.3, f32[16,3,2,8,128]{4,3,2,1,0:T(8,128)} %forcing.1, f32[3,2,8,128]{3,2,1,0:T(8,128)} %start.1, f32[16,3,2,8,128]{4,3,2,1,0:T(8,128)} %latest.1, s32[2,8,128]{2,1,0:T(8,128)} %region.3), custom_call_target="tpu_custom_call" | custom-call | tf_op jit(solution)/shard_map/pack/pallas_call | solution.py:467
  1.8 0.0 copy-start
  1.8 0.0 copy-start.1
  1.8 0.0 copy-start.3
  1.9 33.5 %all_to_all.20.got = f32[16,56,128]{2,1,0:T(8,128)S(1)} all-to-all(f32[16,56,128]{2,1,0:T(8,128)} %bitcast.20), channel_id=1, replica_groups=mesh['yh'=2,'z'=8,'xh'=2,'xl'=2,'yl'=4,'c'=2] {'yh','z'}, dimensions={0} | all-to-all | bytes 917504 | tf_op jit(solution)/shard_map/all_to_all | solution.py:483
  35.4 0.0 copy-done
  35.4 0.0 copy-done.1
  35.4 0.0 copy-done.3
  35.4 0.9 forward.1
  36.3 26.9 %all_to_all.21 = f32[128,1,896]{2,1,0:T(1,128)S(1)} all-to-all(f32[128,1,896]{2,1,0:T(1,128)S(1)} %bitcast.12), channel_id=1, replica_groups=mesh['yh'=2,'z'=8,'xh'=2,'xl'=2,'yl'=4,'c'=2] {'yl','yh','xl','z'}, dimensions={0} | all-to-all | bytes 917504 | tf_op jit(solution)/shard_map/all_to_all | solution.py:494
  63.2 1.9 %collective-permute-start.2 = (f32[896,128]{1,0:T(8,128)S(1)}, f32[896,128]{1,0:T(8,128)S(1)}, u32[]{:S(2)}, u32[]{:S(2)}) collective-permute-start(f32[896,128]{1,0:T(8,128)S(1)} %bitcast.16), channel_id=1, source_target_pairs={{0,1},{1,0},{2,3},{3,2},{4,5},{5,4},{6,7},{7,6},{8,9},{9,8},{10,11... | collective-permute-start | bytes 1376264 | tf_op jit(solution)/shard_map/ppermute | solution.py:513
  65.2 0.0 copy-start.2
  65.2 0.0 copy-start.4
  65.2 2.9 %collective-permute-start.1 = (f32[672,128]{1,0:T(8,128)S(1)}, f32[672,128]{1,0:T(8,128)S(1)}, u32[]{:S(2)}, u32[]{:S(2)}) collective-permute-start(f32[672,128]{1,0:T(8,128)S(1)} %bitcast.21), channel_id=1, source_target_pairs={{0,25},{1,24},{8,17},{9,16},{16,9},{17,8},{24,1},{25,0},{2,27},{3,... | collective-permute-start | bytes 1032200 | tf_op jit(solution)/shard_map/ppermute | solution.py:511
  68.2 4.2 %collective-permute-start = (f32[672,128]{1,0:T(8,128)S(1)}, f32[672,128]{1,0:T(8,128)S(1)}, u32[]{:S(2)}, u32[]{:S(2)}) collective-permute-start(f32[672,128]{1,0:T(8,128)S(1)} %bitcast.22), channel_id=1, source_target_pairs={{0,24},{8,16},{16,8},{24,0},{1,25},{9,17},{17,9},{25,1},{2,26},{10... | collective-permute-start | bytes 1032200 | tf_op jit(solution)/shard_map/ppermute | solution.py:512
  72.4 0.0 collective-permute-done.2.mate
  72.4 0.0 copy-done.2
  72.4 0.0 copy-done.4
  72.4 12.5 %inner.1 = (f32[35,6,8,128]{3,2,1,0:T(8,128)S(1)}, f32[35,6,8,128]{3,2,1,0:T(8,128)S(1)}, f32[35,6,8,128]{3,2,1,0:T(8,128)S(1)}, f32[35,6,8,128]{3,2,1,0:T(8,128)S(1)}, f32[35,8,128]{2,1,0:T(8,128)S(1)}) custom-call(f32[4,128]{1,0:T(4,128)S(1)} %copy-done.2, f32[2,11]{1,0:T(2,128)S(1)} %copy-done.4, f32[896,128]{1,0:T(8,128)S(1)} %bitcast.19, ...), custom_call_target="tpu_custom_call" | custom-call | flops 10000000000 | bytes 20000000 | tf_op jit(solution)/shard_map/inner/pallas_call | solution.py:524
  84.9 0.0 collective-permute-done.1.part_mate
  84.9 1.1 collective-permute-done.part
  86.1 10.2 %outer.1 = f32[768,128]{1,0:T(8,128)S(1)} custom-call(f32[4,128]{1,0:T(4,128)S(1)} %copy-done.2, f32[2,11]{1,0:T(2,128)S(1)} %copy-done.4, f32[672,128]{1,0:T(8,128)S(1)} %collective-permute-done.part, f32[672,128]{1,0:T(8,128)S(1)} %collective-permute-done.1.part_mate, f32[35,6,8,128]{3,2,1,0:T(8,128)S(1)} %get-tuple-element.10.refs_0_, ...), custom_call_target="tpu_custom_call" | custom-call | tf_op jit(solution)/shard_map/outer/pallas_call | solution.py:536
  96.2 22.6 %all_to_all.22 = f32[128,1,768]{2,1,0:T(1,128)S(1)} all-to-all(f32[128,1,768]{2,1,0:T(1,128)S(1)} %bitcast.15), channel_id=1, replica_groups=mesh['yh'=2,'z'=8,'xh'=2,'xl'=2,'yl'=4,'c'=2] {'yl','yh','xl','z'}, dimensions={0} | all-to-all | bytes 786432 | tf_op jit(solution)/shard_map/all_to_all | solution.py:547
  118.9 0.4 inverse.1
  119.3 20.6 %all_to_all.23 = f32[16,48,128]{2,1,0:T(8,128)S(1)} all-to-all(f32[16,48,128]{2,1,0:T(8,128)S(1)} %inverse.1), channel_id=1, replica_groups=mesh['yh'=2,'z'=8,'xh'=2,'xl'=2,'yl'=4,'c'=2] {'yh','z'}, dimensions={0} | all-to-all | bytes 786432 | tf_op jit(solution)/shard_map/all_to_all | solution.py:560
  139.8 0.8 unpack.1
  (3 shorter events, 0.1 us)
Async XLA Ops:
  1.8 33.6 %copy-start = (f32[2,256,256]{2,1,0:T(8,128)S(1)}, f32[2,256,256]{2,1,0:T(8,128)}, u32[]{:S(2)}) copy-start(f32[2,256,256]{2,1,0:T(8,128)} %constant.26.clone.tables) | copy-start | bytes 1572868
  1.8 33.6 %copy-start.1 = (s32[2,8,128]{2,1,0:T(8,128)S(1)}, s32[2,8,128]{2,1,0:T(8,128)}, u32[]{:S(2)}) copy-start(s32[2,8,128]{2,1,0:T(8,128)} %region.3) | copy-start | bytes 24580
  1.8 33.6 %copy-start.3 = (f32[3]{0:T(128)S(1)}, f32[3]{0:T(128)}, u32[]{:S(2)}) copy-start(f32[3]{0:T(128)} %cond.3) | copy-start | bytes 40
  63.2 9.2 %collective-permute-start.2 = (f32[896,128]{1,0:T(8,128)S(1)}, f32[896,128]{1,0:T(8,128)S(1)}, u32[]{:S(2)}, u32[]{:S(2)}) collective-permute-start(f32[896,128]{1,0:T(8,128)S(1)} %bitcast.16), channel_id=1, source_target_pairs={{0,1},{1,0},{2,3},{3,2},{4,5},{5,4},{6,7},{7,6},{8,9},{9,8},{10,11... | collective-permute-start | bytes 1376264 | tf_op jit(solution)/shard_map/ppermute | solution.py:513
  65.2 7.2 %copy-start.2 = (f32[4,128]{1,0:T(4,128)S(1)}, f32[4,128]{1,0:T(4,128)}, u32[]{:S(2)}) copy-start(f32[4,128]{1,0:T(4,128)} %constant.27.clone.terms) | copy-start | bytes 6148
  65.2 7.2 %copy-start.4 = (f32[2,11]{1,0:T(2,128)S(1)}, f32[2,11]{1,0:T(2,128)}, u32[]{:S(2)}) copy-start(f32[2,11]{1,0:T(2,128)} %constant.28.clone.weights) | copy-start | bytes 268
  65.2 19.7 %collective-permute-start.1 = (f32[672,128]{1,0:T(8,128)S(1)}, f32[672,128]{1,0:T(8,128)S(1)}, u32[]{:S(2)}, u32[]{:S(2)}) collective-permute-start(f32[672,128]{1,0:T(8,128)S(1)} %bitcast.21), channel_id=1, source_target_pairs={{0,25},{1,24},{8,17},{9,16},{16,9},{17,8},{24,1},{25,0},{2,27},{3,... | collective-permute-start | bytes 1032200 | tf_op jit(solution)/shard_map/ppermute | solution.py:511
  68.2 17.9 %collective-permute-start = (f32[672,128]{1,0:T(8,128)S(1)}, f32[672,128]{1,0:T(8,128)S(1)}, u32[]{:S(2)}, u32[]{:S(2)}) collective-permute-start(f32[672,128]{1,0:T(8,128)S(1)} %bitcast.22), channel_id=1, source_target_pairs={{0,24},{8,16},{16,8},{24,0},{1,25},{9,17},{17,9},{25,1},{2,26},{10... | collective-permute-start | bytes 1032200 | tf_op jit(solution)/shard_map/ppermute | solution.py:512

commit v9 on v8

--- a/solution.py
+++ b/solution.py
@@ -1,3 +1,4 @@
+import functools
 import itertools
 import math
 
@@ -25,6 +26,7 @@
 GUARD = 1
 INNER = 8
 OUTER = 12
+EARLY = 5
 
 
 def pair_index():
@@ -326,19 +328,28 @@
     return list(enumerate(order))
 
 
-def inner_kernel(terms, weights, mine, mate, field, first, resid, total, sigma, flux_a, flux_b):
+def inner_kernel(sweeps, terms, weights, *refs):
+    *given, field, first, resid, total, sigma, flux_a, flux_b = refs
     ny, nz = sigma.shape[1:]
     blank = jnp.zeros((ny, nz), jnp.float32)
     half_at, core_at = lax.axis_index("xh"), lax.axis_index("c")
     lift, drop = operator(terms, sigma)
     size = flux_a.shape[0] - 1
 
+    begins_all = sweeps.start == 0
     for ref in (first, field):
         store(ref, -1, [blank] * 6)
         store(ref, HALF, [blank] * 6)
-    for source, core in ((mine, core_at), (mate, 1 - core_at)):
-        begin = STRIPE * core
-        fill(first, sigma, source, brick_rows(), (begin, begin + HALF // 2))
+    if begins_all:
+        for source, core in zip(given, (core_at, 1 - core_at)):
+            begin = STRIPE * core
+            fill(first, sigma, source, brick_rows(), (begin, begin + HALF // 2))
+    else:
+        for ref, old in zip((field, first, resid, total), given):
+            for i in range(HALF):
+                store(ref, i, load(old, i))
+        for i in range(HALF):
+            sigma[i + GUARD] = given[4][i + GUARD]
 
     def begin_of(level):
         count = (HALF - level + size - 1) // size
@@ -369,8 +380,12 @@
         return lambda i: jnp.where((i >= low) & (i < high), i, HALF + 1)
 
     begin_with, _, _ = finishers(terms, field, first, resid, total, placed(1))
-    lift(flux_b, first, begin_of(1)[0], half_at == 0)
-    run(1, flux_b, first, -1.0, begin_with, flux_a, field, True)
+    if begins_all:
+        lift(flux_b, first, begin_of(1)[0], half_at == 0)
+        run(1, flux_b, first, -1.0, begin_with, flux_a, field, True)
+    else:
+        low, _ = begin_of(2 + 2 * sweeps.start)
+        lift(flux_a, field, low, (low == 0) & (half_at == 0))
 
     def sweep(s, beside):
         _, keep_first, _ = finishers(terms, field, first, resid, total, placed(2 + 2 * s))
@@ -396,8 +411,9 @@
         return 0
 
     apart = max(s for s in range(SWEEPS) if (HALF - 4 - 2 * s + size - 1) // size >= 3) + 1
-    lax.fori_loop(0, apart, early, 0)
-    lax.fori_loop(apart, SWEEPS - 1, late, 0)
+    between = min(max(apart, sweeps.start), sweeps.stop)
+    lax.fori_loop(sweeps.start, between, early, 0)
+    lax.fori_loop(between, sweeps.stop, late, 0)
 
 
 def outer_kernel(
@@ -503,13 +519,8 @@
     )
     part = jnp.concatenate([near, beyond[:, :, 0]], axis=0).reshape(-1, nz)
     mine = mine.reshape(half * (2 * comps + 1), nz)
-    blocks, cores = lax.axis_size(("xh", "xl")), lax.axis_size("c")
-    chips = [(i, blocks - 1 - i) for i in range(blocks)]
-    across = [
-        (i * cores + c, j * cores + cores - 1 - c) for i, j in chips for c in range(cores)
-    ]
-    part_mate = lax.ppermute(part, ("xh", "xl", "c"), across)
-    part = lax.ppermute(part, ("xh", "xl"), chips)
+    blocks = lax.axis_size(("xh", "xl"))
+    part = lax.ppermute(part, ("xh", "xl"), [(i, blocks - 1 - i) for i in range(blocks)])
     mate = lax.ppermute(mine, "c", [(0, 1), (1, 0)])
 
     terms = jnp.asarray(pair_table(window))
@@ -521,18 +532,24 @@
     def flux(planes):
         return pltpu.VMEM((planes + 1, 2 * comps, ny, nz), f32)
 
-    inner = pl.pallas_call(
-        inner_kernel,
-        out_shape=[jax.ShapeDtypeStruct(shape, f32) for shape in state(HALF + 3 * GUARD)],
-        in_specs=[smem, smem, vmem, vmem],
-        out_specs=[vmem] * 5,
-        scratch_shapes=[flux(INNER)] * 2,
-        compiler_params=params,
-        cost_estimate=pl.CostEstimate(
-            flops=10**10, bytes_accessed=2 * 10**7, transcendentals=0
-        ),
-        name="inner",
-    )(terms, weights, mine, mate)
+    def inner(sweeps, given):
+        return pl.pallas_call(
+            functools.partial(inner_kernel, sweeps),
+            out_shape=[jax.ShapeDtypeStruct(shape, f32) for shape in state(HALF + 3 * GUARD)],
+            in_specs=[smem, smem] + [vmem] * len(given),
+            out_specs=[vmem] * 5,
+            scratch_shapes=[flux(INNER)] * 2,
+            compiler_params=params,
+            cost_estimate=pl.CostEstimate(
+                flops=10**10, bytes_accessed=2 * 10**7, transcendentals=0
+            ),
+            name="inner",
+        )(terms, weights, *given)
+
+    early = inner(range(0, EARLY), (mine, mate))
+    part, early = lax.optimization_barrier((part, early))
+    part_mate = lax.ppermute(part, "c", [(0, 1), (1, 0)])
+    late = inner(range(EARLY, SWEEPS - 1), early)
     solved = pl.pallas_call(
         outer_kernel,
         out_shape=jax.ShapeDtypeStruct((half * 2 * comps, nz), f32),
@@ -542,7 +559,7 @@
         + [flux(OUTER)] * 2,
         compiler_params=params,
         name="outer",
-    )(terms, weights, part, part_mate, *inner)
+    )(terms, weights, part, part_mate, *late)
 
     back = lax.all_to_all(
         solved.reshape(half, 1, 2 * comps * nz), GROUP, 0, 0, tiled=True

time: 141 us -> 143 us (1.014)
  starting transfers between devices: 9.06 us -> 6.62 us
  waiting for transfers between devices: 1.15 us -> 3.49 us
    ppermute x2, starting transfers between devices: 7.16 us -> 4.71 us  [the longest x1 2.8 us: per_device(): lax.ppermute(part, ('xh', 'xl'), [(i, blocks - 1 - i) for i in range(bloc...]
    ppermute x2, waiting for transfers between devices: 1.14 us -> 3.48 us  [the longest x1 3.48 us: per_device(): lax.ppermute(part, ('xh', 'xl'), [(i, blocks - 1 - i) for i in range(bloc...]
    pallas_call x1 -> x2, Pallas kernels: 12.5 us -> 13.3 us  [inner(): pl.pallas_call(functools.partial(inner_kernel, sweeps), out_shape=[jax.Sh...]
where the time goes in v9:
time: 143 us
  blocking collectives  105 us (73%)
  Pallas kernels  27.4 us (19%)
  starting transfers between devices  6.62 us (5%)
  waiting for transfers between devices  3.49 us (2%)
    all_to_all x1, blocking collectives, per_device(): got = lax.all_to_all(packed.reshape(groups, rows, nz), TM, 0, 0, tiled=True)  33.5 us
    all_to_all x1, blocking collectives, per_device(): lax.all_to_all(spectrum.reshape(half, 1, (2 * comps + 1) * nz), GROUP, 0,...  26.9 us
    all_to_all x1, blocking collectives, per_device(): lax.all_to_all(solved.reshape(half, 1, 2 * comps * nz), GROUP, 0, 0, tile...  23.7 us
    all_to_all x1, blocking collectives, per_device(): home = lax.all_to_all(pencil, TM, 0, 0, tiled=True)  21.2 us
    pallas_call x2, Pallas kernels, inner(): pl.pallas_call(functools.partial(inner_kernel, sweeps), out_shape=[jax.Sh...  13.3 us
    pallas_call x1, Pallas kernels, per_device(): pl.pallas_call(outer_kernel, out_shape=jax.ShapeDtypeStruct((half * 2 * c...  10.2 us
    ppermute x1, waiting for transfers between devices, per_device(): lax.ppermute(part, ('xh', 'xl'), [(i, blocks - 1 - i) for i in range(bloc...  3.48 us
  transfers between devices with their start and end apart: 3, of which 1 were waited for; matrix products, arithmetic and copies ran while one was open for 0% of the time, Pallas kernels for 9%

profile of v9, /device:TPU:16, one launch (start us, length us, event | category | flops | bytes accessed | tf_op | source)
XLA Modules:
  0.0 143.0 jit_solution(3534382886915681735)
XLA Ops:
  0.0 1.8 %pack.1 = f32[896,128]{1,0:T(8,128)} custom-call(f32[3]{0:T(128)} %cond.3, f32[16,3,2,8,128]{4,3,2,1,0:T(8,128)} %forcing.1, f32[3,2,8,128]{3,2,1,0:T(8,128)} %start.1, f32[16,3,2,8,128]{4,3,2,1,0:T(8,128)} %latest.1, s32[2,8,128]{2,1,0:T(8,128)} %region.3), custom_call_target="tpu_custom_call" | custom-call | tf_op jit(solution)/shard_map/pack/pallas_call | solution.py:483
  1.8 0.0 copy-start
  1.8 0.0 copy-start.1
  1.8 0.0 copy-start.3
  1.9 33.5 %all_to_all.20.got = f32[16,56,128]{2,1,0:T(8,128)S(1)} all-to-all(f32[16,56,128]{2,1,0:T(8,128)} %bitcast.20), channel_id=1, replica_groups=mesh['yh'=2,'z'=8,'xh'=2,'xl'=2,'yl'=4,'c'=2] {'yh','z'}, dimensions={0} | all-to-all | bytes 917504 | tf_op jit(solution)/shard_map/all_to_all | solution.py:499
  35.4 0.0 copy-done
  35.4 0.0 copy-done.1
  35.4 0.0 copy-done.3
  35.4 0.9 forward.1
  36.3 26.9 %all_to_all.21 = f32[128,1,896]{2,1,0:T(1,128)S(1)} all-to-all(f32[128,1,896]{2,1,0:T(1,128)S(1)} %bitcast.12), channel_id=1, replica_groups=mesh['yh'=2,'z'=8,'xh'=2,'xl'=2,'yl'=4,'c'=2] {'yl','yh','xl','z'}, dimensions={0} | all-to-all | bytes 917504 | tf_op jit(solution)/shard_map/all_to_all | solution.py:510
  63.2 1.9 %collective-permute-start.1 = (f32[896,128]{1,0:T(8,128)S(1)}, f32[896,128]{1,0:T(8,128)S(1)}, u32[]{:S(2)}, u32[]{:S(2)}) collective-permute-start(f32[896,128]{1,0:T(8,128)S(1)} %bitcast.16), channel_id=1, source_target_pairs={{0,1},{1,0},{2,3},{3,2},{4,5},{5,4},{6,7},{7,6},{8,9},{9,8},{10,11... | collective-permute-start | bytes 1376264 | tf_op jit(solution)/shard_map/ppermute | solution.py:524
  65.2 0.0 copy-start.2
  65.2 0.0 copy-start.4
  65.2 2.8 %collective-permute-start = (f32[672,128]{1,0:T(8,128)S(1)}, f32[672,128]{1,0:T(8,128)S(1)}, u32[]{:S(2)}, u32[]{:S(2)}) collective-permute-start(f32[672,128]{1,0:T(8,128)S(1)} %bitcast.21), channel_id=1, source_target_pairs={{0,24},{8,16},{16,8},{24,0},{1,25},{9,17},{17,9},{25,1},{2,26},{10... | collective-permute-start | bytes 1032200 | tf_op jit(solution)/shard_map/ppermute | solution.py:523
  68.0 0.0 collective-permute-done.1.refs_1_
  68.0 0.0 copy-done.2
  68.0 0.0 copy-done.4
  68.1 7.2 %inner.2 = (f32[35,6,8,128]{3,2,1,0:T(8,128)S(1)}, f32[35,6,8,128]{3,2,1,0:T(8,128)S(1)}, f32[35,6,8,128]{3,2,1,0:T(8,128)S(1)}, f32[35,6,8,128]{3,2,1,0:T(8,128)S(1)}, f32[35,8,128]{2,1,0:T(8,128)S(1)}) custom-call(f32[4,128]{1,0:T(4,128)S(1)} %copy-done.2, f32[2,11]{1,0:T(2,128)S(1)} %copy-done.4, f32[896,128]{1,0:T(8,128)S(1)} %bitcast.19, ...), custom_call_target="tpu_custom_call" | custom-call | flops 10000000000 | bytes 20000000 | tf_op jit(solution)/shard_map/inner/pallas_call | solution.py:536
  75.3 3.5 %collective-permute-done.part = f32[672,128]{1,0:T(8,128)S(1)} collective-permute-done((f32[672,128]{1,0:T(8,128)S(1)}, f32[672,128]{1,0:T(8,128)S(1)}, u32[]{:S(2)}, u32[]{:S(2)}) %collective-permute-start) | collective-permute-done | bytes 344096 | tf_op jit(solution)/shard_map/ppermute | solution.py:523
  78.8 1.9 %collective-permute-start.2 = (f32[672,128]{1,0:T(8,128)S(1)}, f32[672,128]{1,0:T(8,128)S(1)}, u32[]{:S(2)}, u32[]{:S(2)}) collective-permute-start(f32[672,128]{1,0:T(8,128)S(1)} %collective-permute-done.part), channel_id=1, source_target_pairs={{0,1},{1,0},{2,3},{3,2},{4,5},{5,4},{6,7},{7,6},{8,9},{9,8},{10,11... | collective-permute-start | bytes 1032200 | tf_op jit(solution)/shard_map/ppermute | solution.py:551
  80.7 6.1 %inner.3 = (f32[35,6,8,128]{3,2,1,0:T(8,128)S(1)}, f32[35,6,8,128]{3,2,1,0:T(8,128)S(1)}, f32[35,6,8,128]{3,2,1,0:T(8,128)S(1)}, f32[35,6,8,128]{3,2,1,0:T(8,128)S(1)}, f32[35,8,128]{2,1,0:T(8,128)S(1)}) custom-call(f32[4,128]{1,0:T(4,128)S(1)} %copy-done.2, f32[2,11]{1,0:T(2,128)S(1)} %copy-done.4, f32[35,6,8,128]{3,2,1,0:T(8,128)S(1)} %get-tuple-element.27.refs_0_, ...), custom_call_target="tpu_custom_call" | custom-call | flops 10000000000 | bytes 20000000 | tf_op jit(solution)/shard_map/inner/pallas_call | solution.py:536
  86.8 0.0 collective-permute-done.2.part_mate
  86.8 10.2 %outer.1 = f32[768,128]{1,0:T(8,128)S(1)} custom-call(f32[4,128]{1,0:T(4,128)S(1)} %copy-done.2, f32[2,11]{1,0:T(2,128)S(1)} %copy-done.4, f32[672,128]{1,0:T(8,128)S(1)} %collective-permute-done.part, f32[672,128]{1,0:T(8,128)S(1)} %collective-permute-done.2.part_mate, f32[35,6,8,128]{3,2,1,0:T(8,128)S(1)} %get-tuple-element.32.refs_0_, ...), custom_call_target="tpu_custom_call" | custom-call | tf_op jit(solution)/shard_map/outer/pallas_call | solution.py:553
  97.0 23.7 %all_to_all.22 = f32[128,1,768]{2,1,0:T(1,128)S(1)} all-to-all(f32[128,1,768]{2,1,0:T(1,128)S(1)} %bitcast.15), channel_id=1, replica_groups=mesh['yh'=2,'z'=8,'xh'=2,'xl'=2,'yl'=4,'c'=2] {'yl','yh','xl','z'}, dimensions={0} | all-to-all | bytes 786432 | tf_op jit(solution)/shard_map/all_to_all | solution.py:564
  120.6 0.4 inverse.1
  121.0 21.2 %all_to_all.23 = f32[16,48,128]{2,1,0:T(8,128)S(1)} all-to-all(f32[16,48,128]{2,1,0:T(8,128)S(1)} %inverse.1), channel_id=1, replica_groups=mesh['yh'=2,'z'=8,'xh'=2,'xl'=2,'yl'=4,'c'=2] {'yh','z'}, dimensions={0} | all-to-all | bytes 786432 | tf_op jit(solution)/shard_map/all_to_all | solution.py:577
  142.2 0.8 unpack.1
  (3 shorter events, 0.1 us)
Async XLA Ops:
  1.8 33.6 %copy-start = (f32[2,256,256]{2,1,0:T(8,128)S(1)}, f32[2,256,256]{2,1,0:T(8,128)}, u32[]{:S(2)}) copy-start(f32[2,256,256]{2,1,0:T(8,128)} %constant.26.clone.tables) | copy-start | bytes 1572868
  1.8 33.6 %copy-start.1 = (s32[2,8,128]{2,1,0:T(8,128)S(1)}, s32[2,8,128]{2,1,0:T(8,128)}, u32[]{:S(2)}) copy-start(s32[2,8,128]{2,1,0:T(8,128)} %region.3) | copy-start | bytes 24580
  1.8 33.6 %copy-start.3 = (f32[3]{0:T(128)S(1)}, f32[3]{0:T(128)}, u32[]{:S(2)}) copy-start(f32[3]{0:T(128)} %cond.3) | copy-start | bytes 40
  63.2 4.9 %collective-permute-start.1 = (f32[896,128]{1,0:T(8,128)S(1)}, f32[896,128]{1,0:T(8,128)S(1)}, u32[]{:S(2)}, u32[]{:S(2)}) collective-permute-start(f32[896,128]{1,0:T(8,128)S(1)} %bitcast.16), channel_id=1, source_target_pairs={{0,1},{1,0},{2,3},{3,2},{4,5},{5,4},{6,7},{7,6},{8,9},{9,8},{10,11... | collective-permute-start | bytes 1376264 | tf_op jit(solution)/shard_map/ppermute | solution.py:524
  65.2 2.9 %copy-start.2 = (f32[4,128]{1,0:T(4,128)S(1)}, f32[4,128]{1,0:T(4,128)}, u32[]{:S(2)}) copy-start(f32[4,128]{1,0:T(4,128)} %constant.27.clone.terms) | copy-start | bytes 6148
  65.2 2.8 %copy-start.4 = (f32[2,11]{1,0:T(2,128)S(1)}, f32[2,11]{1,0:T(2,128)}, u32[]{:S(2)}) copy-start(f32[2,11]{1,0:T(2,128)} %constant.28.clone.weights) | copy-start | bytes 268
  65.2 13.6 %collective-permute-start = (f32[672,128]{1,0:T(8,128)S(1)}, f32[672,128]{1,0:T(8,128)S(1)}, u32[]{:S(2)}, u32[]{:S(2)}) collective-permute-start(f32[672,128]{1,0:T(8,128)S(1)} %bitcast.21), channel_id=1, source_target_pairs={{0,24},{8,16},{16,8},{24,0},{1,25},{9,17},{17,9},{25,1},{2,26},{10... | collective-permute-start | bytes 1032200 | tf_op jit(solution)/shard_map/ppermute | solution.py:523
  78.8 8.0 %collective-permute-start.2 = (f32[672,128]{1,0:T(8,128)S(1)}, f32[672,128]{1,0:T(8,128)S(1)}, u32[]{:S(2)}, u32[]{:S(2)}) collective-permute-start(f32[672,128]{1,0:T(8,128)S(1)} %collective-permute-done.part), channel_id=1, source_target_pairs={{0,1},{1,0},{2,3},{3,2},{4,5},{5,4},{6,7},{7,6},{8,9},{9,8},{10,11... | collective-permute-start | bytes 1032200 | tf_op jit(solution)/shard_map/ppermute | solution.py:551

commit v10 on v9

--- a/solution.py
+++ b/solution.py
@@ -26,7 +26,7 @@
 GUARD = 1
 INNER = 8
 OUTER = 12
-EARLY = 5
+EARLY = 8
 
 
 def pair_index():

time: 143 us -> 141 us (0.986)
  the two profiles are of different devices: /device:TPU:16 before, /device:TPU:8 now
where the time goes in v10:
time: 141 us
  blocking collectives  106 us (75%)
  Pallas kernels  27.4 us (19%)
  starting transfers between devices  7.44 us (5%)
    all_to_all x1, blocking collectives, per_device(): got = lax.all_to_all(packed.reshape(groups, rows, nz), TM, 0, 0, tiled=True)  34.2 us
    all_to_all x1, blocking collectives, per_device(): lax.all_to_all(spectrum.reshape(half, 1, (2 * comps + 1) * nz), GROUP, 0,...  26.7 us
    all_to_all x1, blocking collectives, per_device(): lax.all_to_all(solved.reshape(half, 1, 2 * comps * nz), GROUP, 0, 0, tile...  24.1 us
    all_to_all x1, blocking collectives, per_device(): home = lax.all_to_all(pencil, TM, 0, 0, tiled=True)  20.5 us
    pallas_call x2, Pallas kernels, inner(): pl.pallas_call(functools.partial(inner_kernel, sweeps), out_shape=[jax.Sh...  13.3 us
    pallas_call x1, Pallas kernels, per_device(): pl.pallas_call(outer_kernel, out_shape=jax.ShapeDtypeStruct((half * 2 * c...  10.2 us
    ppermute x1, starting transfers between devices, per_device(): lax.ppermute(part, ('xh', 'xl'), [(i, blocks - 1 - i) for i in range(bloc...  3.4 us
  transfers between devices with their start and end apart: 3, of which 0 were waited for; matrix products, arithmetic and copies ran while one was open for 0% of the time, Pallas kernels for 9%

profile of v10, /device:TPU:8, one launch (start us, length us, event | category | flops | bytes accessed | tf_op | source)
XLA Modules:
  0.0 140.6 jit_solution(4225932293381798215)
XLA Ops:
  0.0 1.8 %pack.1 = f32[896,128]{1,0:T(8,128)} custom-call(f32[3]{0:T(128)} %cond.3, f32[16,3,2,8,128]{4,3,2,1,0:T(8,128)} %forcing.1, f32[3,2,8,128]{3,2,1,0:T(8,128)} %start.1, f32[16,3,2,8,128]{4,3,2,1,0:T(8,128)} %latest.1, s32[2,8,128]{2,1,0:T(8,128)} %region.3), custom_call_target="tpu_custom_call" | custom-call | tf_op jit(solution)/shard_map/pack/pallas_call | solution.py:483
  1.8 0.0 copy-start
  1.8 0.0 copy-start.1
  1.8 0.0 copy-start.3
  1.9 34.2 %all_to_all.20.got = f32[16,56,128]{2,1,0:T(8,128)S(1)} all-to-all(f32[16,56,128]{2,1,0:T(8,128)} %bitcast.20), channel_id=1, replica_groups=mesh['yh'=2,'z'=8,'xh'=2,'xl'=2,'yl'=4,'c'=2] {'yh','z'}, dimensions={0} | all-to-all | bytes 917504 | tf_op jit(solution)/shard_map/all_to_all | solution.py:499
  36.1 0.0 copy-done
  36.1 0.0 copy-done.1
  36.1 0.0 copy-done.3
  36.1 0.9 forward.1
  37.0 26.7 %all_to_all.21 = f32[128,1,896]{2,1,0:T(1,128)S(1)} all-to-all(f32[128,1,896]{2,1,0:T(1,128)S(1)} %bitcast.12), channel_id=1, replica_groups=mesh['yh'=2,'z'=8,'xh'=2,'xl'=2,'yl'=4,'c'=2] {'yl','yh','xl','z'}, dimensions={0} | all-to-all | bytes 917504 | tf_op jit(solution)/shard_map/all_to_all | solution.py:510
  63.7 1.9 %collective-permute-start.1 = (f32[896,128]{1,0:T(8,128)S(1)}, f32[896,128]{1,0:T(8,128)S(1)}, u32[]{:S(2)}, u32[]{:S(2)}) collective-permute-start(f32[896,128]{1,0:T(8,128)S(1)} %bitcast.16), channel_id=1, source_target_pairs={{0,1},{1,0},{2,3},{3,2},{4,5},{5,4},{6,7},{7,6},{8,9},{9,8},{10,11... | collective-permute-start | bytes 1376264 | tf_op jit(solution)/shard_map/ppermute | solution.py:524
  65.7 0.0 copy-start.2
  65.7 0.0 copy-start.4
  65.7 3.4 %collective-permute-start = (f32[672,128]{1,0:T(8,128)S(1)}, f32[672,128]{1,0:T(8,128)S(1)}, u32[]{:S(2)}, u32[]{:S(2)}) collective-permute-start(f32[672,128]{1,0:T(8,128)S(1)} %bitcast.21), channel_id=1, source_target_pairs={{0,24},{8,16},{16,8},{24,0},{1,25},{9,17},{17,9},{25,1},{2,26},{10... | collective-permute-start | bytes 1032200 | tf_op jit(solution)/shard_map/ppermute | solution.py:523
  69.1 0.0 collective-permute-done.1.refs_1_
  69.2 0.0 copy-done.2
  69.2 0.0 copy-done.4
  69.2 10.1 %inner.2 = (f32[35,6,8,128]{3,2,1,0:T(8,128)S(1)}, f32[35,6,8,128]{3,2,1,0:T(8,128)S(1)}, f32[35,6,8,128]{3,2,1,0:T(8,128)S(1)}, f32[35,6,8,128]{3,2,1,0:T(8,128)S(1)}, f32[35,8,128]{2,1,0:T(8,128)S(1)}) custom-call(f32[4,128]{1,0:T(4,128)S(1)} %copy-done.2, f32[2,11]{1,0:T(2,128)S(1)} %copy-done.4, f32[896,128]{1,0:T(8,128)S(1)} %bitcast.19, ...), custom_call_target="tpu_custom_call" | custom-call | flops 10000000000 | bytes 20000000 | tf_op jit(solution)/shard_map/inner/pallas_call | solution.py:536
  79.3 0.0 collective-permute-done.part
  79.3 2.1 %collective-permute-start.2 = (f32[672,128]{1,0:T(8,128)S(1)}, f32[672,128]{1,0:T(8,128)S(1)}, u32[]{:S(2)}, u32[]{:S(2)}) collective-permute-start(f32[672,128]{1,0:T(8,128)S(1)} %collective-permute-done.part), channel_id=1, source_target_pairs={{0,1},{1,0},{2,3},{3,2},{4,5},{5,4},{6,7},{7,6},{8,9},{9,8},{10,11... | collective-permute-start | bytes 1032200 | tf_op jit(solution)/shard_map/ppermute | solution.py:551
  81.5 3.2 %inner.3 = (f32[35,6,8,128]{3,2,1,0:T(8,128)S(1)}, f32[35,6,8,128]{3,2,1,0:T(8,128)S(1)}, f32[35,6,8,128]{3,2,1,0:T(8,128)S(1)}, f32[35,6,8,128]{3,2,1,0:T(8,128)S(1)}, f32[35,8,128]{2,1,0:T(8,128)S(1)}) custom-call(f32[4,128]{1,0:T(4,128)S(1)} %copy-done.2, f32[2,11]{1,0:T(2,128)S(1)} %copy-done.4, f32[35,6,8,128]{3,2,1,0:T(8,128)S(1)} %get-tuple-element.27.refs_0_, ...), custom_call_target="tpu_custom_call" | custom-call | flops 10000000000 | bytes 20000000 | tf_op jit(solution)/shard_map/inner/pallas_call | solution.py:536
  84.6 0.0 collective-permute-done.2.part_mate
  84.6 10.2 %outer.1 = f32[768,128]{1,0:T(8,128)S(1)} custom-call(f32[4,128]{1,0:T(4,128)S(1)} %copy-done.2, f32[2,11]{1,0:T(2,128)S(1)} %copy-done.4, f32[672,128]{1,0:T(8,128)S(1)} %collective-permute-done.part, f32[672,128]{1,0:T(8,128)S(1)} %collective-permute-done.2.part_mate, f32[35,6,8,128]{3,2,1,0:T(8,128)S(1)} %get-tuple-element.32.refs_0_, ...), custom_call_target="tpu_custom_call" | custom-call | tf_op jit(solution)/shard_map/outer/pallas_call | solution.py:553
  94.8 24.1 %all_to_all.22 = f32[128,1,768]{2,1,0:T(1,128)S(1)} all-to-all(f32[128,1,768]{2,1,0:T(1,128)S(1)} %bitcast.15), channel_id=1, replica_groups=mesh['yh'=2,'z'=8,'xh'=2,'xl'=2,'yl'=4,'c'=2] {'yl','yh','xl','z'}, dimensions={0} | all-to-all | bytes 786432 | tf_op jit(solution)/shard_map/all_to_all | solution.py:564
  118.9 0.4 inverse.1
  119.3 20.5 %all_to_all.23 = f32[16,48,128]{2,1,0:T(8,128)S(1)} all-to-all(f32[16,48,128]{2,1,0:T(8,128)S(1)} %inverse.1), channel_id=1, replica_groups=mesh['yh'=2,'z'=8,'xh'=2,'xl'=2,'yl'=4,'c'=2] {'yh','z'}, dimensions={0} | all-to-all | bytes 786432 | tf_op jit(solution)/shard_map/all_to_all | solution.py:577
  139.8 0.8 unpack.1
  (3 shorter events, 0.1 us)
Async XLA Ops:
  1.8 34.3 %copy-start = (f32[2,256,256]{2,1,0:T(8,128)S(1)}, f32[2,256,256]{2,1,0:T(8,128)}, u32[]{:S(2)}) copy-start(f32[2,256,256]{2,1,0:T(8,128)} %constant.26.clone.tables) | copy-start | bytes 1572868
  1.8 34.3 %copy-start.1 = (s32[2,8,128]{2,1,0:T(8,128)S(1)}, s32[2,8,128]{2,1,0:T(8,128)}, u32[]{:S(2)}) copy-start(s32[2,8,128]{2,1,0:T(8,128)} %region.3) | copy-start | bytes 24580
  1.8 34.3 %copy-start.3 = (f32[3]{0:T(128)S(1)}, f32[3]{0:T(128)}, u32[]{:S(2)}) copy-start(f32[3]{0:T(128)} %cond.3) | copy-start | bytes 40
  63.7 5.4 %collective-permute-start.1 = (f32[896,128]{1,0:T(8,128)S(1)}, f32[896,128]{1,0:T(8,128)S(1)}, u32[]{:S(2)}, u32[]{:S(2)}) collective-permute-start(f32[896,128]{1,0:T(8,128)S(1)} %bitcast.16), channel_id=1, source_target_pairs={{0,1},{1,0},{2,3},{3,2},{4,5},{5,4},{6,7},{7,6},{8,9},{9,8},{10,11... | collective-permute-start | bytes 1376264 | tf_op jit(solution)/shard_map/ppermute | solution.py:524
  65.7 3.5 %copy-start.2 = (f32[4,128]{1,0:T(4,128)S(1)}, f32[4,128]{1,0:T(4,128)}, u32[]{:S(2)}) copy-start(f32[4,128]{1,0:T(4,128)} %constant.27.clone.terms) | copy-start | bytes 6148
  65.7 3.4 %copy-start.4 = (f32[2,11]{1,0:T(2,128)S(1)}, f32[2,11]{1,0:T(2,128)}, u32[]{:S(2)}) copy-start(f32[2,11]{1,0:T(2,128)} %constant.28.clone.weights) | copy-start | bytes 268
  65.7 13.6 %collective-permute-start = (f32[672,128]{1,0:T(8,128)S(1)}, f32[672,128]{1,0:T(8,128)S(1)}, u32[]{:S(2)}, u32[]{:S(2)}) collective-permute-start(f32[672,128]{1,0:T(8,128)S(1)} %bitcast.21), channel_id=1, source_target_pairs={{0,24},{8,16},{16,8},{24,0},{1,25},{9,17},{17,9},{25,1},{2,26},{10... | collective-permute-start | bytes 1032200 | tf_op jit(solution)/shard_map/ppermute | solution.py:523
  79.3 5.3 %collective-permute-start.2 = (f32[672,128]{1,0:T(8,128)S(1)}, f32[672,128]{1,0:T(8,128)S(1)}, u32[]{:S(2)}, u32[]{:S(2)}) collective-permute-start(f32[672,128]{1,0:T(8,128)S(1)} %collective-permute-done.part), channel_id=1, source_target_pairs={{0,1},{1,0},{2,3},{3,2},{4,5},{5,4},{6,7},{7,6},{8,9},{9,8},{10,11... | collective-permute-start | bytes 1032200 | tf_op jit(solution)/shard_map/ppermute | solution.py:551

commit v11 on v10

--- a/solution.py
+++ b/solution.py
@@ -184,11 +184,8 @@
             out[b, c, 0] = got[pl.ds(c * steps + b, ny, stride=rows), :]
 
 
-def operator(terms, sigma):
-    ny, nz = sigma.shape[1:]
-    pair = pair_index()
-    p_plus, p_minus, q_term = terms[0, pair], terms[1, pair], terms[2, pair]
-
+def operator(sigma):
+    ny, nz = sigma.shape[2:]
     row = lax.broadcasted_iota(jnp.int32, (ny, nz), 0)
     lane = lax.broadcasted_iota(jnp.int32, (ny, nz), 1)
     row_first, row_last = row == 0, row == ny - 1
@@ -242,10 +239,14 @@
         return field
 
     def add_couple(field, values, weight, sign):
-        sp, sm, sq = weight * p_plus, weight * p_minus, weight * (sign * q_term)
+        sp, sm, sq = weight
+        if sign > 0:
+            return [
+                field[c] + (sp * values[c] - sq * values[3 + c]) for c in range(3)
+            ] + [field[3 + c] + (sm * values[3 + c] + sq * values[c]) for c in range(3)]
         return [
-            field[c] + (sp * values[c] - sq * values[3 + c]) for c in range(3)
-        ] + [field[3 + c] + (sm * values[3 + c] + sq * values[c]) for c in range(3)]
+            field[c] + (sp * values[c] + sq * values[3 + c]) for c in range(3)
+        ] + [field[3 + c] + (sm * values[3 + c] - sq * values[c]) for c in range(3)]
 
     def lift(flux, source, begin, edge):
         now = load(source, begin)
@@ -264,7 +265,7 @@
             i = begin + u
             now = [flux[u + 1, k] for k in range(6)]
             value = adjoints(now, before)
-            finish(i, add_couple(value, load(source, i), sigma[i + GUARD], sign))
+            finish(i, add_couple(value, load(source, i), [sigma[i + GUARD, k] for k in range(3)], sign))
             before = [now[k] for k in (1, 2, 4, 5)]
 
     return lift, drop
@@ -307,14 +308,16 @@
     return begin_with, keep_first, update
 
 
-def fill(first, sigma, source, rows, begins):
-    ny, nz = sigma.shape[1:]
+def fill(terms, first, sigma, source, rows, begins):
+    ny, nz = sigma.shape[2:]
     cols = 7
+    pair = pair_index()
     for row, (x_at, y_at, p) in rows:
         i = begins[x_at] + 2 * STRIPE * y_at + p
         parts = [source[pl.ds(row * cols * ny + k, ny, stride=cols), :] for k in range(cols)]
         store(first, i, parts[:6])
-        sigma[i + GUARD] = parts[6]
+        for k in range(3):
+            sigma[i + GUARD, k] = parts[6] * terms[k, pair]
 
 
 def brick_rows():
@@ -330,10 +333,10 @@
 
 def inner_kernel(sweeps, terms, weights, *refs):
     *given, field, first, resid, total, sigma, flux_a, flux_b = refs
-    ny, nz = sigma.shape[1:]
+    ny, nz = sigma.shape[2:]
     blank = jnp.zeros((ny, nz), jnp.float32)
     half_at, core_at = lax.axis_index("xh"), lax.axis_index("c")
-    lift, drop = operator(terms, sigma)
+    lift, drop = operator(sigma)
     size = flux_a.shape[0] - 1
 
     begins_all = sweeps.start == 0
@@ -343,13 +346,14 @@
     if begins_all:
         for source, core in zip(given, (core_at, 1 - core_at)):
             begin = STRIPE * core
-            fill(first, sigma, source, brick_rows(), (begin, begin + HALF // 2))
+            fill(terms, first, sigma, source, brick_rows(), (begin, begin + HALF // 2))
     else:
         for ref, old in zip((field, first, resid, total), given):
             for i in range(HALF):
                 store(ref, i, load(old, i))
         for i in range(HALF):
-            sigma[i + GUARD] = given[4][i + GUARD]
+            for k in range(3):
+                sigma[i + GUARD, k] = given[4][i + GUARD, k]
 
     def begin_of(level):
         count = (HALF - level + size - 1) // size
@@ -421,9 +425,9 @@
 ):
     given, out, state, (flux_a, flux_b) = refs[:5], refs[5], refs[6:11], refs[11:]
     field, first, resid, total, sigma = state
-    ny, nz = sigma.shape[1:]
+    ny, nz = sigma.shape[2:]
     half_at, core_at = lax.axis_index("xh"), lax.axis_index("c")
-    lift, drop = operator(terms, sigma)
+    lift, drop = operator(sigma)
     size = flux_a.shape[0] - 1
 
     own_low = REACH * half_at
@@ -431,13 +435,14 @@
         for i in range(HALF):
             store(ref, own_low + i, load(old, i))
     for i in range(HALF):
-        sigma[own_low + i + GUARD] = given[4][i + GUARD]
+        for k in range(3):
+            sigma[own_low + i + GUARD, k] = given[4][i + GUARD, k]
     halo_low = HALF * (1 - half_at)
     for source, core in ((part, core_at), (part_mate, 1 - core_at)):
         begin = halo_low + STRIPE * core
         whole_x = begin + (REACH - HALF // 2) * half_at
         half_x = begin + HALF // 2 * (1 - half_at)
-        fill(first, sigma, source, halo_rows(), (whole_x, half_x))
+        fill(terms, first, sigma, source, halo_rows(), (whole_x, half_x))
 
     def begin_of(level, turn):
         low = jnp.where(half_at == 0, HALF - level, level)
@@ -527,7 +532,7 @@
     weights = jnp.asarray(np.array(chebyshev_terms(SWEEPS - 1)[:2], np.float32))
 
     def state(places):
-        return [(places, 2 * comps, ny, nz)] * 4 + [(places, ny, nz)]
+        return [(places, 2 * comps, ny, nz)] * 4 + [(places, 3, ny, nz)]
 
     def flux(planes):
         return pltpu.VMEM((planes + 1, 2 * comps, ny, nz), f32)

time: 141 us -> 141 us (level)
  transfers between devices with their start and end apart: 3 -> 3, of which waited for: 0 -> 1; matrix products, arithmetic and copies ran while one was open for 0% -> 0% of each run, Pallas kernels for 9% -> 9%
where the time goes in v11:
time: 141 us
  blocking collectives  106 us (75%)
  Pallas kernels  27.4 us (19%)
  starting transfers between devices  7.31 us (5%)
    all_to_all x1, blocking collectives, per_device(): got = lax.all_to_all(packed.reshape(groups, rows, nz), TM, 0, 0, tiled=True)  34.2 us
    all_to_all x1, blocking collectives, per_device(): lax.all_to_all(spectrum.reshape(half, 1, (2 * comps + 1) * nz), GROUP, 0,...  26.7 us
    all_to_all x1, blocking collectives, per_device(): lax.all_to_all(solved.reshape(half, 1, 2 * comps * nz), GROUP, 0, 0, tile...  24.1 us
    all_to_all x1, blocking collectives, per_device(): home = lax.all_to_all(pencil, TM, 0, 0, tiled=True)  20.5 us
    pallas_call x2, Pallas kernels, inner(): pl.pallas_call(functools.partial(inner_kernel, sweeps), out_shape=[jax.Sh...  13.2 us
    pallas_call x1, Pallas kernels, per_device(): pl.pallas_call(outer_kernel, out_shape=jax.ShapeDtypeStruct((half * 2 * c...  10.2 us
    ppermute x1, starting transfers between devices, per_device(): lax.ppermute(part, ('xh', 'xl'), [(i, blocks - 1 - i) for i in range(bloc...  3.4 us
  transfers between devices with their start and end apart: 3, of which 1 were waited for; matrix products, arithmetic and copies ran while one was open for 0% of the time, Pallas kernels for 9%

profile of v11, /device:TPU:8, one launch (start us, length us, event | category | flops | bytes accessed | tf_op | source)
XLA Modules:
  0.0 140.6 jit_solution(5631214413456657066)
XLA Ops:
  0.0 1.8 %pack.1 = f32[896,128]{1,0:T(8,128)} custom-call(f32[3]{0:T(128)} %cond.3, f32[16,3,2,8,128]{4,3,2,1,0:T(8,128)} %forcing.1, f32[3,2,8,128]{3,2,1,0:T(8,128)} %start.1, f32[16,3,2,8,128]{4,3,2,1,0:T(8,128)} %latest.1, s32[2,8,128]{2,1,0:T(8,128)} %region.3), custom_call_target="tpu_custom_call" | custom-call | tf_op jit(solution)/shard_map/pack/pallas_call | solution.py:488
  1.8 0.0 copy-start
  1.8 0.0 copy-start.1
  1.8 0.0 copy-start.3
  1.9 34.2 %all_to_all.20.got = f32[16,56,128]{2,1,0:T(8,128)S(1)} all-to-all(f32[16,56,128]{2,1,0:T(8,128)} %bitcast.20), channel_id=1, replica_groups=mesh['yh'=2,'z'=8,'xh'=2,'xl'=2,'yl'=4,'c'=2] {'yh','z'}, dimensions={0} | all-to-all | bytes 917504 | tf_op jit(solution)/shard_map/all_to_all | solution.py:504
  36.1 0.0 copy-done
  36.1 0.0 copy-done.1
  36.1 0.0 copy-done.3
  36.1 0.9 forward.1
  37.0 26.7 %all_to_all.21 = f32[128,1,896]{2,1,0:T(1,128)S(1)} all-to-all(f32[128,1,896]{2,1,0:T(1,128)S(1)} %bitcast.12), channel_id=1, replica_groups=mesh['yh'=2,'z'=8,'xh'=2,'xl'=2,'yl'=4,'c'=2] {'yl','yh','xl','z'}, dimensions={0} | all-to-all | bytes 917504 | tf_op jit(solution)/shard_map/all_to_all | solution.py:515
  63.7 1.9 %collective-permute-start.1 = (f32[896,128]{1,0:T(8,128)S(1)}, f32[896,128]{1,0:T(8,128)S(1)}, u32[]{:S(2)}, u32[]{:S(2)}) collective-permute-start(f32[896,128]{1,0:T(8,128)S(1)} %bitcast.16), channel_id=1, source_target_pairs={{0,1},{1,0},{2,3},{3,2},{4,5},{5,4},{6,7},{7,6},{8,9},{9,8},{10,11... | collective-permute-start | bytes 1376264 | tf_op jit(solution)/shard_map/ppermute | solution.py:529
  65.7 0.0 copy-start.2
  65.7 0.0 copy-start.4
  65.7 3.4 %collective-permute-start = (f32[672,128]{1,0:T(8,128)S(1)}, f32[672,128]{1,0:T(8,128)S(1)}, u32[]{:S(2)}, u32[]{:S(2)}) collective-permute-start(f32[672,128]{1,0:T(8,128)S(1)} %bitcast.21), channel_id=1, source_target_pairs={{0,24},{8,16},{16,8},{24,0},{1,25},{9,17},{17,9},{25,1},{2,26},{10... | collective-permute-start | bytes 1032200 | tf_op jit(solution)/shard_map/ppermute | solution.py:528
  69.1 0.0 collective-permute-done.1.refs_1_
  69.2 0.0 copy-done.2
  69.2 0.0 copy-done.4
  69.2 10.0 %inner.2 = (f32[35,6,8,128]{3,2,1,0:T(8,128)S(1)}, f32[35,6,8,128]{3,2,1,0:T(8,128)S(1)}, f32[35,6,8,128]{3,2,1,0:T(8,128)S(1)}, f32[35,6,8,128]{3,2,1,0:T(8,128)S(1)}, f32[35,3,8,128]{3,2,1,0:T(8,128)S(1)}) custom-call(f32[4,128]{1,0:T(4,128)S(1)} %copy-done.2, f32[2,11]{1,0:T(2,128)S(1)} %copy-done.4, f32[896,128]{1,0:T(8,128)S(1)} %bitcast.19, ...), custom_call_target="tpu_custom_call" | custom-call | flops 10000000000 | bytes 20000000 | tf_op jit(solution)/shard_map/inner/pallas_call | solution.py:541
  79.2 0.1 collective-permute-done.part
  79.3 2.0 %collective-permute-start.2 = (f32[672,128]{1,0:T(8,128)S(1)}, f32[672,128]{1,0:T(8,128)S(1)}, u32[]{:S(2)}, u32[]{:S(2)}) collective-permute-start(f32[672,128]{1,0:T(8,128)S(1)} %collective-permute-done.part), channel_id=1, source_target_pairs={{0,1},{1,0},{2,3},{3,2},{4,5},{5,4},{6,7},{7,6},{8,9},{9,8},{10,11... | collective-permute-start | bytes 1032200 | tf_op jit(solution)/shard_map/ppermute | solution.py:556
  81.3 3.3 %inner.3 = (f32[35,6,8,128]{3,2,1,0:T(8,128)S(1)}, f32[35,6,8,128]{3,2,1,0:T(8,128)S(1)}, f32[35,6,8,128]{3,2,1,0:T(8,128)S(1)}, f32[35,6,8,128]{3,2,1,0:T(8,128)S(1)}, f32[35,3,8,128]{3,2,1,0:T(8,128)S(1)}) custom-call(f32[4,128]{1,0:T(4,128)S(1)} %copy-done.2, f32[2,11]{1,0:T(2,128)S(1)} %copy-done.4, f32[35,6,8,128]{3,2,1,0:T(8,128)S(1)} %get-tuple-element.27.refs_0_, ...), custom_call_target="tpu_custom_call" | custom-call | flops 10000000000 | bytes 20000000 | tf_op jit(solution)/shard_map/inner/pallas_call | solution.py:541
  84.6 0.0 collective-permute-done.2.part_mate
  84.6 10.2 %outer.1 = f32[768,128]{1,0:T(8,128)S(1)} custom-call(f32[4,128]{1,0:T(4,128)S(1)} %copy-done.2, f32[2,11]{1,0:T(2,128)S(1)} %copy-done.4, f32[672,128]{1,0:T(8,128)S(1)} %collective-permute-done.part, f32[672,128]{1,0:T(8,128)S(1)} %collective-permute-done.2.part_mate, f32[35,6,8,128]{3,2,1,0:T(8,128)S(1)} %get-tuple-element.32.refs_0_, ...), custom_call_target="tpu_custom_call" | custom-call | tf_op jit(solution)/shard_map/outer/pallas_call | solution.py:558
  94.8 24.1 %all_to_all.22 = f32[128,1,768]{2,1,0:T(1,128)S(1)} all-to-all(f32[128,1,768]{2,1,0:T(1,128)S(1)} %bitcast.13), channel_id=1, replica_groups=mesh['yh'=2,'z'=8,'xh'=2,'xl'=2,'yl'=4,'c'=2] {'yl','yh','xl','z'}, dimensions={0} | all-to-all | bytes 786432 | tf_op jit(solution)/shard_map/all_to_all | solution.py:569
  118.8 0.4 inverse.1
  119.2 20.5 %all_to_all.23 = f32[16,48,128]{2,1,0:T(8,128)S(1)} all-to-all(f32[16,48,128]{2,1,0:T(8,128)S(1)} %inverse.1), channel_id=1, replica_groups=mesh['yh'=2,'z'=8,'xh'=2,'xl'=2,'yl'=4,'c'=2] {'yh','z'}, dimensions={0} | all-to-all | bytes 786432 | tf_op jit(solution)/shard_map/all_to_all | solution.py:582
  139.8 0.8 unpack.1
  (3 shorter events, 0.1 us)
Async XLA Ops:
  1.8 34.3 %copy-start = (f32[2,256,256]{2,1,0:T(8,128)S(1)}, f32[2,256,256]{2,1,0:T(8,128)}, u32[]{:S(2)}) copy-start(f32[2,256,256]{2,1,0:T(8,128)} %constant.26.clone.tables) | copy-start | bytes 1572868
  1.8 34.3 %copy-start.1 = (s32[2,8,128]{2,1,0:T(8,128)S(1)}, s32[2,8,128]{2,1,0:T(8,128)}, u32[]{:S(2)}) copy-start(s32[2,8,128]{2,1,0:T(8,128)} %region.3) | copy-start | bytes 24580
  1.8 34.3 %copy-start.3 = (f32[3]{0:T(128)S(1)}, f32[3]{0:T(128)}, u32[]{:S(2)}) copy-start(f32[3]{0:T(128)} %cond.3) | copy-start | bytes 40
  63.7 5.4 %collective-permute-start.1 = (f32[896,128]{1,0:T(8,128)S(1)}, f32[896,128]{1,0:T(8,128)S(1)}, u32[]{:S(2)}, u32[]{:S(2)}) collective-permute-start(f32[896,128]{1,0:T(8,128)S(1)} %bitcast.16), channel_id=1, source_target_pairs={{0,1},{1,0},{2,3},{3,2},{4,5},{5,4},{6,7},{7,6},{8,9},{9,8},{10,11... | collective-permute-start | bytes 1376264 | tf_op jit(solution)/shard_map/ppermute | solution.py:529
  65.7 3.5 %copy-start.2 = (f32[4,128]{1,0:T(4,128)S(1)}, f32[4,128]{1,0:T(4,128)}, u32[]{:S(2)}) copy-start(f32[4,128]{1,0:T(4,128)} %constant.27.clone.terms) | copy-start | bytes 6148
  65.7 3.4 %copy-start.4 = (f32[2,11]{1,0:T(2,128)S(1)}, f32[2,11]{1,0:T(2,128)}, u32[]{:S(2)}) copy-start(f32[2,11]{1,0:T(2,128)} %constant.28.clone.weights) | copy-start | bytes 268
  65.7 13.6 %collective-permute-start = (f32[672,128]{1,0:T(8,128)S(1)}, f32[672,128]{1,0:T(8,128)S(1)}, u32[]{:S(2)}, u32[]{:S(2)}) collective-permute-start(f32[672,128]{1,0:T(8,128)S(1)} %bitcast.21), channel_id=1, source_target_pairs={{0,24},{8,16},{16,8},{24,0},{1,25},{9,17},{17,9},{25,1},{2,26},{10... | collective-permute-start | bytes 1032200 | tf_op jit(solution)/shard_map/ppermute | solution.py:528
  79.3 5.3 %collective-permute-start.2 = (f32[672,128]{1,0:T(8,128)S(1)}, f32[672,128]{1,0:T(8,128)S(1)}, u32[]{:S(2)}, u32[]{:S(2)}) collective-permute-start(f32[672,128]{1,0:T(8,128)S(1)} %collective-permute-done.part), channel_id=1, source_target_pairs={{0,1},{1,0},{2,3},{3,2},{4,5},{5,4},{6,7},{7,6},{8,9},{9,8},{10,11... | collective-permute-start | bytes 1032200 | tf_op jit(solution)/shard_map/ppermute | solution.py:556

commit v12 on v10

--- a/solution.py
+++ b/solution.py
@@ -26,7 +26,7 @@
 GUARD = 1
 INNER = 8
 OUTER = 12
-EARLY = 8
+EARLY = 9
 
 
 def pair_index():

time: 141 us -> 141 us (level)
  no operation moved by 1% of the time
where the time goes in v12:
time: 141 us
  blocking collectives  106 us (75%)
  Pallas kernels  27.4 us (19%)
  starting transfers between devices  7.44 us (5%)
    all_to_all x1, blocking collectives, per_device(): got = lax.all_to_all(packed.reshape(groups, rows, nz), TM, 0, 0, tiled=True)  34.2 us
    all_to_all x1, blocking collectives, per_device(): lax.all_to_all(spectrum.reshape(half, 1, (2 * comps + 1) * nz), GROUP, 0,...  26.7 us
    all_to_all x1, blocking collectives, per_device(): lax.all_to_all(solved.reshape(half, 1, 2 * comps * nz), GROUP, 0, 0, tile...  24.1 us
    all_to_all x1, blocking collectives, per_device(): home = lax.all_to_all(pencil, TM, 0, 0, tiled=True)  20.5 us
    pallas_call x2, Pallas kernels, inner(): pl.pallas_call(functools.partial(inner_kernel, sweeps), out_shape=[jax.Sh...  13.3 us
    pallas_call x1, Pallas kernels, per_device(): pl.pallas_call(outer_kernel, out_shape=jax.ShapeDtypeStruct((half * 2 * c...  10.2 us
    ppermute x1, starting transfers between devices, per_device(): lax.ppermute(part, ('xh', 'xl'), [(i, blocks - 1 - i) for i in range(bloc...  3.4 us
  transfers between devices with their start and end apart: 3, of which 0 were waited for; matrix products, arithmetic and copies ran while one was open for 0% of the time, Pallas kernels for 9%

profile of v12, /device:TPU:8, one launch (start us, length us, event | category | flops | bytes accessed | tf_op | source)
XLA Modules:
  0.0 140.6 jit_solution(7089686543027644447)
XLA Ops:
  0.0 1.8 %pack.1 = f32[896,128]{1,0:T(8,128)} custom-call(f32[3]{0:T(128)} %cond.3, f32[16,3,2,8,128]{4,3,2,1,0:T(8,128)} %forcing.1, f32[3,2,8,128]{3,2,1,0:T(8,128)} %start.1, f32[16,3,2,8,128]{4,3,2,1,0:T(8,128)} %latest.1, s32[2,8,128]{2,1,0:T(8,128)} %region.3), custom_call_target="tpu_custom_call" | custom-call | tf_op jit(solution)/shard_map/pack/pallas_call | solution.py:483
  1.8 0.0 copy-start
  1.8 0.0 copy-start.1
  1.8 0.0 copy-start.3
  1.9 34.2 %all_to_all.20.got = f32[16,56,128]{2,1,0:T(8,128)S(1)} all-to-all(f32[16,56,128]{2,1,0:T(8,128)} %bitcast.20), channel_id=1, replica_groups=mesh['yh'=2,'z'=8,'xh'=2,'xl'=2,'yl'=4,'c'=2] {'yh','z'}, dimensions={0} | all-to-all | bytes 917504 | tf_op jit(solution)/shard_map/all_to_all | solution.py:499
  36.1 0.0 copy-done
  36.1 0.0 copy-done.1
  36.1 0.0 copy-done.3
  36.1 0.9 forward.1
  37.0 26.7 %all_to_all.21 = f32[128,1,896]{2,1,0:T(1,128)S(1)} all-to-all(f32[128,1,896]{2,1,0:T(1,128)S(1)} %bitcast.12), channel_id=1, replica_groups=mesh['yh'=2,'z'=8,'xh'=2,'xl'=2,'yl'=4,'c'=2] {'yl','yh','xl','z'}, dimensions={0} | all-to-all | bytes 917504 | tf_op jit(solution)/shard_map/all_to_all | solution.py:510
  63.7 1.9 %collective-permute-start.1 = (f32[896,128]{1,0:T(8,128)S(1)}, f32[896,128]{1,0:T(8,128)S(1)}, u32[]{:S(2)}, u32[]{:S(2)}) collective-permute-start(f32[896,128]{1,0:T(8,128)S(1)} %bitcast.16), channel_id=1, source_target_pairs={{0,1},{1,0},{2,3},{3,2},{4,5},{5,4},{6,7},{7,6},{8,9},{9,8},{10,11... | collective-permute-start | bytes 1376264 | tf_op jit(solution)/shard_map/ppermute | solution.py:524
  65.7 0.0 copy-start.2
  65.7 0.0 copy-start.4
  65.7 3.4 %collective-permute-start = (f32[672,128]{1,0:T(8,128)S(1)}, f32[672,128]{1,0:T(8,128)S(1)}, u32[]{:S(2)}, u32[]{:S(2)}) collective-permute-start(f32[672,128]{1,0:T(8,128)S(1)} %bitcast.21), channel_id=1, source_target_pairs={{0,24},{8,16},{16,8},{24,0},{1,25},{9,17},{17,9},{25,1},{2,26},{10... | collective-permute-start | bytes 1032200 | tf_op jit(solution)/shard_map/ppermute | solution.py:523
  69.1 0.0 collective-permute-done.1.refs_1_
  69.2 0.0 copy-done.2
  69.2 0.0 copy-done.4
  69.2 10.9 %inner.2 = (f32[35,6,8,128]{3,2,1,0:T(8,128)S(1)}, f32[35,6,8,128]{3,2,1,0:T(8,128)S(1)}, f32[35,6,8,128]{3,2,1,0:T(8,128)S(1)}, f32[35,6,8,128]{3,2,1,0:T(8,128)S(1)}, f32[35,8,128]{2,1,0:T(8,128)S(1)}) custom-call(f32[4,128]{1,0:T(4,128)S(1)} %copy-done.2, f32[2,11]{1,0:T(2,128)S(1)} %copy-done.4, f32[896,128]{1,0:T(8,128)S(1)} %bitcast.19, ...), custom_call_target="tpu_custom_call" | custom-call | flops 10000000000 | bytes 20000000 | tf_op jit(solution)/shard_map/inner/pallas_call | solution.py:536
  80.1 0.0 collective-permute-done.part
  80.1 2.1 %collective-permute-start.2 = (f32[672,128]{1,0:T(8,128)S(1)}, f32[672,128]{1,0:T(8,128)S(1)}, u32[]{:S(2)}, u32[]{:S(2)}) collective-permute-start(f32[672,128]{1,0:T(8,128)S(1)} %collective-permute-done.part), channel_id=1, source_target_pairs={{0,1},{1,0},{2,3},{3,2},{4,5},{5,4},{6,7},{7,6},{8,9},{9,8},{10,11... | collective-permute-start | bytes 1032200 | tf_op jit(solution)/shard_map/ppermute | solution.py:551
  82.2 2.4 %inner.3 = (f32[35,6,8,128]{3,2,1,0:T(8,128)S(1)}, f32[35,6,8,128]{3,2,1,0:T(8,128)S(1)}, f32[35,6,8,128]{3,2,1,0:T(8,128)S(1)}, f32[35,6,8,128]{3,2,1,0:T(8,128)S(1)}, f32[35,8,128]{2,1,0:T(8,128)S(1)}) custom-call(f32[4,128]{1,0:T(4,128)S(1)} %copy-done.2, f32[2,11]{1,0:T(2,128)S(1)} %copy-done.4, f32[35,6,8,128]{3,2,1,0:T(8,128)S(1)} %get-tuple-element.27.refs_0_, ...), custom_call_target="tpu_custom_call" | custom-call | flops 10000000000 | bytes 20000000 | tf_op jit(solution)/shard_map/inner/pallas_call | solution.py:536
  84.6 0.0 collective-permute-done.2.part_mate
  84.7 10.2 %outer.1 = f32[768,128]{1,0:T(8,128)S(1)} custom-call(f32[4,128]{1,0:T(4,128)S(1)} %copy-done.2, f32[2,11]{1,0:T(2,128)S(1)} %copy-done.4, f32[672,128]{1,0:T(8,128)S(1)} %collective-permute-done.part, f32[672,128]{1,0:T(8,128)S(1)} %collective-permute-done.2.part_mate, f32[35,6,8,128]{3,2,1,0:T(8,128)S(1)} %get-tuple-element.32.refs_0_, ...), custom_call_target="tpu_custom_call" | custom-call | tf_op jit(solution)/shard_map/outer/pallas_call | solution.py:553
  94.8 24.1 %all_to_all.22 = f32[128,1,768]{2,1,0:T(1,128)S(1)} all-to-all(f32[128,1,768]{2,1,0:T(1,128)S(1)} %bitcast.15), channel_id=1, replica_groups=mesh['yh'=2,'z'=8,'xh'=2,'xl'=2,'yl'=4,'c'=2] {'yl','yh','xl','z'}, dimensions={0} | all-to-all | bytes 786432 | tf_op jit(solution)/shard_map/all_to_all | solution.py:564
  118.9 0.4 inverse.1
  119.3 20.5 %all_to_all.23 = f32[16,48,128]{2,1,0:T(8,128)S(1)} all-to-all(f32[16,48,128]{2,1,0:T(8,128)S(1)} %inverse.1), channel_id=1, replica_groups=mesh['yh'=2,'z'=8,'xh'=2,'xl'=2,'yl'=4,'c'=2] {'yh','z'}, dimensions={0} | all-to-all | bytes 786432 | tf_op jit(solution)/shard_map/all_to_all | solution.py:577
  139.8 0.8 unpack.1
  (3 shorter events, 0.1 us)
Async XLA Ops:
  1.8 34.3 %copy-start = (f32[2,256,256]{2,1,0:T(8,128)S(1)}, f32[2,256,256]{2,1,0:T(8,128)}, u32[]{:S(2)}) copy-start(f32[2,256,256]{2,1,0:T(8,128)} %constant.26.clone.tables) | copy-start | bytes 1572868
  1.8 34.3 %copy-start.1 = (s32[2,8,128]{2,1,0:T(8,128)S(1)}, s32[2,8,128]{2,1,0:T(8,128)}, u32[]{:S(2)}) copy-start(s32[2,8,128]{2,1,0:T(8,128)} %region.3) | copy-start | bytes 24580
  1.8 34.3 %copy-start.3 = (f32[3]{0:T(128)S(1)}, f32[3]{0:T(128)}, u32[]{:S(2)}) copy-start(f32[3]{0:T(128)} %cond.3) | copy-start | bytes 40
  63.7 5.4 %collective-permute-start.1 = (f32[896,128]{1,0:T(8,128)S(1)}, f32[896,128]{1,0:T(8,128)S(1)}, u32[]{:S(2)}, u32[]{:S(2)}) collective-permute-start(f32[896,128]{1,0:T(8,128)S(1)} %bitcast.16), channel_id=1, source_target_pairs={{0,1},{1,0},{2,3},{3,2},{4,5},{5,4},{6,7},{7,6},{8,9},{9,8},{10,11... | collective-permute-start | bytes 1376264 | tf_op jit(solution)/shard_map/ppermute | solution.py:524
  65.7 3.5 %copy-start.2 = (f32[4,128]{1,0:T(4,128)S(1)}, f32[4,128]{1,0:T(4,128)}, u32[]{:S(2)}) copy-start(f32[4,128]{1,0:T(4,128)} %constant.27.clone.terms) | copy-start | bytes 6148
  65.7 3.4 %copy-start.4 = (f32[2,11]{1,0:T(2,128)S(1)}, f32[2,11]{1,0:T(2,128)}, u32[]{:S(2)}) copy-start(f32[2,11]{1,0:T(2,128)} %constant.28.clone.weights) | copy-start | bytes 268
  65.7 14.4 %collective-permute-start = (f32[672,128]{1,0:T(8,128)S(1)}, f32[672,128]{1,0:T(8,128)S(1)}, u32[]{:S(2)}, u32[]{:S(2)}) collective-permute-start(f32[672,128]{1,0:T(8,128)S(1)} %bitcast.21), channel_id=1, source_target_pairs={{0,24},{8,16},{16,8},{24,0},{1,25},{9,17},{17,9},{25,1},{2,26},{10... | collective-permute-start | bytes 1032200 | tf_op jit(solution)/shard_map/ppermute | solution.py:523
  80.1 4.5 %collective-permute-start.2 = (f32[672,128]{1,0:T(8,128)S(1)}, f32[672,128]{1,0:T(8,128)S(1)}, u32[]{:S(2)}, u32[]{:S(2)}) collective-permute-start(f32[672,128]{1,0:T(8,128)S(1)} %collective-permute-done.part), channel_id=1, source_target_pairs={{0,1},{1,0},{2,3},{3,2},{4,5},{5,4},{6,7},{7,6},{8,9},{9,8},{10,11... | collective-permute-start | bytes 1032200 | tf_op jit(solution)/shard_map/ppermute | solution.py:551
